TPU v7x, 512 devices: a whole 4x4x16 slice. The times are simulated.
512 devices in a mesh: tm: 16 (over z), height: 8 (over y, core), width: 4 (over x).
Axes of the slice: x: 4, y: 4, z: 16, core: 2. Of those that a mesh axis runs over, the one named last changes fastest.
Arguments:
- latent: bfloat16 [32, 16, 64, 384], P('tm', 'height', 'width'), may hold values from -6 to 6
- norm_gain: float32 [384], replicated, may hold values from 0.1 to 1.9
- conv_weight: bfloat16 [3, 3, 3, 384, 384], P(None, None, None, None, 'tm'), may hold values from -0.0625 to 0.0625
- attn_gain: float32 [384], replicated, may hold values from 0.1 to 1.9
- w_qkv: bfloat16 [384, 1152], replicated, may hold values from -3 to 3
- w_out: bfloat16 [384, 384], replicated, may hold values from -0.3125 to 0.3125
Outputs:
- decoded: bfloat16 [32, 16, 64, 384], P('tm', 'height', 'width')
All inputs are finite; a program needn't handle non-finite values.
Results may differ from a plain program's by a relative error of at most 0.013.
Values may be sent and summed in bfloat16 or wider, within the bound.
No kernel may reach another device: no remote copies, remote signals or barrier semaphores. Data moves between devices by JAX's collectives and lax.ppermute only.
A program may use at most 64 MiB of HBM per device.

v0:
```python
import jax
import jax.numpy as jnp
from jax import lax
from jax.sharding import PartitionSpec as P


def with_halo(cells, sides, width):
    for axis, dim in sides:
        count = lax.axis_size(axis)
        ends = count - 1
        head = lax.slice_in_dim(cells, 0, width, axis=dim)
        tail = lax.slice_in_dim(cells, cells.shape[dim] - width, cells.shape[dim], axis=dim)
        cells = jnp.concatenate(
            [
                lax.ppermute(tail, axis, [(i, (i + 1) % count) for i in range(ends)]),
                cells,
                lax.ppermute(head, axis, [((i + 1) % count, i) for i in range(ends)]),
            ],
            axis=dim,
        )
    return cells


def shifted(block, axis, distance):
    devices = range(lax.axis_size(axis))
    route = [(i - distance, i) for i in devices if i - distance in devices]
    return lax.ppermute(block, axis, route)


def rms_scale(values, gain):
    mean_sq = jnp.mean(values * values, axis=-1, keepdims=True)
    return values * lax.rsqrt(mean_sq + 1e-06) * gain


def conv_taps(padded, weight):
    frames_out = padded.shape[0] - 2
    tile_rows = padded.shape[1] - 2
    tile_cols = padded.shape[2] - 2
    channels = padded.shape[3]
    out_cols = weight.shape[4]
    summed = jnp.zeros((frames_out * tile_rows * tile_cols, out_cols), jnp.float32)
    for time_tap in range(3):
        for row_tap in range(3):
            for col_tap in range(3):
                window = padded[
                    time_tap : time_tap + frames_out,
                    row_tap : row_tap + tile_rows,
                    col_tap : col_tap + tile_cols,
                ]
                summed = summed + jnp.dot(
                    window.reshape(-1, channels),
                    weight[time_tap, row_tap, col_tap],
                    preferred_element_type=jnp.float32,
                )
    return summed.reshape(frames_out, tile_rows, tile_cols, out_cols)


def local(latent, norm_gain, conv_weight, attn_gain, w_qkv, w_out):
    frames, tile_rows, tile_cols, channels = latent.shape
    latent_f = latent.astype(jnp.float32)
    activated = jax.nn.silu(rms_scale(latent_f, norm_gain)).astype(jnp.bfloat16)
    rimmed = with_halo(activated, (("height", 1), ("width", 2)), 1)
    earlier = shifted(rimmed, "tm", 1)
    padded = jnp.concatenate([earlier, rimmed], axis=0)
    conv_out = conv_taps(padded, lax.all_gather(conv_weight, "tm", axis=4, tiled=True))
    hidden = (latent_f + conv_out).astype(jnp.bfloat16)
    normed = rms_scale(hidden.astype(jnp.float32), attn_gain).astype(jnp.bfloat16)
    projected = jnp.dot(normed.reshape(-1, channels), w_qkv, preferred_element_type=jnp.float32)
    projected = projected.astype(jnp.bfloat16).reshape(frames, tile_rows * tile_cols, 3 * channels)
    query_rows = projected[:, :, :channels]
    key_rows = projected[:, :, channels : 2 * channels]
    value_rows = projected[:, :, 2 * channels :]
    inverse_root = 1.0 / jnp.sqrt(jnp.float32(channels))
    cells = tile_rows * tile_cols
    running_top = jnp.full((frames, cells), -jnp.inf, jnp.float32)
    running_sum = jnp.zeros((frames, cells), jnp.float32)
    weighted = jnp.zeros((frames, cells, channels), jnp.float32)
    scores = (
        jnp.einsum(
            "fqc,fkc->fqk",
            query_rows,
            lax.all_gather(key_rows, ("height", "width"), axis=1, tiled=True),
            preferred_element_type=jnp.float32,
        )
        * inverse_root
    )
    new_top = jnp.max(scores, axis=-1)
    powers = jnp.exp(scores - new_top[:, :, None])
    rescale = jnp.exp(running_top - new_top)
    new_sum = running_sum * rescale + jnp.sum(powers, axis=-1)
    mixed = jnp.einsum(
        "fqk,fkc->fqc",
        powers.astype(jnp.bfloat16),
        lax.all_gather(value_rows, ("height", "width"), axis=1, tiled=True),
        preferred_element_type=jnp.float32,
    )
    running_top, running_sum, weighted = (new_top, new_sum, weighted * rescale[:, :, None] + mixed)
    attended = (weighted / running_sum[:, :, None]).astype(jnp.bfloat16)
    update = jnp.dot(attended.reshape(-1, channels), w_out, preferred_element_type=jnp.float32)
    decoded = hidden.astype(jnp.float32) + update.reshape(frames, tile_rows, tile_cols, channels)
    return decoded.astype(jnp.bfloat16)


def solution(mesh):
    in_specs = (
        P("tm", "height", "width", None),
        P(),
        P(None, None, None, None, "tm"),
        P(),
        P(),
        P(),
    )
    out_specs = P("tm", "height", "width", None)
    return jax.shard_map(local, mesh=mesh, in_specs=in_specs, out_specs=out_specs, check_vma=False)
```

profile of v0, /device:TPU:1, one launch (start us, length us, event | category | flops | bytes accessed | tf_op | source)
XLA Modules:
  0.0 280.4 jit_solution(12701836183451193454)
XLA Ops:
  6.5 0.7 all-gather.4.cloned.1.call-update
  7.3 0.0 all-gather.6.cloned.1.call-start
  7.3 0.9 fusion.29
  8.2 0.9 fusion.36
  9.1 4.6 %collective-permute-start = (bf16[2,1,16,384]{3,2,1,0:T(8,128)(2,1)S(1)}, bf16[2,1,16,384]{3,2,1,0:T(8,128)(2,1)S(1)}, u32[]{:S(2)}, u32[]{:S(2)}) collective-permute-start(bf16[2,1,16,384]{3,2,1,0:T(8,128)(2,1)S(1)} %get-tuple-element.39), channel_id=1, source_target_pairs={{0,4},{4,8},{8,12},{12,16},{16,20},{20,24},{24,28},{1,5},{5,9},{9,... | collective-permute-start | bytes 73736 | tf_op jit(solution)/shard_map/ppermute | solution.py:15
  13.7 5.5 %collective-permute-start.1 = (bf16[2,1,16,384]{3,2,1,0:T(8,128)(2,1)S(1)}, bf16[2,1,16,384]{3,2,1,0:T(8,128)(2,1)S(1)}, u32[]{:S(2)}, u32[]{:S(2)}) collective-permute-start(bf16[2,1,16,384]{3,2,1,0:T(8,128)(2,1)S(1)} %get-tuple-element.40), channel_id=1, source_target_pairs={{4,0},{8,4},{12,8},{16,12},{20,16},{24,20},{28,24},{5,1},{9,5},{13... | collective-permute-start | bytes 73736 | tf_op jit(solution)/shard_map/ppermute | solution.py:17
  19.2 0.0 collective-permute-done
  19.2 0.8 collective-permute-done.1
  20.1 1.9 collective-permute-start.2
  22.0 1.3 collective-permute-start.3
  23.4 0.0 collective-permute-done.2
  23.4 3.1 %collective-permute-done.3 = bf16[2,4,1,384]{3,2,1,0:T(2,128)(2,1)S(1)} collective-permute-done((bf16[2,4,1,384]{3,2,1,0:T(2,128)(2,1)S(1)}, bf16[2,4,1,384]{3,2,1,0:T(2,128)(2,1)S(1)}, u32[]{:S(2)}, u32[]{:S(2)}) %collective-permute-start.3) | collective-permute-done | bytes 6176 | tf_op jit(solution)/shard_map/ppermute | solution.py:17
  26.5 0.1 pad_maximum_fusion
  26.5 3.5 %collective-permute-start.4 = (bf16[2,4,18,384]{3,2,1,0:T(8,128)(2,1)S(1)}, bf16[2,4,18,384]{3,2,1,0:T(8,128)(2,1)S(1)}, u32[]{:S(2)}, u32[]{:S(2)}) collective-permute-start(bf16[2,4,18,384]{3,2,1,0:T(8,128)(2,1)S(1)} %pad_maximum_fusion), channel_id=1, source_target_pairs={{0,32},{32,64},{64,96},{96,128},{128,160},{160,192},{192,224},{224... | collective-permute-start | bytes 331784 | tf_op jit(solution)/shard_map/ppermute | solution.py:27
  30.1 0.1 maximum_maximum_fusion.1
  30.2 5.6 %collective-permute-done.4 = bf16[2,4,18,384]{3,2,1,0:T(8,128)(2,1)S(1)} collective-permute-done((bf16[2,4,18,384]{3,2,1,0:T(8,128)(2,1)S(1)}, bf16[2,4,18,384]{3,2,1,0:T(8,128)(2,1)S(1)}, u32[]{:S(2)}, u32[]{:S(2)}) %collective-permute-start.4) | collective-permute-done | bytes 110624 | tf_op jit(solution)/shard_map/ppermute | solution.py:27
  35.8 0.1 maximum_maximum_fusion
  35.9 0.1 fusion.44
  36.0 0.0 copy-start.1
  36.0 0.0 copy-start.3
  36.0 0.1 fusion.48
  36.1 82.1 %all-gather.4.cloned.1.call-done = bf16[3,3,3,384,384]{3,4,2,1,0:T(8,128)(2,1)} async-done(((bf16[3,3,3,384,24]{3,4,2,1,0:T(8,128)(2,1)}), bf16[3,3,3,384,384]{3,4,2,1,0:T(8,128)(2,1)}) %all-gather.4.cloned.1.call-update) | async-done | bytes 7962640 | tf_op jit(solution)/shard_map/all_gather | solution.py:65
  118.1 1.2 fusion.15
  119.3 1.2 fusion.16
  120.5 1.2 fusion.17
  121.7 1.2 fusion.18
  122.9 1.2 fusion.19
  124.1 1.2 fusion.20
  125.3 1.2 fusion.21
  126.5 1.2 fusion.22
  127.7 1.2 fusion.23
  128.9 1.2 fusion.14
  130.0 1.2 fusion.13
  131.3 1.2 fusion.10
  132.5 1.2 convolution_add_fusion.16
  133.7 1.2 convolution_add_fusion.15
  134.9 1.2 convolution_add_fusion.14
  136.1 1.2 convolution_add_fusion.13
  137.3 1.2 convolution_add_fusion.12
  138.5 1.2 convolution_add_fusion.11
  139.6 1.2 convolution_add_fusion.10
  140.8 1.2 convolution_add_fusion.9
  142.0 1.2 convolution_add_fusion.8
  143.2 1.2 fusion.2
  144.4 1.2 convolution_add_fusion.6
  145.6 1.2 convolution_add_fusion.5
  146.8 1.2 convolution_add_fusion.4
  148.0 1.2 convolution_add_fusion.3
  149.2 1.2 fusion.1
  150.4 0.0 copy-done.1
  150.4 0.1 fusion.38
  150.5 0.0 copy-done.3
  150.5 0.1 fusion.40
  150.6 0.3 convolution_convert_fusion
  150.9 0.6 fusion.45
  151.5 0.0 all-gather.6.cloned.1.call-update
  151.6 0.0 all-gather.8.cloned.1.call-start
  151.6 0.7 all-gather.8.cloned.1.call-update
  152.3 57.7 %all-gather.6.cloned.1.call-done = bf16[2,1024,384]{2,1,0:T(8,128)(2,1)} async-done(((bf16[2,32,384]{2,1,0:T(8,128)(2,1)}), bf16[2,1024,384]{2,1,0:T(8,128)(2,1)}) %all-gather.6.cloned.1.call-update) | async-done | bytes 1572880 | tf_op jit(solution)/shard_map/all_gather | solution.py:82
  210.1 2.1 fusion.50
  212.1 0.2 fusion.25
  212.3 58.9 %all-gather.8.cloned.1.call-done = bf16[2,1024,384]{2,1,0:T(8,128)(2,1)} async-done(((bf16[2,32,384]{2,1,0:T(8,128)(2,1)}), bf16[2,1024,384]{2,1,0:T(8,128)(2,1)}) %all-gather.8.cloned.1.call-update) | async-done | bytes 1572880 | tf_op jit(solution)/shard_map/all_gather | solution.py:94
  271.3 1.8 fusion.11
  273.1 0.8 fusion.12
  (12 shorter events, 0.1 us)
Async XLA Ops:
  6.5 144.1 %copy-start = (bf16[384,1152]{1,0:T(8,128)(2,1)S(1)}, bf16[384,1152]{1,0:T(8,128)(2,1)}, u32[]{:S(2)}) copy-start(bf16[384,1152]{1,0:T(8,128)(2,1)} %param.10) | copy-start | bytes 2654212
  6.5 111.6 %all-gather.4.cloned.1.call-start = ((), (), s32[]{:S(2)}) async-start(), calls=%async_computation | async-start | bytes 8460288 | tf_op jit(solution)/shard_map/all_gather | solution.py:65
  7.3 202.8 %all-gather.6.cloned.1.call-start = ((), (), s32[]{:S(2)}) async-start(), calls=%async_computation.1 | async-start | bytes 1622016 | tf_op jit(solution)/shard_map/all_gather | solution.py:82
  9.1 10.1 %collective-permute-start = (bf16[2,1,16,384]{3,2,1,0:T(8,128)(2,1)S(1)}, bf16[2,1,16,384]{3,2,1,0:T(8,128)(2,1)S(1)}, u32[]{:S(2)}, u32[]{:S(2)}) collective-permute-start(bf16[2,1,16,384]{3,2,1,0:T(8,128)(2,1)S(1)} %get-tuple-element.39), channel_id=1, source_target_pairs={{0,4},{4,8},{8,12},{12,16},{16,20},{20,24},{24,28},{1,5},{5,9},{9,... | collective-permute-start | bytes 73736 | tf_op jit(solution)/shard_map/ppermute | solution.py:15
  13.7 6.3 %collective-permute-start.1 = (bf16[2,1,16,384]{3,2,1,0:T(8,128)(2,1)S(1)}, bf16[2,1,16,384]{3,2,1,0:T(8,128)(2,1)S(1)}, u32[]{:S(2)}, u32[]{:S(2)}) collective-permute-start(bf16[2,1,16,384]{3,2,1,0:T(8,128)(2,1)S(1)} %get-tuple-element.40), channel_id=1, source_target_pairs={{4,0},{8,4},{12,8},{16,12},{20,16},{24,20},{28,24},{5,1},{9,5},{13... | collective-permute-start | bytes 73736 | tf_op jit(solution)/shard_map/ppermute | solution.py:17
  20.1 3.3 %collective-permute-start.2 = (bf16[2,4,1,384]{3,2,1,0:T(2,128)(2,1)S(1)}, bf16[2,4,1,384]{3,2,1,0:T(2,128)(2,1)S(1)}, u32[]{:S(2)}, u32[]{:S(2)}) collective-permute-start(bf16[2,4,1,384]{3,2,1,0:T(2,128)(2,1)S(1)} %get-tuple-element.35), channel_id=1, source_target_pairs={{0,1},{1,2},{2,3},{4,5},{5,6},{6,7},{8,9},{9,10},{10,11},{12,13},{... | collective-permute-start | bytes 18440 | tf_op jit(solution)/shard_map/ppermute | solution.py:15
  22.0 4.4 %collective-permute-start.3 = (bf16[2,4,1,384]{3,2,1,0:T(2,128)(2,1)S(1)}, bf16[2,4,1,384]{3,2,1,0:T(2,128)(2,1)S(1)}, u32[]{:S(2)}, u32[]{:S(2)}) collective-permute-start(bf16[2,4,1,384]{3,2,1,0:T(2,128)(2,1)S(1)} %get-tuple-element.36), channel_id=1, source_target_pairs={{1,0},{2,1},{3,2},{5,4},{6,5},{7,6},{9,8},{10,9},{11,10},{13,12},{... | collective-permute-start | bytes 18440 | tf_op jit(solution)/shard_map/ppermute | solution.py:17
  26.5 9.3 %collective-permute-start.4 = (bf16[2,4,18,384]{3,2,1,0:T(8,128)(2,1)S(1)}, bf16[2,4,18,384]{3,2,1,0:T(8,128)(2,1)S(1)}, u32[]{:S(2)}, u32[]{:S(2)}) collective-permute-start(bf16[2,4,18,384]{3,2,1,0:T(8,128)(2,1)S(1)} %pad_maximum_fusion), channel_id=1, source_target_pairs={{0,32},{32,64},{64,96},{96,128},{128,160},{160,192},{192,224},{224... | collective-permute-start | bytes 331784 | tf_op jit(solution)/shard_map/ppermute | solution.py:27
  36.0 114.4 %copy-start.1 = (bf16[2,2,16,384]{3,2,1,0:T(8,128)(2,1)S(1)}, bf16[2,2,16,384]{3,2,1,0:T(8,128)(2,1)}, u32[]{:S(2)}) copy-start(bf16[2,2,16,384]{3,2,1,0:T(8,128)(2,1)} %param.6) | copy-start | bytes 147460
  36.0 114.5 %copy-start.3 = (f32[384]{0:T(512)S(1)}, f32[384]{0:T(512)}, u32[]{:S(2)}) copy-start(f32[384]{0:T(512)} %param.9) | copy-start | bytes 4612
  130.0 143.0 %copy-start.2 = (bf16[384,384]{1,0:T(8,128)(2,1)S(1)}, bf16[384,384]{1,0:T(8,128)(2,1)}, u32[]{:S(2)}) copy-start(bf16[384,384]{1,0:T(8,128)(2,1)} %param.11) | copy-start | bytes 884740
  151.6 119.7 %all-gather.8.cloned.1.call-start = ((), (), s32[]{:S(2)}) async-start(), calls=%async_computation.2 | async-start | bytes 1622016 | tf_op jit(solution)/shard_map/all_gather | solution.py:94
Sparse Core Ops, SparseCore 0:
  9.4 108.6 all-gather.3
  151.7 58.3 all-gather.5
  213.2 57.9 all-gather.7
where the time goes:
time: 282 us; the launch traced here: 280 us
  waiting for transfers between devices  210 us (74%)
  matrix products  37.2 us (13%)
  starting transfers between devices  16.9 us (6%)
  between operations  13.3 us (5%)
    all_gather x1, waiting for transfers between devices, local(): lax.all_gather(conv_weight, 'tm', axis=4, tiled=True)  82.1 us
    all_gather x1, waiting for transfers between devices, local(): lax.all_gather(value_rows, ('height', 'width'), axis=1, tiled=True)  58.9 us
    all_gather x1, waiting for transfers between devices, local(): lax.all_gather(key_rows, ('height', 'width'), axis=1, tiled=True)  57.7 us
    dot_general x27, matrix products, conv_taps(): jnp.dot(window.reshape(-1, channels), weight[time_tap, row_tap, col_tap],...  32.2 us
    ppermute x2, starting transfers between devices, with_halo(): lax.ppermute(head, axis, [((i + 1) % count, i) for i in range(ends)])  6.78 us
    ppermute x2, starting transfers between devices, with_halo(): lax.ppermute(tail, axis, [(i, (i + 1) % count) for i in range(ends)])  6.54 us
  transfers between devices with their start and end apart: 8, of which 6 were waited for; matrix products, arithmetic and copies ran while one was open for 2% of the time, Pallas kernels for 0%

commit v1 on v0

v1 whole, which is shorter than its diff:
```python
import functools

import jax
import jax.numpy as jnp
from jax import lax
from jax.experimental import pallas as pl
from jax.experimental.pallas import tpu as pltpu
from jax.sharding import Mesh, PartitionSpec as P

F32 = jnp.float32
BF16 = jnp.bfloat16
TAPS = 27
GROUP = 24
SLOT = 32
DEPTH = 896
PLANE = ("y", "width")
VMEM = pl.BlockSpec(memory_space=pltpu.VMEM)
SMEM = pl.BlockSpec(memory_space=pltpu.SMEM)
LIMIT = 48 * 1024 * 1024


def call(body, out, specs, flops=1_000_000, moved=1_000_000, scratch=()):
    many = isinstance(out, (tuple, list))
    return pl.pallas_call(
        body,
        out_shape=out,
        in_specs=specs,
        out_specs=[VMEM] * len(out) if many else VMEM,
        scratch_shapes=list(scratch),
        compiler_params=pltpu.CompilerParams(vmem_limit_bytes=LIMIT),
        cost_estimate=pl.CostEstimate(flops=flops, bytes_accessed=moved, transcendentals=0),
    )


def rms_scale(values, gain):
    mean_sq = jnp.mean(values * values, axis=-1, keepdims=True)
    return values * lax.rsqrt(mean_sq + 1e-06) * gain


def weight_body(chip_ref, weight_ref, out_ref):
    start = chip_ref[0] * GROUP
    source = lax.broadcasted_iota(jnp.int32, (384, 128), 0)
    target = lax.broadcasted_iota(jnp.int32, (384, 128), 1)
    tiles = [jnp.zeros((GROUP, 128), F32) for _ in range(7)]
    for place in range(4):
        offset = target - place * SLOT
        wanted = (offset >= 0) & (offset < GROUP) & (source == start + offset)
        pick = wanted.astype(F32).astype(BF16)
        for tile in range(7):
            tap = tile * 4 + place
            if tap < TAPS:
                tiles[tile] += jnp.dot(weight_ref[tap], pick, preferred_element_type=F32)
    for tile in range(7):
        value = tiles[tile].astype(BF16)
        for plane in range(out_ref.shape[0]):
            out_ref[plane, :, tile * 128 : tile * 128 + 128] = value


def activate_body(before_ref, now_ref, gain_ref, out_ref):
    gain = gain_ref[...]
    halves = []
    for ref in (before_ref, now_ref):
        scaled = rms_scale(ref[...].astype(F32), gain)
        halves.append(scaled / (1.0 + jnp.exp(-scaled)))
    turned = jnp.concatenate(halves, axis=0).T
    later = pltpu.roll(turned, 96, 1)
    blank = jnp.zeros((SLOT - GROUP, 128), F32)
    for core, whole in ((0, turned), (1, later)):
        for chip in range(16):
            block = jnp.concatenate([whole[chip * GROUP : chip * GROUP + GROUP], blank], axis=0)
            out_ref[chip // 4, core, chip % 4] = block.astype(BF16)


def patch_body(cells_ref, out_ref):
    source = lax.broadcasted_iota(jnp.int32, (128, 384), 0)
    target = lax.broadcasted_iota(jnp.int32, (128, 384), 1)
    frame, row, col = source // 32, (source // 16) % 2, source % 16
    lane = lax.broadcasted_iota(jnp.int32, (256, 128), 1)
    grid = jnp.zeros((256, 384), F32)
    for width in range(4):
        place = (frame < 3) & (target == frame * 128 + row * 64 + width * 16 + col)
        rows = jnp.concatenate([cells_ref[height, width] for height in range(8)], axis=0)
        grid += jnp.dot(rows, place.astype(F32).astype(BF16), preferred_element_type=F32)
    blank = jnp.zeros((SLOT, 128), F32)
    for time_tap in range(3):
        still = grid[:, time_tap * 128 : time_tap * 128 + 128]
        left = jnp.where(lane % 64 == 0, 0.0, pltpu.roll(still, 1, 1))
        right = jnp.where(lane % 64 == 63, 0.0, pltpu.roll(still, 127, 1))
        for col_tap, base in enumerate((left, still, right)):
            swapped = pltpu.roll(base, 64, 1)
            above = jnp.concatenate([blank, swapped[:-SLOT]], axis=0)
            below = jnp.concatenate([swapped[SLOT:], blank], axis=0)
            up = jnp.where(lane < 64, above, swapped)
            down = jnp.where(lane < 64, swapped, below)
            for row_tap, value in enumerate((up, base, down)):
                tap = (time_tap * 3 + row_tap) * 3 + col_tap
                value = value.astype(BF16)
                for height in range(8):
                    out_ref[tap * SLOT : tap * SLOT + SLOT, height * 128 : height * 128 + 128] = value[
                        height * SLOT : height * SLOT + SLOT
                    ]
    out_ref[TAPS * SLOT :, :] = jnp.zeros((DEPTH - TAPS * SLOT, 1024), BF16)


def conv_body(patch_ref, weight_ref, out_ref):
    for part in range(4):
        turned = jnp.dot(
            weight_ref[...], patch_ref[:, part * 256 : part * 256 + 256], preferred_element_type=F32
        )
        summed = turned.T.astype(BF16)
        for row in range(4):
            for width in range(4):
                out_ref[part * 4 + width, row * 16 : row * 16 + 16, :] = summed[
                    row * 64 + width * 16 : row * 64 + width * 16 + 16
                ]


def hidden_body(part_ref, latent_ref, gain_ref, hidden_ref, normed_ref):
    summed = latent_ref[...].astype(F32)
    for source in range(16):
        summed += part_ref[source].astype(F32)
    hidden = summed.astype(BF16)
    hidden_ref[...] = hidden
    normed = rms_scale(hidden.astype(F32), gain_ref[...]).astype(BF16)
    for target in range(16):
        normed_ref[target] = normed


def query_body(normed_ref, w_ref, out_ref):
    query = jnp.dot(normed_ref[0], w_ref[:, :384], preferred_element_type=F32).astype(BF16)
    out_ref[...] = lax.dot_general(
        query, w_ref[:, 384:768], (((1,), (1,)), ((), ())), preferred_element_type=F32
    ).astype(BF16)


def attend_body(core_ref, query_ref, cells_ref, hidden_ref, w_ref, w_out_ref, keep_ref, send_ref):
    cells = cells_ref[...]
    scores = lax.dot_general(
        query_ref[...], cells, (((1,), (1,)), ((), ())), preferred_element_type=F32
    ) * (1.0 / 384.0**0.5)
    powers = jnp.exp(scores - jnp.max(scores, axis=-1, keepdims=True))
    total = jnp.sum(powers, axis=-1, keepdims=True)
    mixed = jnp.dot(powers.astype(BF16), cells, preferred_element_type=F32) / total
    attended = jnp.dot(mixed.astype(BF16), w_ref[:, 768:], preferred_element_type=F32)
    update = jnp.dot(attended.astype(BF16), w_out_ref[...], preferred_element_type=F32)
    decoded = (hidden_ref[...].astype(F32) + update).astype(BF16)
    first = core_ref[0] == 0
    keep_ref[...] = jnp.where(first, decoded[:32], decoded[32:])
    send_ref[...] = jnp.where(first, decoded[32:], decoded[:32])


def local(latent, norm_gain, conv_weight, attn_gain, w_qkv, w_out):
    channels = 384
    core = lax.axis_index("core")
    chip = lax.axis_index("y") * 4 + lax.axis_index("width")
    swap = [(0, 1), (1, 0)]
    shape = jax.ShapeDtypeStruct
    with jax.named_scope("weight_slices"):
        turned = jnp.transpose(conv_weight.reshape(TAPS, channels, GROUP), (0, 2, 1))
        pieces = call(weight_body, shape((16, GROUP, DEPTH), BF16), [SMEM, VMEM])(
            chip.astype(jnp.int32).reshape(1), turned
        )
        weight = lax.all_to_all(pieces, "tm", 0, 0).reshape(channels, DEPTH)
    with jax.named_scope("earlier_frames"):
        cells = latent.reshape(64, channels)
        before = lax.ppermute(cells, "tm", [(i, i + 1) for i in range(15)])
    with jax.named_scope("activated"):
        blocks = call(activate_body, shape((4, 2, 4, SLOT, 128), BF16), [VMEM] * 3)(
            before, cells, norm_gain.reshape(1, channels)
        )
        blocks = lax.all_to_all(blocks.reshape(32, SLOT, 128), ("y", "core", "width"), 0, 0)
        patches = call(patch_body, shape((DEPTH, 1024), BF16), [VMEM])(blocks.reshape(8, 4, SLOT, 128))
    with jax.named_scope("own_latent"):
        first = core == 0
        kept = jnp.where(first, cells[:32], cells[32:])
        other = lax.ppermute(jnp.where(first, cells[32:], cells[:32]), "core", swap)
        own = jnp.where(first, jnp.concatenate([kept, other]), jnp.concatenate([other, kept]))
    with jax.named_scope("conv"):
        parts = call(conv_body, shape((16, 64, channels), BF16), [VMEM] * 2, 700_000_000)(patches, weight)
        parts = lax.all_to_all(parts, PLANE, 0, 0)
    with jax.named_scope("hidden"):
        hidden, normed = call(
            hidden_body, [shape((64, channels), BF16), shape((16, 64, channels), BF16)], [VMEM] * 3
        )(parts, own, attn_gain.reshape(1, channels))
    with jax.named_scope("keys"):
        gathered = lax.all_to_all(normed, PLANE, 0, 0).reshape(1024, channels)
    with jax.named_scope("query"):
        query = call(query_body, shape((64, channels), BF16), [VMEM] * 2, 40_000_000)(normed, w_qkv)
    with jax.named_scope("attention"):
        half = shape((32, channels), BF16)
        keep, send = call(attend_body, [half, half], [SMEM] + [VMEM] * 5, 200_000_000)(
            core.astype(jnp.int32).reshape(1), query, gathered, hidden, w_qkv, w_out
        )
        other = lax.ppermute(send, "core", swap)
        out = jnp.where(first, jnp.concatenate([keep, other]), jnp.concatenate([other, keep]))
    return out.reshape(latent.shape)


def solution(mesh):
    devices = mesh.devices.reshape(16, 4, 2, 4)
    fine = Mesh(devices, ("tm", "y", "core", "width"))
    cells = P("tm", ("y", "core"), "width", None)
    in_specs = (cells, P(), P(None, None, None, None, "tm"), P(), P(), P())
    return jax.shard_map(local, mesh=fine, in_specs=in_specs, out_specs=cells, check_vma=False)
```

time: 282 us -> 117 us (0.41)
  waiting for transfers between devices: 210 us -> 51 us
  matrix products: 37.2 us -> 0 us
  starting transfers between devices: 16.9 us -> 53.6 us
  between operations: 13.3 us -> 0.15 us
  Pallas kernels: 0 us -> 8.72 us
    all_gather x3 -> x0, waiting for transfers between devices: 199 us -> none  [the longest x1 82.1 us: local(): lax.all_gather(conv_weight, 'tm', axis=4, tiled=True)]
    all_to_all x0 -> x4, waiting for transfers between devices: none -> 48.6 us  [the longest x1 29.9 us: local(): weight = lax.all_to_all(pieces, 'tm', 0, 0).reshape(channels, DEPTH)]
    dot_general x31 -> x0, matrix products: 37.2 us -> none  [the longest x27 32.2 us: conv_taps(): jnp.dot(window.reshape(-1, channels), weight[time_tap, row_tap, col_tap],...]
    all_to_all x0 -> x4, starting transfers between devices: none -> 34.5 us  [the longest x1 16.4 us: local(): weight = lax.all_to_all(pieces, 'tm', 0, 0).reshape(channels, DEPTH)]
    pallas_call x0 -> x7, Pallas kernels: none -> 8.72 us  [the longest x1 1.97 us: local(): call(conv_body, shape((16, 64, channels), BF16), [VMEM] * 2, 700000000)]
    ppermute x5 -> x3, waiting for transfers between devices: 9.54 us -> 2.42 us  [the longest x1 0.83 us: local(): other = lax.ppermute(send, 'core', swap)]
    ppermute x5 -> x3, starting transfers between devices: 16.9 us -> 19 us  [the longest x1 8.36 us: local(): other = lax.ppermute(send, 'core', swap)]
  transfers between devices with their start and end apart: 8 -> 7, of which waited for: 6 -> 7; matrix products, arithmetic and copies ran while one was open for 2% -> 1% of each run, Pallas kernels for 0% -> 3%
where the time goes in v1:
time: 117 us
  starting transfers between devices  53.6 us (46%)
  waiting for transfers between devices  51 us (44%)
  Pallas kernels  8.72 us (7%)
  local copies, waits for them, and re-layouts  2.53 us (2%)
    all_to_all x1, waiting for transfers between devices, local(): weight = lax.all_to_all(pieces, 'tm', 0, 0).reshape(channels, DEPTH)  29.9 us
    all_to_all x1, starting transfers between devices, local(): weight = lax.all_to_all(pieces, 'tm', 0, 0).reshape(channels, DEPTH)  16.4 us
    all_to_all x1, waiting for transfers between devices, local(): gathered = lax.all_to_all(normed, PLANE, 0, 0).reshape(1024, channels)  9.03 us
    all_to_all x1, starting transfers between devices, local(): lax.all_to_all(blocks.reshape(32, SLOT, 128), ('y', 'core', 'width'), 0, 0)  8.61 us
    ppermute x1, starting transfers between devices, local(): other = lax.ppermute(send, 'core', swap)  8.36 us
    all_to_all x1, waiting for transfers between devices, local(): lax.all_to_all(blocks.reshape(32, SLOT, 128), ('y', 'core', 'width'), 0, 0)  6.38 us
    ppermute x1, starting transfers between devices, local(): other = lax.ppermute(jnp.where(first, cells[32:], cells[:32]), 'core', swap)  6.31 us
    all_to_all x1, starting transfers between devices, local(): parts = lax.all_to_all(parts, PLANE, 0, 0)  5.7 us
  transfers between devices with their start and end apart: 7, of which 7 were waited for; matrix products, arithmetic and copies ran while one was open for 1% of the time, Pallas kernels for 3%

profile of v1, /device:TPU:1, one launch (start us, length us, event | category | flops | bytes accessed | tf_op | source)
XLA Modules:
  0.0 116.6 jit_solution(4601239763141596498)
XLA Ops:
  0.0 4.4 %collective-permute-start = (bf16[64,384]{1,0:T(8,128)(2,1)}, bf16[64,384]{1,0:T(8,128)(2,1)S(1)}, u32[]{:S(2)}, u32[]{:S(2)}) collective-permute-start(bf16[64,384]{1,0:T(8,128)(2,1)} %bitcast.17), channel_id=1, source_target_pairs={{0,32},{32,64},{64,96},{96,128},{128,160},{160,192},{192,224},{224... | collective-permute-start | bytes 147464 | tf_op jit(solution)/shard_map/earlier_frames/ppermute | solution.py:166
  4.4 0.7 reshape.43.gain_ref
  5.1 0.8 collective-permute-done.before_ref
  5.8 0.0 copy-start.3
  5.8 0.8 copy-done.3
  6.6 1.0 activated.2
  7.7 8.6 %all-to-all-start = ((bf16[32,32,128]{2,1,0:T(8,128)(2,1)}), bf16[32,32,128]{2,1,0:T(8,128)(2,1)S(1)}, u32[]{:S(2)}, u32[]{:S(2)}) async-start(bf16[32,32,128]{2,1,0:T(8,128)(2,1)} %bitcast.2), calls=%async_computation | async-start | bytes 524288 | tf_op jit(solution)/shard_map/activated/all_to_all | solution.py:171
  16.3 0.0 copy-start.1
  16.3 1.0 copy-done.1
  17.3 1.5 %weight_slices.1 = bf16[16,24,896]{2,1,0:T(8,128)(2,1)} custom-call(s32[1]{0:T(128)} %bitcast.4.chip_ref, bf16[27,24,384]{2,1,0:T(8,128)(2,1)S(1)} %bitcast.16), custom_call_target="tpu_custom_call" | custom-call | flops 1000000 | bytes 1000000 | tf_op jit(solution)/shard_map/weight_slices/pallas_call | solution.py:160
  18.8 6.4 %all-to-all-done = bf16[32,32,128]{2,1,0:T(8,128)(2,1)S(1)} async-done(((bf16[32,32,128]{2,1,0:T(8,128)(2,1)}), bf16[32,32,128]{2,1,0:T(8,128)(2,1)S(1)}, u32[]{:S(2)}, u32[]{:S(2)}) %all-to-all-start) | async-done | bytes 262176 | tf_op jit(solution)/shard_map/activated/all_to_all | solution.py:171
  25.2 16.4 %all-to-all-start.1 = ((bf16[16,24,896]{2,1,0:T(8,128)(2,1)}), bf16[16,24,896]{2,1,0:T(8,128)(2,1)S(1)}, u32[]{:S(2)}, u32[]{:S(2)}) async-start(bf16[16,24,896]{2,1,0:T(8,128)(2,1)} %weight_slices.1), calls=%async_computation.1 | async-start | bytes 1376256 | tf_op jit(solution)/shard_map/weight_slices/all_to_all | solution.py:163
  41.6 0.7 activated.3.patch_ref
  42.3 29.9 %all-to-all-done.1 = bf16[16,24,896]{2,1,0:T(8,128)(2,1)S(1)} async-done(((bf16[16,24,896]{2,1,0:T(8,128)(2,1)}), bf16[16,24,896]{2,1,0:T(8,128)(2,1)S(1)}, u32[]{:S(2)}, u32[]{:S(2)}) %all-to-all-start.1) | async-done | bytes 688160 | tf_op jit(solution)/shard_map/weight_slices/all_to_all | solution.py:163
  72.2 0.0 copy-start.4
  72.2 0.0 copy-start.5
  72.3 2.0 %conv.1 = bf16[16,64,384]{2,1,0:T(8,128)(2,1)} custom-call(bf16[896,1024]{1,0:T(8,128)(2,1)S(1)} %activated.3.patch_ref, bf16[384,896]{1,0:T(8,128)(2,1)S(1)} %bitcast.14), custom_call_target="tpu_custom_call" | custom-call | flops 700000000 | bytes 1000000 | tf_op jit(solution)/shard_map/conv/pallas_call | solution.py:179
  74.2 0.0 copy-start
  74.2 5.7 %all-to-all-start.2 = ((bf16[16,64,384]{2,1,0:T(8,128)(2,1)}), bf16[16,64,384]{2,1,0:T(8,128)(2,1)S(1)}, u32[]{:S(2)}, u32[]{:S(2)}) async-start(bf16[16,64,384]{2,1,0:T(8,128)(2,1)} %conv.1), calls=%async_computation.2 | async-start | bytes 1572864 | tf_op jit(solution)/shard_map/conv/all_to_all | solution.py:180
  79.9 0.0 copy-done.4
  80.0 6.3 %collective-permute-start.1 = (bf16[32,384]{1,0:T(8,128)(2,1)S(1)}, bf16[32,384]{1,0:T(8,128)(2,1)S(1)}, u32[]{:S(2)}, u32[]{:S(2)}) collective-permute-start(bf16[32,384]{1,0:T(8,128)(2,1)S(1)} %bitcast.20), channel_id=1, source_target_pairs={{0,4},{4,0},{1,5},{5,1},{2,6},{6,2},{3,7},{7,3},{8,12},{12,8},{9,1... | collective-permute-start | bytes 73736 | tf_op jit(solution)/shard_map/own_latent/ppermute | solution.py:176
  86.3 0.0 copy-done.5
  86.3 0.8 collective-permute-done.1
  87.1 3.2 %all-to-all-done.2.part_ref = bf16[16,64,384]{2,1,0:T(8,128)(2,1)S(1)} async-done(((bf16[16,64,384]{2,1,0:T(8,128)(2,1)}), bf16[16,64,384]{2,1,0:T(8,128)(2,1)S(1)}, u32[]{:S(2)}, u32[]{:S(2)}) %all-to-all-start.2) | async-done | bytes 786464 | tf_op jit(solution)/shard_map/conv/all_to_all | solution.py:180
  90.4 1.1 hidden.1
  91.5 0.0 copy-start.2
  91.5 3.8 %all-to-all-start.3 = ((bf16[16,64,384]{2,1,0:T(8,128)(2,1)}), bf16[16,64,384]{2,1,0:T(8,128)(2,1)S(1)}, u32[]{:S(2)}, u32[]{:S(2)}) async-start(bf16[16,64,384]{2,1,0:T(8,128)(2,1)} %get-tuple-element.9.normed_ref), calls=%async_computation.3 | async-start | bytes 1572864 | tf_op jit(solution)/shard_map/keys/all_to_all | solution.py:186
  95.3 0.0 copy-done
  95.3 1.5 %query.1.query_ref = bf16[64,384]{1,0:T(8,128)(2,1)S(1)} custom-call(bf16[16,64,384]{2,1,0:T(8,128)(2,1)} %get-tuple-element.9.normed_ref, bf16[384,1152]{1,0:T(8,128)(2,1)S(1)} %copy-done), custom_call_target="tpu_custom_call" | custom-call | flops 40000000 | bytes 1000000 | tf_op jit(solution)/shard_map/query/pallas_call | solution.py:188
  96.8 9.0 %all-to-all-done.3 = bf16[16,64,384]{2,1,0:T(8,128)(2,1)S(1)} async-done(((bf16[16,64,384]{2,1,0:T(8,128)(2,1)}), bf16[16,64,384]{2,1,0:T(8,128)(2,1)S(1)}, u32[]{:S(2)}, u32[]{:S(2)}) %all-to-all-start.3) | async-done | bytes 786464 | tf_op jit(solution)/shard_map/keys/all_to_all | solution.py:186
  105.8 0.0 copy-done.2
  105.8 1.0 attention.1
  106.8 8.4 %collective-permute-start.2 = (bf16[32,384]{1,0:T(8,128)(2,1)S(1)}, bf16[32,384]{1,0:T(8,128)(2,1)S(1)}, u32[]{:S(2)}, u32[]{:S(2)}) collective-permute-start(bf16[32,384]{1,0:T(8,128)(2,1)S(1)} %get-tuple-element.12), channel_id=1, source_target_pairs={{0,4},{4,0},{1,5},{5,1},{2,6},{6,2},{3,7},{7,3},{8,12},{12,8},{9,1... | collective-permute-start | bytes 73736 | tf_op jit(solution)/shard_map/attention/ppermute | solution.py:194
  115.2 0.8 collective-permute-done.2
  116.0 0.6 maximum_select_fusion.1
  (3 shorter events, 0.0 us)
Async XLA Ops:
  0.0 5.8 %collective-permute-start = (bf16[64,384]{1,0:T(8,128)(2,1)}, bf16[64,384]{1,0:T(8,128)(2,1)S(1)}, u32[]{:S(2)}, u32[]{:S(2)}) collective-permute-start(bf16[64,384]{1,0:T(8,128)(2,1)} %bitcast.17), channel_id=1, source_target_pairs={{0,32},{32,64},{64,96},{96,128},{128,160},{160,192},{192,224},{224... | collective-permute-start | bytes 147464 | tf_op jit(solution)/shard_map/earlier_frames/ppermute | solution.py:166
  5.8 0.8 copy-start.3
  7.7 17.5 %all-to-all-start = ((bf16[32,32,128]{2,1,0:T(8,128)(2,1)}), bf16[32,32,128]{2,1,0:T(8,128)(2,1)S(1)}, u32[]{:S(2)}, u32[]{:S(2)}) async-start(bf16[32,32,128]{2,1,0:T(8,128)(2,1)} %bitcast.2), calls=%async_computation | async-start | bytes 524288 | tf_op jit(solution)/shard_map/activated/all_to_all | solution.py:171
  16.3 1.0 copy-start.1
  25.2 47.1 %all-to-all-start.1 = ((bf16[16,24,896]{2,1,0:T(8,128)(2,1)}), bf16[16,24,896]{2,1,0:T(8,128)(2,1)S(1)}, u32[]{:S(2)}, u32[]{:S(2)}) async-start(bf16[16,24,896]{2,1,0:T(8,128)(2,1)} %weight_slices.1), calls=%async_computation.1 | async-start | bytes 1376256 | tf_op jit(solution)/shard_map/weight_slices/all_to_all | solution.py:163
  72.2 7.7 %copy-start.4 = (bf16[2,2,16,384]{3,2,1,0:T(8,128)(2,1)S(1)}, bf16[2,2,16,384]{3,2,1,0:T(8,128)(2,1)}, u32[]{:S(2)}) copy-start(bf16[2,2,16,384]{3,2,1,0:T(8,128)(2,1)} %param.6) | copy-start | bytes 147460
  72.2 14.0 %copy-start.5 = (f32[384]{0:T(512)S(1)}, f32[384]{0:T(512)}, u32[]{:S(2)}) copy-start(f32[384]{0:T(512)} %param.9) | copy-start | bytes 4612
  74.2 21.0 %copy-start = (bf16[384,1152]{1,0:T(8,128)(2,1)S(1)}, bf16[384,1152]{1,0:T(8,128)(2,1)}, u32[]{:S(2)}) copy-start(bf16[384,1152]{1,0:T(8,128)(2,1)} %w_ref.3) | copy-start | bytes 2654212
  74.2 16.1 %all-to-all-start.2 = ((bf16[16,64,384]{2,1,0:T(8,128)(2,1)}), bf16[16,64,384]{2,1,0:T(8,128)(2,1)S(1)}, u32[]{:S(2)}, u32[]{:S(2)}) async-start(bf16[16,64,384]{2,1,0:T(8,128)(2,1)} %conv.1), calls=%async_computation.2 | async-start | bytes 1572864 | tf_op jit(solution)/shard_map/conv/all_to_all | solution.py:180
  80.0 7.1 %collective-permute-start.1 = (bf16[32,384]{1,0:T(8,128)(2,1)S(1)}, bf16[32,384]{1,0:T(8,128)(2,1)S(1)}, u32[]{:S(2)}, u32[]{:S(2)}) collective-permute-start(bf16[32,384]{1,0:T(8,128)(2,1)S(1)} %bitcast.20), channel_id=1, source_target_pairs={{0,4},{4,0},{1,5},{5,1},{2,6},{6,2},{3,7},{7,3},{8,12},{12,8},{9,1... | collective-permute-start | bytes 73736 | tf_op jit(solution)/shard_map/own_latent/ppermute | solution.py:176
  91.5 14.3 %copy-start.2 = (bf16[384,384]{1,0:T(8,128)(2,1)S(1)}, bf16[384,384]{1,0:T(8,128)(2,1)}, u32[]{:S(2)}) copy-start(bf16[384,384]{1,0:T(8,128)(2,1)} %w_out_ref.1) | copy-start | bytes 884740
  91.5 14.3 %all-to-all-start.3 = ((bf16[16,64,384]{2,1,0:T(8,128)(2,1)}), bf16[16,64,384]{2,1,0:T(8,128)(2,1)S(1)}, u32[]{:S(2)}, u32[]{:S(2)}) async-start(bf16[16,64,384]{2,1,0:T(8,128)(2,1)} %get-tuple-element.9.normed_ref), calls=%async_computation.3 | async-start | bytes 1572864 | tf_op jit(solution)/shard_map/keys/all_to_all | solution.py:186
  106.8 9.2 %collective-permute-start.2 = (bf16[32,384]{1,0:T(8,128)(2,1)S(1)}, bf16[32,384]{1,0:T(8,128)(2,1)S(1)}, u32[]{:S(2)}, u32[]{:S(2)}) collective-permute-start(bf16[32,384]{1,0:T(8,128)(2,1)S(1)} %get-tuple-element.12), channel_id=1, source_target_pairs={{0,4},{4,0},{1,5},{5,1},{2,6},{6,2},{3,7},{7,3},{8,12},{12,8},{9,1... | collective-permute-start | bytes 73736 | tf_op jit(solution)/shard_map/attention/ppermute | solution.py:194

commit v2 on v1

v2 whole, which is shorter than its diff:
```python
import functools

import jax
import jax.numpy as jnp
from jax import lax
from jax.experimental import pallas as pl
from jax.experimental.pallas import tpu as pltpu
from jax.sharding import Mesh, PartitionSpec as P

F32 = jnp.float32
BF16 = jnp.bfloat16
TAPS = 27
GROUP = 24
HALF = 14
DEPTH = 384
PLANE = ("y", "width")
VMEM = pl.BlockSpec(memory_space=pltpu.VMEM)
SMEM = pl.BlockSpec(memory_space=pltpu.SMEM)
LIMIT = 24 * 1024 * 1024


def call(body, out, specs, flops=1_000_000, moved=1_000_000, scratch=()):
    many = isinstance(out, (tuple, list))
    return pl.pallas_call(
        body,
        out_shape=out,
        in_specs=specs,
        out_specs=[VMEM] * len(out) if many else VMEM,
        scratch_shapes=list(scratch),
        compiler_params=pltpu.CompilerParams(vmem_limit_bytes=LIMIT),
        cost_estimate=pl.CostEstimate(flops=flops, bytes_accessed=moved, transcendentals=0),
    )


def rms_scale(values, gain):
    mean_sq = jnp.mean(values * values, axis=-1, keepdims=True)
    return values * lax.rsqrt(mean_sq + 1e-06) * gain


def weight_body(place_ref, weight_ref, out_ref):
    start = place_ref[0] * GROUP
    first_tap = place_ref[1] * HALF
    source = lax.broadcasted_iota(jnp.int32, (384, 128), 0)
    target = lax.broadcasted_iota(jnp.int32, (384, 128), 1)
    pick = ((target < GROUP) & (source == start + target)).astype(F32).astype(BF16)
    rows = [weight_ref[jnp.minimum(first_tap + tap, TAPS - 1)] for tap in range(HALF)]
    picked = jnp.dot(jnp.concatenate(rows, axis=0), pick, preferred_element_type=F32)
    lane = lax.broadcasted_iota(jnp.int32, (GROUP, 128), 1)
    tiles = [jnp.zeros((GROUP, 128), F32) for _ in range(3)]
    for tap in range(HALF):
        value = picked[tap * GROUP : tap * GROUP + GROUP]
        if tap == HALF - 1:
            value = jnp.where(first_tap + tap < TAPS, value, 0.0)
        tile, offset = divmod(tap * GROUP, 128)
        value = pltpu.roll(value, offset, 1) if offset else value
        if offset + GROUP > 128:
            tiles[tile] += jnp.where(lane >= offset, value, 0.0)
            tiles[tile + 1] += jnp.where(lane < offset, value, 0.0)
        else:
            tiles[tile] += value
    whole = jnp.concatenate(tiles, axis=1).astype(BF16)
    for plane in range(16):
        out_ref[plane] = whole


def activate_body(before_ref, now_ref, gain_ref, out_ref):
    gain = gain_ref[...]
    halves = []
    for ref in (before_ref, now_ref):
        scaled = rms_scale(ref[...].astype(F32), gain)
        halves.append(scaled / (1.0 + jnp.exp(-scaled)))
    turned = jnp.concatenate(halves, axis=0).T
    later = pltpu.roll(turned, 96, 1)
    for core, whole in ((0, turned), (1, later)):
        for chip in range(16):
            out_ref[chip // 4, core, chip % 4] = whole[chip * GROUP : chip * GROUP + GROUP].astype(BF16)


def patch_body(cells_ref, out_ref, held_ref):
    source = lax.broadcasted_iota(jnp.int32, (128, 384), 0)
    target = lax.broadcasted_iota(jnp.int32, (128, 384), 1)
    frame, row, col = source // 32, (source // 16) % 2, source % 16
    lane = lax.broadcasted_iota(jnp.int32, (8 * GROUP, 128), 1)
    grid = jnp.zeros((8 * GROUP, 384), F32)
    for width in range(4):
        place = (frame < 3) & (target == frame * 128 + row * 64 + width * 16 + col)
        rows = jnp.concatenate([cells_ref[height, width].astype(F32) for height in range(8)], axis=0)
        grid += jnp.dot(rows.astype(BF16), place.astype(F32).astype(BF16), preferred_element_type=F32)
    blank = jnp.zeros((GROUP, 128), F32)
    for time_tap in range(3):
        still = grid[:, time_tap * 128 : time_tap * 128 + 128]
        left = jnp.where(lane % 64 == 0, 0.0, pltpu.roll(still, 1, 1))
        right = jnp.where(lane % 64 == 63, 0.0, pltpu.roll(still, 127, 1))
        for col_tap, base in enumerate((left, still, right)):
            swapped = pltpu.roll(base, 64, 1)
            above = jnp.concatenate([blank, swapped[:-GROUP]], axis=0)
            below = jnp.concatenate([swapped[GROUP:], blank], axis=0)
            up = jnp.where(lane < 64, above, swapped)
            down = jnp.where(lane < 64, swapped, below)
            for row_tap, value in enumerate((up, base, down)):
                half, tap = divmod((time_tap * 3 + row_tap) * 3 + col_tap, HALF)
                for height in range(8):
                    held_ref[
                        half, tap * GROUP : tap * GROUP + GROUP, height * 128 : height * 128 + 128
                    ] = value[height * GROUP : height * GROUP + GROUP]
    held_ref[0, HALF * GROUP :, :] = jnp.zeros((DEPTH - HALF * GROUP, 1024), F32)
    held_ref[1, (TAPS - HALF) * GROUP :, :] = jnp.zeros((DEPTH - (TAPS - HALF) * GROUP, 1024), F32)
    out_ref[...] = held_ref[...].astype(BF16)


def conv_body(place_ref, patch_ref, mine_ref, other_ref, out_ref):
    core = place_ref[1]
    for part in range(4):
        cut = slice(part * 256, part * 256 + 256)
        turned = jnp.dot(mine_ref[...], patch_ref[core, :, cut], preferred_element_type=F32)
        turned += jnp.dot(other_ref[...], patch_ref[1 - core, :, cut], preferred_element_type=F32)
        summed = turned.T.astype(BF16)
        for row in range(4):
            for width in range(4):
                out_ref[part * 4 + width, row * 16 : row * 16 + 16, :] = summed[
                    row * 64 + width * 16 : row * 64 + width * 16 + 16
                ]


def hidden_body(part_ref, latent_ref, gain_ref, hidden_ref, normed_ref):
    summed = latent_ref[...].astype(F32)
    for source in range(16):
        summed += part_ref[source].astype(F32)
    hidden = summed.astype(BF16)
    hidden_ref[...] = hidden
    normed = rms_scale(hidden.astype(F32), gain_ref[...]).astype(BF16)
    for target in range(16):
        normed_ref[target] = normed


def query_body(normed_ref, w_ref, out_ref):
    query = jnp.dot(normed_ref[0], w_ref[:, :384], preferred_element_type=F32).astype(BF16)
    out_ref[...] = lax.dot_general(
        query, w_ref[:, 384:768], (((1,), (1,)), ((), ())), preferred_element_type=F32
    ).astype(BF16)


def attend_body(place_ref, query_ref, cells_ref, hidden_ref, w_ref, w_out_ref, keep_ref, send_ref):
    cells = cells_ref[...]
    scores = lax.dot_general(
        query_ref[...], cells, (((1,), (1,)), ((), ())), preferred_element_type=F32
    ) * (1.0 / 384.0**0.5)
    powers = jnp.exp(scores - jnp.max(scores, axis=-1, keepdims=True))
    total = jnp.sum(powers, axis=-1, keepdims=True)
    mixed = jnp.dot(powers.astype(BF16), cells, preferred_element_type=F32) / total
    attended = jnp.dot(mixed.astype(BF16), w_ref[:, 768:], preferred_element_type=F32)
    update = jnp.dot(attended.astype(BF16), w_out_ref[...], preferred_element_type=F32)
    decoded = (hidden_ref[...].astype(F32) + update).astype(BF16)
    first = place_ref[1] == 0
    keep_ref[...] = jnp.where(first, decoded[:32], decoded[32:])
    send_ref[...] = jnp.where(first, decoded[32:], decoded[:32])


def local(latent, norm_gain, conv_weight, attn_gain, w_qkv, w_out):
    channels = 384
    core = lax.axis_index("core")
    chip = lax.axis_index("y") * 4 + lax.axis_index("width")
    place = jnp.stack([chip, core]).astype(jnp.int32)
    swap = [(0, 1), (1, 0)]
    shape = jax.ShapeDtypeStruct
    with jax.named_scope("earlier_frames"):
        cells = latent.reshape(64, channels)
        before = lax.ppermute(cells, "tm", [(i, i + 1) for i in range(15)])
    with jax.named_scope("weight_slices"):
        turned = jnp.transpose(conv_weight.reshape(TAPS, channels, GROUP), (0, 2, 1))
        pieces = call(weight_body, shape((16, GROUP, DEPTH), BF16), [SMEM, VMEM])(place, turned)
        mine = lax.all_to_all(pieces, "tm", 0, 0).reshape(channels, DEPTH)
        other_half = lax.ppermute(mine, "core", swap)
    with jax.named_scope("activated"):
        before, pieces = lax.optimization_barrier((before, pieces))
        blocks = call(activate_body, shape((4, 2, 4, GROUP, 128), BF16), [VMEM] * 3)(
            before, cells, norm_gain.reshape(1, channels)
        )
        blocks = lax.all_to_all(blocks.reshape(32, GROUP, 128), ("y", "core", "width"), 0, 0)
        patches = call(
            patch_body,
            shape((2, DEPTH, 1024), BF16),
            [VMEM],
            scratch=[pltpu.VMEM((2, DEPTH, 1024), F32)],
        )(blocks.reshape(8, 4, GROUP, 128))
    with jax.named_scope("own_latent"):
        first = core == 0
        kept = jnp.where(first, cells[:32], cells[32:])
        other = lax.ppermute(jnp.where(first, cells[32:], cells[:32]), "core", swap)
        own = jnp.where(first, jnp.concatenate([kept, other]), jnp.concatenate([other, kept]))
    with jax.named_scope("conv"):
        parts = call(conv_body, shape((16, 64, channels), BF16), [SMEM] + [VMEM] * 3, 700_000_000)(
            place, patches, mine, other_half
        )
        parts = lax.all_to_all(parts, PLANE, 0, 0)
    with jax.named_scope("hidden"):
        hidden, normed = call(
            hidden_body, [shape((64, channels), BF16), shape((16, 64, channels), BF16)], [VMEM] * 3
        )(parts, own, attn_gain.reshape(1, channels))
    with jax.named_scope("keys"):
        gathered = lax.all_to_all(normed, PLANE, 0, 0).reshape(1024, channels)
    with jax.named_scope("query"):
        query = call(query_body, shape((64, channels), BF16), [VMEM] * 2, 40_000_000)(normed, w_qkv)
    with jax.named_scope("attention"):
        half = shape((32, channels), BF16)
        keep, send = call(attend_body, [half, half], [SMEM] + [VMEM] * 5, 200_000_000)(
            place, query, gathered, hidden, w_qkv, w_out
        )
        other = lax.ppermute(send, "core", swap)
        out = jnp.where(first, jnp.concatenate([keep, other]), jnp.concatenate([other, keep]))
    return out.reshape(latent.shape)


def solution(mesh):
    devices = mesh.devices.reshape(16, 4, 2, 4)
    fine = Mesh(devices, ("tm", "y", "core", "width"))
    cells = P("tm", ("y", "core"), "width", None)
    in_specs = (cells, P(), P(None, None, None, None, "tm"), P(), P(), P())
    return jax.shard_map(local, mesh=fine, in_specs=in_specs, out_specs=cells, check_vma=False)
```

time: 117 us -> 108 us (0.923)
  blocking collectives: 0 us -> 45.3 us
  starting transfers between devices: 53.6 us -> 25.9 us
  waiting for transfers between devices: 51 us -> 24 us
    all_to_all x0 -> x2, blocking collectives: none -> 45.3 us  [the longest x1 29.3 us: local(): mine = lax.all_to_all(pieces, 'tm', 0, 0).reshape(channels, DEPTH)]
    all_to_all x2 -> x0, waiting for transfers between devices: 36.3 us -> none  [the longest x1 29.9 us: local(): weight = lax.all_to_all(pieces, 'tm', 0, 0).reshape(channels, DEPTH)]
    all_to_all x2 -> x0, starting transfers between devices: 25.1 us -> none  [the longest x1 16.4 us: local(): weight = lax.all_to_all(pieces, 'tm', 0, 0).reshape(channels, DEPTH)]
    ppermute x0 -> x1, starting transfers between devices: none -> 8.37 us  [local(): other_half = lax.ppermute(mine, 'core', swap)]
    all_to_all x1, waiting for transfers between devices: 3.24 us -> 10.3 us  [local(): parts = lax.all_to_all(parts, PLANE, 0, 0)]
    ppermute x1, starting transfers between devices: 8.36 us -> 4.45 us  [local(): other = lax.ppermute(send, 'core', swap)]
    ppermute x1, starting transfers between devices: 6.31 us -> 2.45 us  [local(): other = lax.ppermute(jnp.where(first, cells[32:], cells[:32]), 'core', swap)]
    all_to_all x1, waiting for transfers between devices: 9.03 us -> 11.2 us  [local(): gathered = lax.all_to_all(normed, PLANE, 0, 0).reshape(1024, channels)]
  transfers between devices with their start and end apart: 7 -> 6, of which waited for: 7 -> 5; matrix products, arithmetic and copies ran while one was open for 1% -> 1% of each run, Pallas kernels for 3% -> 2%
where the time goes in v2:
time: 108 us; the launch traced here: 107 us
  blocking collectives  45.3 us (42%)
  starting transfers between devices  25.9 us (24%)
  waiting for transfers between devices  24 us (22%)
  Pallas kernels  8.39 us (8%)
  local copies, waits for them, and re-layouts  2.54 us (2%)
    all_to_all x1, blocking collectives, local(): mine = lax.all_to_all(pieces, 'tm', 0, 0).reshape(channels, DEPTH)  29.3 us
    all_to_all x1, blocking collectives, local(): lax.all_to_all(blocks.reshape(32, GROUP, 128), ('y', 'core', 'width'), 0, 0)  16 us
    all_to_all x1, waiting for transfers between devices, local(): gathered = lax.all_to_all(normed, PLANE, 0, 0).reshape(1024, channels)  11.2 us
    all_to_all x1, waiting for transfers between devices, local(): parts = lax.all_to_all(parts, PLANE, 0, 0)  10.3 us
    ppermute x1, starting transfers between devices, local(): other_half = lax.ppermute(mine, 'core', swap)  8.37 us
    ppermute x1, starting transfers between devices, local(): other = lax.ppermute(send, 'core', swap)  4.45 us
    all_to_all x1, starting transfers between devices, local(): gathered = lax.all_to_all(normed, PLANE, 0, 0).reshape(1024, channels)  3.82 us
    all_to_all x1, starting transfers between devices, local(): parts = lax.all_to_all(parts, PLANE, 0, 0)  3.74 us
  transfers between devices with their start and end apart: 6, of which 5 were waited for; matrix products, arithmetic and copies ran while one was open for 1% of the time, Pallas kernels for 2%

profile of v2, /device:TPU:1, one launch (start us, length us, event | category | flops | bytes accessed | tf_op | source)
XLA Modules:
  0.0 107.0 jit_solution(13505836471205580619)
XLA Ops:
  0.0 0.1 pad_add_fusion.place_ref
  0.1 0.0 copy-start.1
  0.1 1.0 copy-done.1
  1.1 0.9 weight_slices.1
  2.0 29.3 %all_to_all.20 = bf16[16,24,384]{2,1,0:T(8,128)(2,1)S(1)} all-to-all(bf16[16,24,384]{2,1,0:T(8,128)(2,1)S(1)} %weight_slices.1), channel_id=1, replica_groups=mesh['tm'=16,'y'=4,'core'=2,'width'=4] {'tm'}, dimensions={0} | all-to-all | bytes 589824 | tf_op jit(solution)/shard_map/weight_slices/all_to_all | solution.py:172
  31.3 8.4 %collective-permute-start.1 = (bf16[384,384]{1,0:T(8,128)(2,1)S(1)}, bf16[384,384]{1,0:T(8,128)(2,1)S(1)}, u32[]{:S(2)}, u32[]{:S(2)}) collective-permute-start(bf16[384,384]{1,0:T(8,128)(2,1)S(1)} %bitcast.14), channel_id=1, source_target_pairs={{0,4},{4,0},{1,5},{5,1},{2,6},{6,2},{3,7},{7,3},{8,12},{12,8},{9,1... | collective-permute-start | bytes 884744 | tf_op jit(solution)/shard_map/weight_slices/ppermute | solution.py:173
  39.7 3.0 %collective-permute-start = (bf16[64,384]{1,0:T(8,128)(2,1)}, bf16[64,384]{1,0:T(8,128)(2,1)S(1)}, u32[]{:S(2)}, u32[]{:S(2)}) collective-permute-start(bf16[64,384]{1,0:T(8,128)(2,1)} %bitcast.19), channel_id=1, source_target_pairs={{0,32},{32,64},{64,96},{96,128},{128,160},{160,192},{192,224},{224... | collective-permute-start | bytes 147464 | tf_op jit(solution)/shard_map/earlier_frames/ppermute | solution.py:168
  42.7 0.7 reshape.37.gain_ref
  43.4 0.8 collective-permute-done.before_ref
  44.2 0.0 copy-start.3
  44.2 0.8 copy-done.3
  45.0 0.3 activated.2
  45.3 16.0 %all_to_all.21 = bf16[32,24,128]{2,1,0:T(8,128)(2,1)S(1)} all-to-all(bf16[32,24,128]{2,1,0:T(8,128)(2,1)S(1)} %bitcast.17), channel_id=1, replica_groups=mesh['tm'=16,'y'=4,'core'=2,'width'=4] {'y','core','width'}, dimensions={0} | all-to-all | bytes 393216 | tf_op jit(solution)/shard_map/activated/all_to_all | solution.py:179
  61.3 0.6 activated.3.patch_ref
  61.8 0.0 copy-start.4
  61.9 0.0 collective-permute-done.1.other_ref
  61.9 2.5 %conv.1 = bf16[16,64,384]{2,1,0:T(8,128)(2,1)} custom-call(s32[2]{0:T(128)S(1)} %pad_add_fusion.place_ref, bf16[2,384,1024]{2,1,0:T(8,128)(2,1)S(1)} %activated.3.patch_ref, bf16[384,384]{1,0:T(8,128)(2,1)S(1)} %bitcast.15, bf16[384,384]{1,0:T(8,128)(2,1)S(1)} %collective-permute-done.1.other_ref), custom_call_target="tpu_custom_call" | custom-call | flops 700000000 | bytes 1000000 | tf_op jit(solution)/shard_map/conv/pallas_call | solution.py:192
  64.4 0.0 copy-start.5
  64.4 3.7 %all-to-all-start.2 = ((bf16[16,64,384]{2,1,0:T(8,128)(2,1)}), bf16[16,64,384]{2,1,0:T(8,128)(2,1)S(1)}, u32[]{:S(2)}, u32[]{:S(2)}) async-start(bf16[16,64,384]{2,1,0:T(8,128)(2,1)} %conv.1), calls=%async_computation.2 | async-start | bytes 1572864 | tf_op jit(solution)/shard_map/conv/all_to_all | solution.py:195
  68.2 0.0 copy-start
  68.2 0.0 copy-done.4
  68.2 2.4 %collective-permute-start.2 = (bf16[32,384]{1,0:T(8,128)(2,1)S(1)}, bf16[32,384]{1,0:T(8,128)(2,1)S(1)}, u32[]{:S(2)}, u32[]{:S(2)}) collective-permute-start(bf16[32,384]{1,0:T(8,128)(2,1)S(1)} %bitcast.22), channel_id=1, source_target_pairs={{0,4},{4,0},{1,5},{5,1},{2,6},{6,2},{3,7},{7,3},{8,12},{12,8},{9,1... | collective-permute-start | bytes 73736 | tf_op jit(solution)/shard_map/own_latent/ppermute | solution.py:189
  70.7 0.0 copy-done.5
  70.7 0.8 collective-permute-done.2
  71.5 10.3 %all-to-all-done.2.part_ref = bf16[16,64,384]{2,1,0:T(8,128)(2,1)S(1)} async-done(((bf16[16,64,384]{2,1,0:T(8,128)(2,1)}), bf16[16,64,384]{2,1,0:T(8,128)(2,1)S(1)}, u32[]{:S(2)}, u32[]{:S(2)}) %all-to-all-start.2) | async-done | bytes 786464 | tf_op jit(solution)/shard_map/conv/all_to_all | solution.py:195
  81.8 1.1 %hidden.1 = (bf16[64,384]{1,0:T(8,128)(2,1)S(1)}, bf16[16,64,384]{2,1,0:T(8,128)(2,1)}) custom-call(bf16[16,64,384]{2,1,0:T(8,128)(2,1)S(1)} %all-to-all-done.2.part_ref, bf16[64,384]{1,0:T(8,128)(2,1)S(1)} %maximum_select_fusion.latent_ref, f32[1,384]{1,0:T(1,128)S(1)} %reshape.41.gain_ref), custom_call_target="tpu_custom_call" | custom-call | flops 1000000 | bytes 1000000 | tf_op jit(solution)/shard_map/hidden/pallas_call | solution.py:197
  83.0 0.0 copy-start.2
  83.0 3.8 %all-to-all-start.3 = ((bf16[16,64,384]{2,1,0:T(8,128)(2,1)}), bf16[16,64,384]{2,1,0:T(8,128)(2,1)S(1)}, u32[]{:S(2)}, u32[]{:S(2)}) async-start(bf16[16,64,384]{2,1,0:T(8,128)(2,1)} %get-tuple-element.11.normed_ref), calls=%async_computation.3 | async-start | bytes 1572864 | tf_op jit(solution)/shard_map/keys/all_to_all | solution.py:201
  86.8 0.0 copy-done
  86.8 1.5 %query.1.query_ref = bf16[64,384]{1,0:T(8,128)(2,1)S(1)} custom-call(bf16[16,64,384]{2,1,0:T(8,128)(2,1)} %get-tuple-element.11.normed_ref, bf16[384,1152]{1,0:T(8,128)(2,1)S(1)} %copy-done), custom_call_target="tpu_custom_call" | custom-call | flops 40000000 | bytes 1000000 | tf_op jit(solution)/shard_map/query/pallas_call | solution.py:203
  88.3 11.2 %all-to-all-done.3 = bf16[16,64,384]{2,1,0:T(8,128)(2,1)S(1)} async-done(((bf16[16,64,384]{2,1,0:T(8,128)(2,1)}), bf16[16,64,384]{2,1,0:T(8,128)(2,1)S(1)}, u32[]{:S(2)}, u32[]{:S(2)}) %all-to-all-start.3) | async-done | bytes 786464 | tf_op jit(solution)/shard_map/keys/all_to_all | solution.py:201
  99.6 0.0 copy-done.2
  99.6 1.5 %attention.1 = (bf16[32,384]{1,0:T(8,128)(2,1)S(1)}, bf16[32,384]{1,0:T(8,128)(2,1)S(1)}) custom-call(s32[2]{0:T(128)S(1)} %pad_add_fusion.place_ref, bf16[64,384]{1,0:T(8,128)(2,1)S(1)} %query.1.query_ref, bf16[1024,384]{1,0:T(8,128)(2,1)S(1)} %bitcast.13, bf16[64,384]{1,0:T(8,128)(2,1)S(1)} %get-tuple-element.12.hidden_ref, bf16[384,1152]{1,0:T(8,128)(2,1)S(1)} %copy-done, ...), custom_call_target="tpu_custom_call" | custom-call | flops 200000000 | bytes 1000000 | tf_op jit(solution)/shard_map/attention/pallas_call | solution.py:206
  101.1 4.4 %collective-permute-start.3 = (bf16[32,384]{1,0:T(8,128)(2,1)S(1)}, bf16[32,384]{1,0:T(8,128)(2,1)S(1)}, u32[]{:S(2)}, u32[]{:S(2)}) collective-permute-start(bf16[32,384]{1,0:T(8,128)(2,1)S(1)} %get-tuple-element.14), channel_id=1, source_target_pairs={{0,4},{4,0},{1,5},{5,1},{2,6},{6,2},{3,7},{7,3},{8,12},{12,8},{9,1... | collective-permute-start | bytes 73736 | tf_op jit(solution)/shard_map/attention/ppermute | solution.py:209
  105.5 0.8 collective-permute-done.3
  106.4 0.6 maximum_select_fusion.1
  (3 shorter events, 0.0 us)
Async XLA Ops:
  0.1 1.0 copy-start.1
  31.3 30.6 %collective-permute-start.1 = (bf16[384,384]{1,0:T(8,128)(2,1)S(1)}, bf16[384,384]{1,0:T(8,128)(2,1)S(1)}, u32[]{:S(2)}, u32[]{:S(2)}) collective-permute-start(bf16[384,384]{1,0:T(8,128)(2,1)S(1)} %bitcast.14), channel_id=1, source_target_pairs={{0,4},{4,0},{1,5},{5,1},{2,6},{6,2},{3,7},{7,3},{8,12},{12,8},{9,1... | collective-permute-start | bytes 884744 | tf_op jit(solution)/shard_map/weight_slices/ppermute | solution.py:173
  39.7 4.5 %collective-permute-start = (bf16[64,384]{1,0:T(8,128)(2,1)}, bf16[64,384]{1,0:T(8,128)(2,1)S(1)}, u32[]{:S(2)}, u32[]{:S(2)}) collective-permute-start(bf16[64,384]{1,0:T(8,128)(2,1)} %bitcast.19), channel_id=1, source_target_pairs={{0,32},{32,64},{64,96},{96,128},{128,160},{160,192},{192,224},{224... | collective-permute-start | bytes 147464 | tf_op jit(solution)/shard_map/earlier_frames/ppermute | solution.py:168
  44.2 0.8 copy-start.3
  61.8 6.3 %copy-start.4 = (bf16[2,2,16,384]{3,2,1,0:T(8,128)(2,1)S(1)}, bf16[2,2,16,384]{3,2,1,0:T(8,128)(2,1)}, u32[]{:S(2)}) copy-start(bf16[2,2,16,384]{3,2,1,0:T(8,128)(2,1)} %param.6) | copy-start | bytes 147460
  64.4 6.3 %copy-start.5 = (f32[384]{0:T(512)S(1)}, f32[384]{0:T(512)}, u32[]{:S(2)}) copy-start(f32[384]{0:T(512)} %param.9) | copy-start | bytes 4612
  64.4 17.4 %all-to-all-start.2 = ((bf16[16,64,384]{2,1,0:T(8,128)(2,1)}), bf16[16,64,384]{2,1,0:T(8,128)(2,1)S(1)}, u32[]{:S(2)}, u32[]{:S(2)}) async-start(bf16[16,64,384]{2,1,0:T(8,128)(2,1)} %conv.1), calls=%async_computation.2 | async-start | bytes 1572864 | tf_op jit(solution)/shard_map/conv/all_to_all | solution.py:195
  68.2 18.6 %copy-start = (bf16[384,1152]{1,0:T(8,128)(2,1)S(1)}, bf16[384,1152]{1,0:T(8,128)(2,1)}, u32[]{:S(2)}) copy-start(bf16[384,1152]{1,0:T(8,128)(2,1)} %w_ref.3) | copy-start | bytes 2654212
  68.2 3.3 %collective-permute-start.2 = (bf16[32,384]{1,0:T(8,128)(2,1)S(1)}, bf16[32,384]{1,0:T(8,128)(2,1)S(1)}, u32[]{:S(2)}, u32[]{:S(2)}) collective-permute-start(bf16[32,384]{1,0:T(8,128)(2,1)S(1)} %bitcast.22), channel_id=1, source_target_pairs={{0,4},{4,0},{1,5},{5,1},{2,6},{6,2},{3,7},{7,3},{8,12},{12,8},{9,1... | collective-permute-start | bytes 73736 | tf_op jit(solution)/shard_map/own_latent/ppermute | solution.py:189
  83.0 16.6 %copy-start.2 = (bf16[384,384]{1,0:T(8,128)(2,1)S(1)}, bf16[384,384]{1,0:T(8,128)(2,1)}, u32[]{:S(2)}) copy-start(bf16[384,384]{1,0:T(8,128)(2,1)} %w_out_ref.1) | copy-start | bytes 884740
  83.0 16.6 %all-to-all-start.3 = ((bf16[16,64,384]{2,1,0:T(8,128)(2,1)}), bf16[16,64,384]{2,1,0:T(8,128)(2,1)S(1)}, u32[]{:S(2)}, u32[]{:S(2)}) async-start(bf16[16,64,384]{2,1,0:T(8,128)(2,1)} %get-tuple-element.11.normed_ref), calls=%async_computation.3 | async-start | bytes 1572864 | tf_op jit(solution)/shard_map/keys/all_to_all | solution.py:201
  101.1 5.3 %collective-permute-start.3 = (bf16[32,384]{1,0:T(8,128)(2,1)S(1)}, bf16[32,384]{1,0:T(8,128)(2,1)S(1)}, u32[]{:S(2)}, u32[]{:S(2)}) collective-permute-start(bf16[32,384]{1,0:T(8,128)(2,1)S(1)} %get-tuple-element.14), channel_id=1, source_target_pairs={{0,4},{4,0},{1,5},{5,1},{2,6},{6,2},{3,7},{7,3},{8,12},{12,8},{9,1... | collective-permute-start | bytes 73736 | tf_op jit(solution)/shard_map/attention/ppermute | solution.py:209

commit v3 on v2

--- a/solution.py
+++ b/solution.py
@@ -11,8 +11,7 @@
 BF16 = jnp.bfloat16
 TAPS = 27
 GROUP = 24
-HALF = 14
-DEPTH = 384
+DEPTH = 768
 PLANE = ("y", "width")
 VMEM = pl.BlockSpec(memory_space=pltpu.VMEM)
 SMEM = pl.BlockSpec(memory_space=pltpu.SMEM)
@@ -39,18 +38,15 @@
 
 def weight_body(place_ref, weight_ref, out_ref):
     start = place_ref[0] * GROUP
-    first_tap = place_ref[1] * HALF
     source = lax.broadcasted_iota(jnp.int32, (384, 128), 0)
     target = lax.broadcasted_iota(jnp.int32, (384, 128), 1)
     pick = ((target < GROUP) & (source == start + target)).astype(F32).astype(BF16)
-    rows = [weight_ref[jnp.minimum(first_tap + tap, TAPS - 1)] for tap in range(HALF)]
+    rows = [weight_ref[tap] for tap in range(TAPS)]
     picked = jnp.dot(jnp.concatenate(rows, axis=0), pick, preferred_element_type=F32)
     lane = lax.broadcasted_iota(jnp.int32, (GROUP, 128), 1)
-    tiles = [jnp.zeros((GROUP, 128), F32) for _ in range(3)]
-    for tap in range(HALF):
+    tiles = [jnp.zeros((GROUP, 128), F32) for _ in range(DEPTH // 128)]
+    for tap in range(TAPS):
         value = picked[tap * GROUP : tap * GROUP + GROUP]
-        if tap == HALF - 1:
-            value = jnp.where(first_tap + tap < TAPS, value, 0.0)
         tile, offset = divmod(tap * GROUP, 128)
         value = pltpu.roll(value, offset, 1) if offset else value
         if offset + GROUP > 128:
@@ -58,9 +54,7 @@
             tiles[tile + 1] += jnp.where(lane < offset, value, 0.0)
         else:
             tiles[tile] += value
-    whole = jnp.concatenate(tiles, axis=1).astype(BF16)
-    for plane in range(16):
-        out_ref[plane] = whole
+    out_ref[...] = jnp.concatenate(tiles, axis=1).astype(BF16)
 
 
 def activate_body(before_ref, now_ref, gain_ref, out_ref):
@@ -98,22 +92,19 @@
             up = jnp.where(lane < 64, above, swapped)
             down = jnp.where(lane < 64, swapped, below)
             for row_tap, value in enumerate((up, base, down)):
-                half, tap = divmod((time_tap * 3 + row_tap) * 3 + col_tap, HALF)
+                tap = (time_tap * 3 + row_tap) * 3 + col_tap
                 for height in range(8):
                     held_ref[
-                        half, tap * GROUP : tap * GROUP + GROUP, height * 128 : height * 128 + 128
+                        tap * GROUP : tap * GROUP + GROUP, height * 128 : height * 128 + 128
                     ] = value[height * GROUP : height * GROUP + GROUP]
-    held_ref[0, HALF * GROUP :, :] = jnp.zeros((DEPTH - HALF * GROUP, 1024), F32)
-    held_ref[1, (TAPS - HALF) * GROUP :, :] = jnp.zeros((DEPTH - (TAPS - HALF) * GROUP, 1024), F32)
+    held_ref[TAPS * GROUP :, :] = jnp.zeros((DEPTH - TAPS * GROUP, 1024), F32)
     out_ref[...] = held_ref[...].astype(BF16)
 
 
-def conv_body(place_ref, patch_ref, mine_ref, other_ref, out_ref):
-    core = place_ref[1]
+def conv_body(patch_ref, weight_ref, out_ref):
     for part in range(4):
         cut = slice(part * 256, part * 256 + 256)
-        turned = jnp.dot(mine_ref[...], patch_ref[core, :, cut], preferred_element_type=F32)
-        turned += jnp.dot(other_ref[...], patch_ref[1 - core, :, cut], preferred_element_type=F32)
+        turned = jnp.dot(weight_ref[...], patch_ref[:, cut], preferred_element_type=F32)
         summed = turned.T.astype(BF16)
         for row in range(4):
             for width in range(4):
@@ -168,20 +159,19 @@
         before = lax.ppermute(cells, "tm", [(i, i + 1) for i in range(15)])
     with jax.named_scope("weight_slices"):
         turned = jnp.transpose(conv_weight.reshape(TAPS, channels, GROUP), (0, 2, 1))
-        pieces = call(weight_body, shape((16, GROUP, DEPTH), BF16), [SMEM, VMEM])(place, turned)
-        mine = lax.all_to_all(pieces, "tm", 0, 0).reshape(channels, DEPTH)
-        other_half = lax.ppermute(mine, "core", swap)
+        piece = call(weight_body, shape((GROUP, DEPTH), BF16), [SMEM, VMEM])(place, turned)
     with jax.named_scope("activated"):
-        before, pieces = lax.optimization_barrier((before, pieces))
         blocks = call(activate_body, shape((4, 2, 4, GROUP, 128), BF16), [VMEM] * 3)(
             before, cells, norm_gain.reshape(1, channels)
         )
+        piece, blocks = lax.optimization_barrier((piece, blocks))
+        weight = lax.all_gather(piece, "tm", axis=0, tiled=True)
         blocks = lax.all_to_all(blocks.reshape(32, GROUP, 128), ("y", "core", "width"), 0, 0)
         patches = call(
             patch_body,
-            shape((2, DEPTH, 1024), BF16),
+            shape((DEPTH, 1024), BF16),
             [VMEM],
-            scratch=[pltpu.VMEM((2, DEPTH, 1024), F32)],
+            scratch=[pltpu.VMEM((DEPTH, 1024), F32)],
         )(blocks.reshape(8, 4, GROUP, 128))
     with jax.named_scope("own_latent"):
         first = core == 0
@@ -189,9 +179,7 @@
         other = lax.ppermute(jnp.where(first, cells[32:], cells[:32]), "core", swap)
         own = jnp.where(first, jnp.concatenate([kept, other]), jnp.concatenate([other, kept]))
     with jax.named_scope("conv"):
-        parts = call(conv_body, shape((16, 64, channels), BF16), [SMEM] + [VMEM] * 3, 700_000_000)(
-            place, patches, mine, other_half
-        )
+        parts = call(conv_body, shape((16, 64, channels), BF16), [VMEM] * 2, 700_000_000)(patches, weight)
         parts = lax.all_to_all(parts, PLANE, 0, 0)
     with jax.named_scope("hidden"):
         hidden, normed = call(

time: 108 us -> 98.5 us (0.912)
  starting transfers between devices: 25.9 us -> 43.7 us
  blocking collectives: 45.3 us -> 31.3 us
  waiting for transfers between devices: 24 us -> 11 us
    all_to_all x2 -> x0, blocking collectives: 45.3 us -> none  [the longest x1 29.3 us: local(): mine = lax.all_to_all(pieces, 'tm', 0, 0).reshape(channels, DEPTH)]
    all_gather x0 -> x1, blocking collectives: none -> 31.3 us  [local(): weight = lax.all_gather(piece, 'tm', axis=0, tiled=True)]
    all_to_all x1, waiting for transfers between devices: 10.3 us -> 0.33 us  [local(): parts = lax.all_to_all(parts, PLANE, 0, 0)]
    ppermute x1 -> x0, starting transfers between devices: 8.37 us -> none  [local(): other_half = lax.ppermute(mine, 'core', swap)]
    all_to_all x0 -> x1, starting transfers between devices: none -> 8.04 us  [local(): lax.all_to_all(blocks.reshape(32, GROUP, 128), ('y', 'core', 'width'), 0, 0)]
    ppermute x1, starting transfers between devices: 2.45 us -> 9.21 us  [local(): other = lax.ppermute(jnp.where(first, cells[32:], cells[:32]), 'core', swap)]
    ppermute x1, starting transfers between devices: 4.45 us -> 8.26 us  [local(): other = lax.ppermute(send, 'core', swap)]
    all_to_all x1, starting transfers between devices: 3.74 us -> 7.11 us  [local(): parts = lax.all_to_all(parts, PLANE, 0, 0)]
  transfers between devices with their start and end apart: 6 -> 6, of which waited for: 5 -> 4; matrix products, arithmetic and copies ran while one was open for 1% -> 1% of each run, Pallas kernels for 2% -> 2%
where the time goes in v3:
time: 98.5 us; the launch traced here: 97.8 us
  starting transfers between devices  43.7 us (44%)
  blocking collectives  31.3 us (32%)
  waiting for transfers between devices  11 us (11%)
  Pallas kernels  8.38 us (9%)
  local copies, waits for them, and re-layouts  2.53 us (3%)
    all_gather x1, blocking collectives, local(): weight = lax.all_gather(piece, 'tm', axis=0, tiled=True)  31.3 us
    ppermute x1, starting transfers between devices, local(): other = lax.ppermute(jnp.where(first, cells[32:], cells[:32]), 'core', swap)  9.21 us
    all_to_all x1, waiting for transfers between devices, local(): gathered = lax.all_to_all(normed, PLANE, 0, 0).reshape(1024, channels)  9 us
    ppermute x1, starting transfers between devices, local(): other = lax.ppermute(send, 'core', swap)  8.26 us
    all_to_all x1, starting transfers between devices, local(): lax.all_to_all(blocks.reshape(32, GROUP, 128), ('y', 'core', 'width'), 0, 0)  8.04 us
    all_to_all x1, starting transfers between devices, local(): parts = lax.all_to_all(parts, PLANE, 0, 0)  7.11 us
    all_to_all x1, starting transfers between devices, local(): gathered = lax.all_to_all(normed, PLANE, 0, 0).reshape(1024, channels)  6.75 us
    ppermute x1, starting transfers between devices, local(): before = lax.ppermute(cells, 'tm', [(i, i + 1) for i in range(15)])  4.36 us
  transfers between devices with their start and end apart: 6, of which 4 were waited for; matrix products, arithmetic and copies ran while one was open for 1% of the time, Pallas kernels for 2%

profile of v3, /device:TPU:1, one launch (start us, length us, event | category | flops | bytes accessed | tf_op | source)
XLA Modules:
  0.0 97.8 jit_solution(17057955645569073962)
XLA Ops:
  0.0 4.4 %collective-permute-start = (bf16[64,384]{1,0:T(8,128)(2,1)}, bf16[64,384]{1,0:T(8,128)(2,1)S(1)}, u32[]{:S(2)}, u32[]{:S(2)}) collective-permute-start(bf16[64,384]{1,0:T(8,128)(2,1)} %bitcast.15), channel_id=1, source_target_pairs={{0,32},{32,64},{64,96},{96,128},{128,160},{160,192},{192,224},{224... | collective-permute-start | bytes 147464 | tf_op jit(solution)/shard_map/earlier_frames/ppermute | solution.py:159
  4.4 0.1 pad_add_fusion.place_ref
  4.5 0.7 reshape.34.gain_ref
  5.1 0.0 copy-start.1
  5.1 1.0 %copy-done.1 = bf16[3,3,3,384,24]{3,4,2,1,0:T(8,128)(2,1)S(1)} copy-done((bf16[3,3,3,384,24]{3,4,2,1,0:T(8,128)(2,1)S(1)}, bf16[3,3,3,384,24]{3,4,2,1,0:T(8,128)(2,1)}, u32[]{:S(2)}) %copy-start.1) | copy-done | bytes 497688
  6.2 0.9 weight_slices.1
  7.1 0.0 collective-permute-done.before_ref
  7.1 0.0 copy-start.3
  7.1 0.8 copy-done.3
  7.9 1.0 activated.2
  8.9 8.0 %all-to-all-start = ((bf16[32,24,128]{2,1,0:T(8,128)(2,1)}), bf16[32,24,128]{2,1,0:T(8,128)(2,1)S(1)}, u32[]{:S(2)}, u32[]{:S(2)}) async-start(bf16[32,24,128]{2,1,0:T(8,128)(2,1)} %bitcast.5), calls=%async_computation | async-start | bytes 393216 | tf_op jit(solution)/shard_map/activated/all_to_all | solution.py:169
  16.9 31.3 %all_gather.3.weight_ref = bf16[384,768]{1,0:T(8,128)(2,1)S(1)} all-gather(bf16[24,768]{1,0:T(8,128)(2,1)S(1)} %weight_slices.1), channel_id=1, replica_groups=mesh['tm'=16,'y'=4,'core'=2,'width'=4] {'tm'}, dimensions={0}, use_global_device_ids=true | all-gather | bytes 626688 | tf_op jit(solution)/shard_map/activated/all_gather | solution.py:168
  48.3 0.0 all-to-all-done
  48.3 0.5 activated.3.patch_ref
  48.8 0.0 copy-start.4
  48.8 1.8 %conv.1 = bf16[16,64,384]{2,1,0:T(8,128)(2,1)} custom-call(bf16[768,1024]{1,0:T(8,128)(2,1)S(1)} %activated.3.patch_ref, bf16[384,768]{1,0:T(8,128)(2,1)S(1)} %all_gather.3.weight_ref), custom_call_target="tpu_custom_call" | custom-call | flops 700000000 | bytes 1000000 | tf_op jit(solution)/shard_map/conv/pallas_call | solution.py:182
  50.6 0.0 copy-start.5
  50.6 7.1 %all-to-all-start.1 = ((bf16[16,64,384]{2,1,0:T(8,128)(2,1)}), bf16[16,64,384]{2,1,0:T(8,128)(2,1)S(1)}, u32[]{:S(2)}, u32[]{:S(2)}) async-start(bf16[16,64,384]{2,1,0:T(8,128)(2,1)} %conv.1), calls=%async_computation.1 | async-start | bytes 1572864 | tf_op jit(solution)/shard_map/conv/all_to_all | solution.py:183
  57.8 0.0 copy-start
  57.8 0.0 copy-done.4
  57.8 9.2 %collective-permute-start.1 = (bf16[32,384]{1,0:T(8,128)(2,1)S(1)}, bf16[32,384]{1,0:T(8,128)(2,1)S(1)}, u32[]{:S(2)}, u32[]{:S(2)}) collective-permute-start(bf16[32,384]{1,0:T(8,128)(2,1)S(1)} %bitcast.18), channel_id=1, source_target_pairs={{0,4},{4,0},{1,5},{5,1},{2,6},{6,2},{3,7},{7,3},{8,12},{12,8},{9,1... | collective-permute-start | bytes 73736 | tf_op jit(solution)/shard_map/own_latent/ppermute | solution.py:179
  67.0 0.0 copy-done.5
  67.0 0.8 collective-permute-done.1
  67.9 0.3 all-to-all-done.1.part_ref
  68.2 1.1 %hidden.1 = (bf16[64,384]{1,0:T(8,128)(2,1)S(1)}, bf16[16,64,384]{2,1,0:T(8,128)(2,1)}) custom-call(bf16[16,64,384]{2,1,0:T(8,128)(2,1)S(1)} %all-to-all-done.1.part_ref, bf16[64,384]{1,0:T(8,128)(2,1)S(1)} %maximum_select_fusion.latent_ref, f32[1,384]{1,0:T(1,128)S(1)} %reshape.37.gain_ref), custom_call_target="tpu_custom_call" | custom-call | flops 1000000 | bytes 1000000 | tf_op jit(solution)/shard_map/hidden/pallas_call | solution.py:185
  69.3 0.0 copy-start.2
  69.3 6.7 %all-to-all-start.2 = ((bf16[16,64,384]{2,1,0:T(8,128)(2,1)}), bf16[16,64,384]{2,1,0:T(8,128)(2,1)S(1)}, u32[]{:S(2)}, u32[]{:S(2)}) async-start(bf16[16,64,384]{2,1,0:T(8,128)(2,1)} %get-tuple-element.13.normed_ref), calls=%async_computation.2 | async-start | bytes 1572864 | tf_op jit(solution)/shard_map/keys/all_to_all | solution.py:189
  76.1 0.0 copy-done
  76.1 1.5 %query.1.query_ref = bf16[64,384]{1,0:T(8,128)(2,1)S(1)} custom-call(bf16[16,64,384]{2,1,0:T(8,128)(2,1)} %get-tuple-element.13.normed_ref, bf16[384,1152]{1,0:T(8,128)(2,1)S(1)} %copy-done), custom_call_target="tpu_custom_call" | custom-call | flops 40000000 | bytes 1000000 | tf_op jit(solution)/shard_map/query/pallas_call | solution.py:191
  77.6 9.0 %all-to-all-done.2 = bf16[16,64,384]{2,1,0:T(8,128)(2,1)S(1)} async-done(((bf16[16,64,384]{2,1,0:T(8,128)(2,1)}), bf16[16,64,384]{2,1,0:T(8,128)(2,1)S(1)}, u32[]{:S(2)}, u32[]{:S(2)}) %all-to-all-start.2) | async-done | bytes 786464 | tf_op jit(solution)/shard_map/keys/all_to_all | solution.py:189
  86.6 0.0 copy-done.2
  86.6 1.5 %attention.1 = (bf16[32,384]{1,0:T(8,128)(2,1)S(1)}, bf16[32,384]{1,0:T(8,128)(2,1)S(1)}) custom-call(s32[2]{0:T(128)S(1)} %pad_add_fusion.place_ref, bf16[64,384]{1,0:T(8,128)(2,1)S(1)} %query.1.query_ref, bf16[1024,384]{1,0:T(8,128)(2,1)S(1)} %bitcast.12, bf16[64,384]{1,0:T(8,128)(2,1)S(1)} %get-tuple-element.14.hidden_ref, bf16[384,1152]{1,0:T(8,128)(2,1)S(1)} %copy-done, ...), custom_call_target="tpu_custom_call" | custom-call | flops 200000000 | bytes 1000000 | tf_op jit(solution)/shard_map/attention/pallas_call | solution.py:194
  88.1 8.3 %collective-permute-start.2 = (bf16[32,384]{1,0:T(8,128)(2,1)S(1)}, bf16[32,384]{1,0:T(8,128)(2,1)S(1)}, u32[]{:S(2)}, u32[]{:S(2)}) collective-permute-start(bf16[32,384]{1,0:T(8,128)(2,1)S(1)} %get-tuple-element.16), channel_id=1, source_target_pairs={{0,4},{4,0},{1,5},{5,1},{2,6},{6,2},{3,7},{7,3},{8,12},{12,8},{9,1... | collective-permute-start | bytes 73736 | tf_op jit(solution)/shard_map/attention/ppermute | solution.py:197
  96.4 0.8 collective-permute-done.2
  97.2 0.6 maximum_select_fusion.1
  (3 shorter events, 0.0 us)
Async XLA Ops:
  0.0 7.1 %collective-permute-start = (bf16[64,384]{1,0:T(8,128)(2,1)}, bf16[64,384]{1,0:T(8,128)(2,1)S(1)}, u32[]{:S(2)}, u32[]{:S(2)}) collective-permute-start(bf16[64,384]{1,0:T(8,128)(2,1)} %bitcast.15), channel_id=1, source_target_pairs={{0,32},{32,64},{64,96},{96,128},{128,160},{160,192},{192,224},{224... | collective-permute-start | bytes 147464 | tf_op jit(solution)/shard_map/earlier_frames/ppermute | solution.py:159
  5.1 1.0 %copy-start.1 = (bf16[3,3,3,384,24]{3,4,2,1,0:T(8,128)(2,1)S(1)}, bf16[3,3,3,384,24]{3,4,2,1,0:T(8,128)(2,1)}, u32[]{:S(2)}) copy-start(bf16[3,3,3,384,24]{3,4,2,1,0:T(8,128)(2,1)} %param.8) | copy-start | bytes 1492996
  7.1 0.8 copy-start.3
  8.9 39.4 %all-to-all-start = ((bf16[32,24,128]{2,1,0:T(8,128)(2,1)}), bf16[32,24,128]{2,1,0:T(8,128)(2,1)S(1)}, u32[]{:S(2)}, u32[]{:S(2)}) async-start(bf16[32,24,128]{2,1,0:T(8,128)(2,1)} %bitcast.5), calls=%async_computation | async-start | bytes 393216 | tf_op jit(solution)/shard_map/activated/all_to_all | solution.py:169
  48.8 8.9 %copy-start.4 = (bf16[2,2,16,384]{3,2,1,0:T(8,128)(2,1)S(1)}, bf16[2,2,16,384]{3,2,1,0:T(8,128)(2,1)}, u32[]{:S(2)}) copy-start(bf16[2,2,16,384]{3,2,1,0:T(8,128)(2,1)} %param.6) | copy-start | bytes 147460
  50.6 16.4 %copy-start.5 = (f32[384]{0:T(512)S(1)}, f32[384]{0:T(512)}, u32[]{:S(2)}) copy-start(f32[384]{0:T(512)} %param.9) | copy-start | bytes 4612
  50.6 17.6 %all-to-all-start.1 = ((bf16[16,64,384]{2,1,0:T(8,128)(2,1)}), bf16[16,64,384]{2,1,0:T(8,128)(2,1)S(1)}, u32[]{:S(2)}, u32[]{:S(2)}) async-start(bf16[16,64,384]{2,1,0:T(8,128)(2,1)} %conv.1), calls=%async_computation.1 | async-start | bytes 1572864 | tf_op jit(solution)/shard_map/conv/all_to_all | solution.py:183
  57.8 18.3 %copy-start = (bf16[384,1152]{1,0:T(8,128)(2,1)S(1)}, bf16[384,1152]{1,0:T(8,128)(2,1)}, u32[]{:S(2)}) copy-start(bf16[384,1152]{1,0:T(8,128)(2,1)} %w_ref.3) | copy-start | bytes 2654212
  57.8 10.0 %collective-permute-start.1 = (bf16[32,384]{1,0:T(8,128)(2,1)S(1)}, bf16[32,384]{1,0:T(8,128)(2,1)S(1)}, u32[]{:S(2)}, u32[]{:S(2)}) collective-permute-start(bf16[32,384]{1,0:T(8,128)(2,1)S(1)} %bitcast.18), channel_id=1, source_target_pairs={{0,4},{4,0},{1,5},{5,1},{2,6},{6,2},{3,7},{7,3},{8,12},{12,8},{9,1... | collective-permute-start | bytes 73736 | tf_op jit(solution)/shard_map/own_latent/ppermute | solution.py:179
  69.3 17.3 %copy-start.2 = (bf16[384,384]{1,0:T(8,128)(2,1)S(1)}, bf16[384,384]{1,0:T(8,128)(2,1)}, u32[]{:S(2)}) copy-start(bf16[384,384]{1,0:T(8,128)(2,1)} %w_out_ref.1) | copy-start | bytes 884740
  69.3 17.3 %all-to-all-start.2 = ((bf16[16,64,384]{2,1,0:T(8,128)(2,1)}), bf16[16,64,384]{2,1,0:T(8,128)(2,1)S(1)}, u32[]{:S(2)}, u32[]{:S(2)}) async-start(bf16[16,64,384]{2,1,0:T(8,128)(2,1)} %get-tuple-element.13.normed_ref), calls=%async_computation.2 | async-start | bytes 1572864 | tf_op jit(solution)/shard_map/keys/all_to_all | solution.py:189
  88.1 9.1 %collective-permute-start.2 = (bf16[32,384]{1,0:T(8,128)(2,1)S(1)}, bf16[32,384]{1,0:T(8,128)(2,1)S(1)}, u32[]{:S(2)}, u32[]{:S(2)}) collective-permute-start(bf16[32,384]{1,0:T(8,128)(2,1)S(1)} %get-tuple-element.16), channel_id=1, source_target_pairs={{0,4},{4,0},{1,5},{5,1},{2,6},{6,2},{3,7},{7,3},{8,12},{12,8},{9,1... | collective-permute-start | bytes 73736 | tf_op jit(solution)/shard_map/attention/ppermute | solution.py:197

commit v4 on v3

v4 whole, which is shorter than its diff:
```python
import functools

import jax
import jax.numpy as jnp
from jax import lax
from jax.experimental import pallas as pl
from jax.experimental.pallas import tpu as pltpu
from jax.sharding import Mesh, PartitionSpec as P

F32 = jnp.float32
BF16 = jnp.bfloat16
TAPS = 27
GROUP = 24
SLOT = 96
DEPTH = 2688
PLANE = ("y", "width")
VMEM = pl.BlockSpec(memory_space=pltpu.VMEM)
SMEM = pl.BlockSpec(memory_space=pltpu.SMEM)
LIMIT = 32 * 1024 * 1024


def call(body, out, specs, flops=1_000_000, moved=1_000_000, scratch=()):
    many = isinstance(out, (tuple, list))
    return pl.pallas_call(
        body,
        out_shape=out,
        in_specs=specs,
        out_specs=[VMEM] * len(out) if many else VMEM,
        scratch_shapes=list(scratch),
        compiler_params=pltpu.CompilerParams(vmem_limit_bytes=LIMIT),
        cost_estimate=pl.CostEstimate(flops=flops, bytes_accessed=moved, transcendentals=0),
    )


def one_hot(shape, match):
    row = lax.broadcasted_iota(jnp.int32, shape, 0)
    col = lax.broadcasted_iota(jnp.int32, shape, 1)
    return match(row, col).astype(F32).astype(BF16)


def channel_of(place):
    return place % SLOT // 6 * GROUP + place // SLOT * 6 + place % 6


def weight_body(place_ref, weight_ref, out_ref):
    start = place_ref[3] * SLOT
    pick = one_hot((384, 128), lambda source, target: (target < SLOT) & (source == start + target))
    rows = jnp.concatenate([weight_ref[tap] for tap in range(TAPS)], axis=0)
    picked = jnp.dot(rows, pick, preferred_element_type=F32)
    upper = place_ref[1] // 2
    picked = jnp.where(upper == 0, picked, pltpu.roll(picked, TAPS * GROUP - 12, 0))
    picked = jnp.where(place_ref[1] % 2 == 0, picked, pltpu.roll(picked, TAPS * GROUP - 6, 0))
    lane = lax.broadcasted_iota(jnp.int32, (8, 128), 1)
    kept = lax.broadcasted_iota(jnp.int32, (8, 128), 0) < 6
    tiles = [jnp.zeros((8, 128), F32) for _ in range(DEPTH // 128)]
    for tap in range(TAPS):
        value = jnp.where(kept, picked[tap * GROUP : tap * GROUP + 8], 0.0)
        tile, offset = divmod(tap * SLOT, 128)
        value = pltpu.roll(value, offset, 1) if offset else value
        if offset + SLOT > 128:
            tiles[tile] += jnp.where(lane >= offset, value, 0.0)
            tiles[tile + 1] += jnp.where(lane < offset, value, 0.0)
        else:
            tiles[tile] += value
    out_ref[...] = jnp.concatenate(tiles, axis=1).astype(BF16)


def activate_body(before_ref, now_ref, gain_ref, out_ref):
    gain = gain_ref[...]
    halves = []
    for ref in (before_ref, now_ref):
        scaled = rms_scale(ref[...].astype(F32), gain)
        halves.append(scaled / (1.0 + jnp.exp(-scaled)))
    turned = jnp.concatenate(halves, axis=0).T
    later = pltpu.roll(turned, 96, 1)
    now = now_ref[...]
    order = one_hot((384, 384), lambda place, source: source == channel_of(place))
    latent = lax.dot_general(
        order, jnp.concatenate([now, now], axis=0), (((1,), (1,)), ((), ())), preferred_element_type=F32
    )
    lane = lax.broadcasted_iota(jnp.int32, (GROUP, 128), 1)
    for row in range(4):
        for core in range(2):
            packed = jnp.zeros((GROUP, 128), F32)
            for member in range(4):
                part = latent[row * SLOT + member * GROUP : row * SLOT + member * GROUP + GROUP]
                shift = (32 * member - 32 * core) % 128
                part = pltpu.roll(part, shift, 1) if shift else part
                packed += jnp.where((lane >= 32 * member) & (lane < 32 * member + 32), part, 0.0)
            packed = packed.astype(BF16)
            whole = (later if core else turned).astype(BF16)
            for width in range(4):
                out_ref[row, core, width, :SLOT, :] = whole[width * SLOT : width * SLOT + SLOT]
                out_ref[row, core, width, SLOT:, :] = packed


def patch_body(place_ref, cells_ref, out_ref, latent_ref):
    source = lax.broadcasted_iota(jnp.int32, (128, 384), 0)
    target = lax.broadcasted_iota(jnp.int32, (128, 384), 1)
    frame, row, col = source // 32, (source // 16) % 2, source % 16
    lane = lax.broadcasted_iota(jnp.int32, (8 * SLOT, 128), 1)
    grid = jnp.zeros((8 * SLOT, 384), F32)
    for width in range(4):
        place = (frame < 3) & (target == frame * 128 + row * 64 + width * 16 + col)
        rows = jnp.concatenate([cells_ref[height, width, :SLOT, :] for height in range(8)], axis=0)
        grid += jnp.dot(rows, place.astype(F32).astype(BF16), preferred_element_type=F32)
    blank = jnp.zeros((SLOT, 128), F32)
    for time_tap in range(3):
        still = grid[:, time_tap * 128 : time_tap * 128 + 128]
        left = jnp.where(lane % 64 == 0, 0.0, pltpu.roll(still, 1, 1))
        right = jnp.where(lane % 64 == 63, 0.0, pltpu.roll(still, 127, 1))
        for col_tap, base in enumerate((left, still, right)):
            swapped = pltpu.roll(base, 64, 1)
            above = jnp.concatenate([blank, swapped[:-SLOT]], axis=0)
            below = jnp.concatenate([swapped[SLOT:], blank], axis=0)
            up = jnp.where(lane < 64, above, swapped)
            down = jnp.where(lane < 64, swapped, below)
            for row_tap, value in enumerate((up, base, down)):
                tap = (time_tap * 3 + row_tap) * 3 + col_tap
                value = value.astype(BF16)
                for height in range(8):
                    out_ref[tap * SLOT : tap * SLOT + SLOT, height * 128 : height * 128 + 128] = value[
                        height * SLOT : height * SLOT + SLOT
                    ]
    out_ref[TAPS * SLOT :, :] = jnp.zeros((DEPTH - TAPS * SLOT, 1024), BF16)
    lane = lax.broadcasted_iota(jnp.int32, (GROUP, 128), 1)
    for member in range(4):
        for tile in range(2):
            packed = jnp.zeros((GROUP, 128), F32)
            for height in range(4):
                part = cells_ref[tile * 4 + height, place_ref[3]].astype(F32)[SLOT:]
                shift = (32 * height - 32 * member) % 128
                part = pltpu.roll(part, shift, 1) if shift else part
                packed += jnp.where((lane >= 32 * height) & (lane < 32 * height + 32), part, 0.0)
            latent_ref[member * GROUP : member * GROUP + GROUP, tile * 128 : tile * 128 + 128] = packed


def conv_body(patch_ref, weight_ref, out_ref):
    dense = one_hot((SLOT, 128), lambda row, col: col == row // 6 * 8 + row % 6)
    weight = jnp.dot(dense, weight_ref[...], preferred_element_type=F32).astype(BF16)
    pieces = []
    for part in range(4):
        cut = slice(part * 256, part * 256 + 256)
        pieces.append(jnp.dot(weight, patch_ref[:, cut], preferred_element_type=F32).T)
    for width in range(4):
        rows = [
            pieces[row // 4][row % 4 * 64 + width * 16 : row % 4 * 64 + width * 16 + 16] for row in range(16)
        ]
        out_ref[width] = jnp.concatenate(rows, axis=0).T.astype(BF16)


def hidden_body(part_ref, latent_ref, out_ref):
    summed = latent_ref[...]
    for source in range(4):
        summed += part_ref[source].astype(F32)
    hidden = summed.astype(BF16)
    for target in range(16):
        out_ref[target] = hidden


def column_scale(values, gain):
    mean_sq = jnp.mean(values * values, axis=0, keepdims=True)
    return values * lax.rsqrt(mean_sq + 1e-06) * gain


def attend_body(place_ref, block_ref, gain_ref, w_ref, w_out_ref, keep_ref, send_ref, hidden_ref):
    for row in range(4):
        for width in range(4):
            hidden_ref[row * SLOT : row * SLOT + SLOT, width * 256 : width * 256 + 256] = block_ref[
                row * 4 + width
            ].astype(F32)
    gain = gain_ref[...]
    cells = column_scale(hidden_ref[...], gain).astype(BF16)
    own_start = pl.multiple_of(place_ref[3] * 256 + place_ref[1] // 2 * 128, 128)
    own = hidden_ref[:, pl.ds(own_start, 128)]
    own_normed = column_scale(own, gain).T
    own = own.T
    upper = place_ref[1] % 2 == 0
    order = one_hot((384, 384), lambda place, source: source == channel_of(place))
    hidden = jnp.where(upper, own[:64], own[64:]).astype(BF16)
    normed = jnp.where(upper, own_normed[:64], own_normed[64:]).astype(BF16)
    both = jnp.concatenate([hidden, normed], axis=0)
    both = jnp.dot(both, order, preferred_element_type=F32)
    hidden, normed = both[:64], both[64:].astype(BF16)
    query = jnp.dot(normed, w_ref[:, :384], preferred_element_type=F32).astype(BF16)
    query = lax.dot_general(
        query, w_ref[:, 384:768], (((1,), (1,)), ((), ())), preferred_element_type=F32
    ).astype(BF16)
    query = lax.dot_general(
        query, order, (((1,), (1,)), ((), ())), preferred_element_type=F32
    ).astype(BF16)
    scores = jnp.dot(query, cells, preferred_element_type=F32) * (1.0 / 384.0**0.5)
    powers = jnp.exp(scores - jnp.max(scores, axis=-1, keepdims=True))
    total = jnp.sum(powers, axis=-1, keepdims=True)
    mixed = lax.dot_general(
        powers.astype(BF16), cells, (((1,), (1,)), ((), ())), preferred_element_type=F32
    )
    mixed = jnp.dot((mixed / total).astype(BF16), order, preferred_element_type=F32).astype(BF16)
    attended = jnp.dot(mixed, w_ref[:, 768:], preferred_element_type=F32).astype(BF16)
    update = jnp.dot(attended, w_out_ref[...], preferred_element_type=F32)
    decoded = (hidden + update).astype(BF16)
    first = place_ref[2] == 0
    keep_ref[...] = jnp.where(first, decoded[:32], decoded[32:])
    send_ref[...] = jnp.where(first, decoded[32:], decoded[:32])


def rms_scale(values, gain):
    mean_sq = jnp.mean(values * values, axis=-1, keepdims=True)
    return values * lax.rsqrt(mean_sq + 1e-06) * gain


def local(latent, norm_gain, conv_weight, attn_gain, w_qkv, w_out):
    channels = 384
    core = lax.axis_index("core")
    place = [lax.axis_index("tm"), lax.axis_index("y"), core, lax.axis_index("width")]
    place = jnp.stack(place).astype(jnp.int32)
    swap = [(0, 1), (1, 0)]
    shape = jax.ShapeDtypeStruct
    with jax.named_scope("earlier_frames"):
        cells = latent.reshape(64, channels)
        before = lax.ppermute(cells, "tm", [(i, i + 1) for i in range(15)])
    with jax.named_scope("weight_slices"):
        turned = jnp.transpose(conv_weight.reshape(TAPS, channels, GROUP), (0, 2, 1))
        piece = call(weight_body, shape((8, DEPTH), BF16), [SMEM, VMEM])(place, turned)
    with jax.named_scope("activated"):
        blocks = call(activate_body, shape((4, 2, 4, SLOT + GROUP, 128), BF16), [VMEM] * 3)(
            before, cells, norm_gain.reshape(1, channels)
        )
        piece, blocks = lax.optimization_barrier((piece, blocks))
        weight = lax.all_gather(piece, "tm", axis=0, tiled=True)
        blocks = lax.all_to_all(blocks.reshape(32, SLOT + GROUP, 128), ("y", "core", "width"), 0, 0)
        patches, own = call(
            patch_body, [shape((DEPTH, 1024), BF16), shape((SLOT, 256), F32)], [SMEM, VMEM]
        )(place, blocks.reshape(8, 4, SLOT + GROUP, 128))
    with jax.named_scope("conv"):
        parts = call(conv_body, shape((4, SLOT, 256), BF16), [VMEM] * 2, 700_000_000)(patches, weight)
        parts = lax.all_to_all(parts, "width", 0, 0)
    with jax.named_scope("hidden"):
        hidden = call(hidden_body, shape((16, SLOT, 256), BF16), [VMEM] * 2)(parts, own)
        hidden = lax.all_to_all(hidden, PLANE, 0, 0)
    with jax.named_scope("attention"):
        gain = attn_gain.reshape(16, 4, 6).transpose(1, 0, 2).reshape(channels, 1)
        half = shape((32, channels), BF16)
        keep, send = call(
            attend_body,
            [half, half],
            [SMEM] + [VMEM] * 4,
            200_000_000,
            scratch=[pltpu.VMEM((channels, 1024), F32)],
        )(place, hidden, gain, w_qkv, w_out)
        got = lax.ppermute(send, "core", swap)
        out = jnp.where(core == 0, jnp.concatenate([keep, got]), jnp.concatenate([got, keep]))
    return out.reshape(latent.shape)


def solution(mesh):
    devices = mesh.devices.reshape(16, 4, 2, 4)
    fine = Mesh(devices, ("tm", "y", "core", "width"))
    cells = P("tm", ("y", "core"), "width", None)
    in_specs = (cells, P(), P(None, None, None, None, "tm"), P(), P(), P())
    return jax.shard_map(local, mesh=fine, in_specs=in_specs, out_specs=cells, check_vma=False)
```

time: 98.5 us -> 95.3 us (0.968)
  starting transfers between devices: 43.7 us -> 29.2 us
  blocking collectives: 31.3 us -> 41.2 us
  Pallas kernels: 8.38 us -> 9.89 us
    all_to_all x3 -> x2, starting transfers between devices: 21.9 us -> 12.9 us  [the longest x1 8.04 us: local(): lax.all_to_all(blocks.reshape(32, SLOT + GROUP, 128), ('y', 'core', 'widt...]
    all_to_all x0 -> x1, blocking collectives: none -> 8.35 us  [local(): parts = lax.all_to_all(parts, 'width', 0, 0)]
    ppermute x2 -> x1, starting transfers between devices: 17.5 us -> 11.9 us  [local(): got = lax.ppermute(send, 'core', swap)]
    pallas_call x7 -> x6, Pallas kernels: 8.38 us -> 9.89 us  [the longest x1 2.78 us: local(): call(attend_body, [half, half], [SMEM] + [VMEM] * 4, 200000000, scratch=[...]
    all_gather x1, blocking collectives: 31.3 us -> 32.8 us  [local(): weight = lax.all_gather(piece, 'tm', axis=0, tiled=True)]
    all_to_all x3 -> x2, waiting for transfers between devices: 9.34 us -> 10.1 us  [the longest x1 10.1 us: local(): hidden = lax.all_to_all(hidden, PLANE, 0, 0)]
  transfers between devices with their start and end apart: 6 -> 4, of which waited for: 4 -> 2; matrix products, arithmetic and copies ran while one was open for 1% -> 1% of each run, Pallas kernels for 2% -> 1%
where the time goes in v4:
time: 95.3 us; the launch traced here: 94.8 us
  blocking collectives  41.2 us (43%)
  starting transfers between devices  29.2 us (31%)
  waiting for transfers between devices  11 us (12%)
  Pallas kernels  9.89 us (10%)
  local copies, waits for them, and re-layouts  2.8 us (3%)
    all_gather x1, blocking collectives, local(): weight = lax.all_gather(piece, 'tm', axis=0, tiled=True)  32.8 us
    ppermute x1, starting transfers between devices, local(): got = lax.ppermute(send, 'core', swap)  11.9 us
    all_to_all x1, waiting for transfers between devices, local(): hidden = lax.all_to_all(hidden, PLANE, 0, 0)  10.1 us
    all_to_all x1, blocking collectives, local(): parts = lax.all_to_all(parts, 'width', 0, 0)  8.35 us
    all_to_all x1, starting transfers between devices, local(): lax.all_to_all(blocks.reshape(32, SLOT + GROUP, 128), ('y', 'core', 'widt...  8.04 us
    all_to_all x1, starting transfers between devices, local(): hidden = lax.all_to_all(hidden, PLANE, 0, 0)  4.82 us
    ppermute x1, starting transfers between devices, local(): before = lax.ppermute(cells, 'tm', [(i, i + 1) for i in range(15)])  4.36 us
    pallas_call x1, Pallas kernels, local(): call(attend_body, [half, half], [SMEM] + [VMEM] * 4, 200000000, scratch=[...  2.78 us
  transfers between devices with their start and end apart: 4, of which 2 were waited for; matrix products, arithmetic and copies ran while one was open for 1% of the time, Pallas kernels for 1%

profile of v4, /device:TPU:1, one launch (start us, length us, event | category | flops | bytes accessed | tf_op | source)
XLA Modules:
  0.0 94.8 jit_solution(9000365032614661694)
XLA Ops:
  0.0 4.4 %collective-permute-start = (bf16[64,384]{1,0:T(8,128)(2,1)}, bf16[64,384]{1,0:T(8,128)(2,1)S(1)}, u32[]{:S(2)}, u32[]{:S(2)}) collective-permute-start(bf16[64,384]{1,0:T(8,128)(2,1)} %bitcast.14), channel_id=1, source_target_pairs={{0,32},{32,64},{64,96},{96,128},{128,160},{160,192},{192,224},{224... | collective-permute-start | bytes 147464 | tf_op jit(solution)/shard_map/earlier_frames/ppermute | solution.py:221
  4.4 0.1 pad_add_fusion.place_ref
  4.5 0.7 reshape.28.gain_ref
  5.1 0.0 copy-start.1
  5.1 1.0 %copy-done.1 = bf16[3,3,3,384,24]{3,4,2,1,0:T(8,128)(2,1)S(1)} copy-done((bf16[3,3,3,384,24]{3,4,2,1,0:T(8,128)(2,1)S(1)}, bf16[3,3,3,384,24]{3,4,2,1,0:T(8,128)(2,1)}, u32[]{:S(2)}) %copy-start.1) | copy-done | bytes 497688
  6.2 0.9 weight_slices.1
  7.1 0.0 collective-permute-done.before_ref
  7.1 0.0 copy-start.3
  7.1 0.8 copy-done.3
  7.9 1.6 %activated.2 = bf16[4,2,4,120,128]{4,3,2,1,0:T(8,128)(2,1)} custom-call(bf16[64,384]{1,0:T(8,128)(2,1)S(1)} %collective-permute-done.before_ref, bf16[64,384]{1,0:T(8,128)(2,1)S(1)} %bitcast.15, f32[1,384]{1,0:T(1,128)S(1)} %reshape.28.gain_ref), custom_call_target="tpu_custom_call" | custom-call | flops 1000000 | bytes 1000000 | tf_op jit(solution)/shard_map/activated/pallas_call | solution.py:226
  9.5 8.0 %all-to-all-start = ((bf16[32,120,128]{2,1,0:T(8,128)(2,1)}), bf16[32,120,128]{2,1,0:T(8,128)(2,1)S(1)}, u32[]{:S(2)}, u32[]{:S(2)}) async-start(bf16[32,120,128]{2,1,0:T(8,128)(2,1)} %bitcast.7), calls=%async_computation | async-start | bytes 1966080 | tf_op jit(solution)/shard_map/activated/all_to_all | solution.py:231
  17.5 0.0 copy-start.4
  17.5 32.8 %all_gather.3.weight_ref = bf16[128,2688]{1,0:T(8,128)(2,1)S(1)} all-gather(bf16[8,2688]{1,0:T(8,128)(2,1)S(1)} %weight_slices.1), channel_id=1, replica_groups=mesh['tm'=16,'y'=4,'core'=2,'width'=4] {'tm'}, dimensions={0}, use_global_device_ids=true | all-gather | bytes 731136 | tf_op jit(solution)/shard_map/activated/all_gather | solution.py:230
  50.4 0.0 copy-start
  50.4 0.0 copy-start.2
  50.4 0.0 all-to-all-done
  50.4 2.3 %activated.3 = (bf16[2688,1024]{1,0:T(8,128)(2,1)S(1)}, f32[96,256]{1,0:T(8,128)S(1)}) custom-call(s32[4]{0:T(128)S(1)} %pad_add_fusion.place_ref, bf16[8,4,120,128]{3,2,1,0:T(8,128)(2,1)S(1)} %bitcast.12), custom_call_target="tpu_custom_call" | custom-call | flops 1000000 | bytes 1000000 | tf_op jit(solution)/shard_map/activated/pallas_call | solution.py:232
  52.6 1.4 %conv.1 = bf16[4,96,256]{2,1,0:T(8,128)(2,1)S(1)} custom-call(bf16[2688,1024]{1,0:T(8,128)(2,1)S(1)} %get-tuple-element.12.patch_ref, bf16[128,2688]{1,0:T(8,128)(2,1)S(1)} %all_gather.3.weight_ref), custom_call_target="tpu_custom_call" | custom-call | flops 700000000 | bytes 1000000 | tf_op jit(solution)/shard_map/conv/pallas_call | solution.py:236
  54.0 8.3 %all_to_all.15.part_ref = bf16[4,96,256]{2,1,0:T(8,128)(2,1)S(1)} all-to-all(bf16[4,96,256]{2,1,0:T(8,128)(2,1)S(1)} %conv.1), channel_id=1, replica_groups=mesh['tm'=16,'y'=4,'core'=2,'width'=4] {'width'}, dimensions={0} | all-to-all | bytes 393216 | tf_op jit(solution)/shard_map/conv/all_to_all | solution.py:237
  62.4 1.0 %hidden.1 = bf16[16,96,256]{2,1,0:T(8,128)(2,1)} custom-call(bf16[4,96,256]{2,1,0:T(8,128)(2,1)S(1)} %all_to_all.15.part_ref, f32[96,256]{1,0:T(8,128)S(1)} %get-tuple-element.14.latent_ref), custom_call_target="tpu_custom_call" | custom-call | flops 1000000 | bytes 1000000 | tf_op jit(solution)/shard_map/hidden/pallas_call | solution.py:239
  63.3 4.8 %all-to-all-start.2 = ((bf16[16,96,256]{2,1,0:T(8,128)(2,1)}), bf16[16,96,256]{2,1,0:T(8,128)(2,1)S(1)}, u32[]{:S(2)}, u32[]{:S(2)}) async-start(bf16[16,96,256]{2,1,0:T(8,128)(2,1)} %hidden.1), calls=%async_computation.2 | async-start | bytes 1572864 | tf_op jit(solution)/shard_map/hidden/all_to_all | solution.py:240
  68.2 0.0 copy-done.4
  68.2 0.2 reshape.31
  68.3 0.1 reshape.33.gain_ref
  68.5 10.1 %all-to-all-done.2.block_ref = bf16[16,96,256]{2,1,0:T(8,128)(2,1)S(1)} async-done(((bf16[16,96,256]{2,1,0:T(8,128)(2,1)}), bf16[16,96,256]{2,1,0:T(8,128)(2,1)S(1)}, u32[]{:S(2)}, u32[]{:S(2)}) %all-to-all-start.2) | async-done | bytes 786464 | tf_op jit(solution)/shard_map/hidden/all_to_all | solution.py:240
  78.6 0.0 copy-done
  78.6 0.0 copy-done.2
  78.6 2.8 %attention.1 = (bf16[32,384]{1,0:T(8,128)(2,1)S(1)}, bf16[32,384]{1,0:T(8,128)(2,1)S(1)}) custom-call(s32[4]{0:T(128)S(1)} %pad_add_fusion.place_ref, bf16[16,96,256]{2,1,0:T(8,128)(2,1)S(1)} %all-to-all-done.2.block_ref, f32[384,1]{1,0:T(8,128)S(1)} %reshape.33.gain_ref, bf16[384,1152]{1,0:T(8,128)(2,1)S(1)} %copy-done, bf16[384,384]{1,0:T(8,128)(2,1)S(1)} %copy-done.2), custom_call_target="tpu_custom_call" | custom-call | flops 200000000 | bytes 1000000 | tf_op jit(solution)/shard_map/attention/pallas_call | solution.py:244
  81.4 11.9 %collective-permute-start.1 = (bf16[32,384]{1,0:T(8,128)(2,1)S(1)}, bf16[32,384]{1,0:T(8,128)(2,1)S(1)}, u32[]{:S(2)}, u32[]{:S(2)}) collective-permute-start(bf16[32,384]{1,0:T(8,128)(2,1)S(1)} %get-tuple-element.16), channel_id=1, source_target_pairs={{0,4},{4,0},{1,5},{5,1},{2,6},{6,2},{3,7},{7,3},{8,12},{12,8},{9,1... | collective-permute-start | bytes 73736 | tf_op jit(solution)/shard_map/attention/ppermute | solution.py:251
  93.3 0.8 collective-permute-done.1
  94.2 0.6 maximum_select_fusion
  (1 shorter events, 0.0 us)
Async XLA Ops:
  0.0 7.1 %collective-permute-start = (bf16[64,384]{1,0:T(8,128)(2,1)}, bf16[64,384]{1,0:T(8,128)(2,1)S(1)}, u32[]{:S(2)}, u32[]{:S(2)}) collective-permute-start(bf16[64,384]{1,0:T(8,128)(2,1)} %bitcast.14), channel_id=1, source_target_pairs={{0,32},{32,64},{64,96},{96,128},{128,160},{160,192},{192,224},{224... | collective-permute-start | bytes 147464 | tf_op jit(solution)/shard_map/earlier_frames/ppermute | solution.py:221
  5.1 1.0 %copy-start.1 = (bf16[3,3,3,384,24]{3,4,2,1,0:T(8,128)(2,1)S(1)}, bf16[3,3,3,384,24]{3,4,2,1,0:T(8,128)(2,1)}, u32[]{:S(2)}) copy-start(bf16[3,3,3,384,24]{3,4,2,1,0:T(8,128)(2,1)} %param.8) | copy-start | bytes 1492996
  7.1 0.8 copy-start.3
  9.5 40.9 %all-to-all-start = ((bf16[32,120,128]{2,1,0:T(8,128)(2,1)}), bf16[32,120,128]{2,1,0:T(8,128)(2,1)S(1)}, u32[]{:S(2)}, u32[]{:S(2)}) async-start(bf16[32,120,128]{2,1,0:T(8,128)(2,1)} %bitcast.7), calls=%async_computation | async-start | bytes 1966080 | tf_op jit(solution)/shard_map/activated/all_to_all | solution.py:231
  17.5 50.6 %copy-start.4 = (f32[384]{0:T(512)S(1)}, f32[384]{0:T(512)}, u32[]{:S(2)}) copy-start(f32[384]{0:T(512)} %param.9) | copy-start | bytes 4612
  50.4 28.2 %copy-start = (bf16[384,1152]{1,0:T(8,128)(2,1)S(1)}, bf16[384,1152]{1,0:T(8,128)(2,1)}, u32[]{:S(2)}) copy-start(bf16[384,1152]{1,0:T(8,128)(2,1)} %w_ref.1) | copy-start | bytes 2654212
  50.4 28.2 %copy-start.2 = (bf16[384,384]{1,0:T(8,128)(2,1)S(1)}, bf16[384,384]{1,0:T(8,128)(2,1)}, u32[]{:S(2)}) copy-start(bf16[384,384]{1,0:T(8,128)(2,1)} %w_out_ref.1) | copy-start | bytes 884740
  63.3 15.3 %all-to-all-start.2 = ((bf16[16,96,256]{2,1,0:T(8,128)(2,1)}), bf16[16,96,256]{2,1,0:T(8,128)(2,1)S(1)}, u32[]{:S(2)}, u32[]{:S(2)}) async-start(bf16[16,96,256]{2,1,0:T(8,128)(2,1)} %hidden.1), calls=%async_computation.2 | async-start | bytes 1572864 | tf_op jit(solution)/shard_map/hidden/all_to_all | solution.py:240
  81.4 12.8 %collective-permute-start.1 = (bf16[32,384]{1,0:T(8,128)(2,1)S(1)}, bf16[32,384]{1,0:T(8,128)(2,1)S(1)}, u32[]{:S(2)}, u32[]{:S(2)}) collective-permute-start(bf16[32,384]{1,0:T(8,128)(2,1)S(1)} %get-tuple-element.16), channel_id=1, source_target_pairs={{0,4},{4,0},{1,5},{5,1},{2,6},{6,2},{3,7},{7,3},{8,12},{12,8},{9,1... | collective-permute-start | bytes 73736 | tf_op jit(solution)/shard_map/attention/ppermute | solution.py:251

commit v5 on v4

v5 whole, which is shorter than its diff:
```python
import functools

import jax
import jax.numpy as jnp
from jax import lax
from jax.experimental import pallas as pl
from jax.experimental.pallas import tpu as pltpu
from jax.sharding import Mesh, PartitionSpec as P

F32 = jnp.float32
BF16 = jnp.bfloat16
TAPS = 27
GROUP = 24
SLOT = 96
BAND = 896
PLANE = ("width", "y")
VMEM = pl.BlockSpec(memory_space=pltpu.VMEM)
SMEM = pl.BlockSpec(memory_space=pltpu.SMEM)
HBM = pl.BlockSpec(memory_space=pltpu.HBM)
LIMIT = 12 * 1024 * 1024
FIRST_LIMIT = 54784 * 1024


def call(body, out, specs, flops=1_000_000, moved=1_000_000, scratch=(), limit=LIMIT):
    many = isinstance(out, (tuple, list))
    return pl.pallas_call(
        body,
        out_shape=out,
        in_specs=specs,
        out_specs=[VMEM] * len(out) if many else VMEM,
        scratch_shapes=list(scratch),
        compiler_params=pltpu.CompilerParams(vmem_limit_bytes=limit),
        cost_estimate=pl.CostEstimate(flops=flops, bytes_accessed=moved, transcendentals=0),
    )


def one_hot(shape, column_of):
    row = lax.broadcasted_iota(jnp.int32, (shape[0], 1), 0)
    col = lax.broadcasted_iota(jnp.int32, shape, 1)
    return (col == column_of(row)).astype(F32).astype(BF16)


def channel_of(place):
    return place % SLOT // 6 * GROUP + place // SLOT * 6 + place % 6


def activated(values, gain):
    scaled = rms_scale(values.astype(F32), gain)
    return scaled / (1.0 + jnp.exp(-scaled))


def first_body(place_ref, weight_hbm, latent_hbm, gain_ref, piece_ref, own_ref, pack_ref, weight_ref, latent_ref, sems):
    weight_copy = pltpu.make_async_copy(weight_hbm, weight_ref, sems.at[0])
    latent_copy = pltpu.make_async_copy(latent_hbm, latent_ref, sems.at[1])
    weight_copy.start()
    latent_copy.start()
    start = place_ref[3] * SLOT
    pick = one_hot((384, 128), lambda row: jnp.where(row - start < SLOT, row - start, -1))
    order = one_hot((384, 384), channel_of)
    latent_copy.wait()
    now = latent_ref[...]
    own_ref[...] = activated(now, gain_ref[...])
    latent = lax.dot_general(
        order, jnp.concatenate([now, now], axis=0), (((1,), (1,)), ((), ())), preferred_element_type=F32
    )
    lane = lax.broadcasted_iota(jnp.int32, (GROUP, 128), 1)
    for row in range(4):
        for core in range(2):
            packed = jnp.zeros((GROUP, 128), F32)
            for member in range(4):
                part = latent[row * SLOT + member * GROUP : row * SLOT + member * GROUP + GROUP]
                shift = (32 * member - 32 * core) % 128
                part = pltpu.roll(part, shift, 1) if shift else part
                packed += jnp.where((lane >= 32 * member) & (lane < 32 * member + 32), part, 0.0)
            pack_ref[row, core] = packed.astype(BF16)
    weight_copy.wait()
    rows = jnp.concatenate([weight_ref[tap] for tap in range(TAPS)], axis=0)
    picked = jnp.dot(rows, pick, preferred_element_type=F32)
    upper = place_ref[1] // 2
    picked = jnp.where(upper == 0, picked, pltpu.roll(picked, TAPS * GROUP - 12, 0))
    picked = jnp.where(place_ref[1] % 2 == 0, picked, pltpu.roll(picked, TAPS * GROUP - 6, 0))
    lane = lax.broadcasted_iota(jnp.int32, (8, 128), 1)
    kept = lax.broadcasted_iota(jnp.int32, (8, 128), 0) < 6
    tiles = [jnp.zeros((8, 128), F32) for _ in range(3 * BAND // 128)]
    for row_tap in range(3):
        for slot in range(9):
            tap = slot // 3 * 9 + row_tap * 3 + slot % 3
            value = jnp.where(kept, picked[tap * GROUP : tap * GROUP + 8], 0.0)
            tile, offset = divmod(row_tap * BAND + slot * SLOT, 128)
            value = pltpu.roll(value, offset, 1) if offset else value
            if offset + SLOT > 128:
                tiles[tile] += jnp.where(lane >= offset, value, 0.0)
                tiles[tile + 1] += jnp.where(lane < offset, value, 0.0)
            else:
                tiles[tile] += value
    main, spare = [], [[], []]
    for tile in range(BAND // 128):
        stack = jnp.concatenate([tiles[band * 7 + tile][:6] for band in range(3)], axis=0)
        main.append(stack[:16])
        spare[0].append(stack[16:17])
        spare[1].append(stack[17:])
    spare = jnp.concatenate(spare[0] + spare[1] + [jnp.zeros((2, 128), F32)], axis=0)
    piece_ref[...] = jnp.concatenate(main + [spare], axis=1).astype(BF16)


def block_body(before_ref, own_ref, pack_ref, gain_ref, out_ref):
    early = activated(before_ref[...], gain_ref[...])
    turned = jnp.concatenate([early, own_ref[...]], axis=0).T
    later = pltpu.roll(turned, 96, 1).astype(BF16)
    turned = turned.astype(BF16)
    for row in range(4):
        for core in range(2):
            whole = later if core else turned
            for width in range(4):
                out_ref[width, row, core, :SLOT, :] = whole[width * SLOT : width * SLOT + SLOT]
                out_ref[width, row, core, SLOT:, :] = pack_ref[row, core]


def grid_place(row):
    frame = row // 32 % 4
    target = frame * 128 + row // 16 % 2 * 64 + row // 128 * 16 + row % 16
    return jnp.where(frame < 3, target, -1)


def main_place(row):
    part = row // SLOT * 6 + row % 6
    return jnp.where(part < 16, row % SLOT // 6 * 16 + part, -1)


def spare_place(tile, row):
    part = row % 6 - 4
    return jnp.where(part >= 0, row // 6 * 16 + part * 7 + tile, -1)


def conv_body(place_ref, cells_ref, weight_ref, out_ref, latent_ref, flat_ref):
    lane = lax.broadcasted_iota(jnp.int32, (8 * SLOT, 128), 1) % 64
    rows = [
        jnp.concatenate([cells_ref[width, height, :SLOT, :] for height in range(8)], axis=0)
        for width in range(4)
    ]
    grid = jnp.dot(
        jnp.concatenate(rows, axis=1), one_hot((512, 384), grid_place), preferred_element_type=F32
    )
    for time_tap in range(3):
        still = grid[:, time_tap * 128 : time_tap * 128 + 128]
        left = jnp.where(lane == 0, 0.0, pltpu.roll(still, 1, 1))
        right = jnp.where(lane == 63, 0.0, pltpu.roll(still, 127, 1))
        for col_tap, base in enumerate((left, still, right)):
            slot = (time_tap * 3 + col_tap) * SLOT
            base = base.astype(BF16)
            for height in range(8):
                flat_ref[slot : slot + SLOT, height * 128 : height * 128 + 128] = base[
                    height * SLOT : height * SLOT + SLOT
                ]
    flat_ref[9 * SLOT :, :] = jnp.zeros((BAND - 9 * SLOT, 1024), BF16)
    main = jnp.dot(one_hot((3 * SLOT, 256), main_place), weight_ref[:, :BAND], preferred_element_type=F32)
    spare = [
        jnp.dot(
            one_hot((SLOT, 256), functools.partial(spare_place, tile)),
            weight_ref[:, BAND:],
            preferred_element_type=F32,
        )
        for tile in range(BAND // 128)
    ]
    last = main[2 * SLOT :] + jnp.concatenate(spare, axis=1)
    weight = jnp.concatenate([main[: 2 * SLOT], last], axis=0).astype(BF16)
    whole = jnp.dot(weight, flat_ref[...], preferred_element_type=F32)
    lane = lax.broadcasted_iota(jnp.int32, (SLOT, 1024), 1)
    total = whole[SLOT : 2 * SLOT]
    total += jnp.where(lane < 64, 0.0, pltpu.roll(whole[:SLOT], 64, 1))
    total += jnp.where(lane < 960, pltpu.roll(whole[2 * SLOT :], 960, 1), 0.0)
    pieces = [total[:, part * 256 : part * 256 + 256].T for part in range(4)]
    for width in range(4):
        rows = [
            pieces[row // 4][row % 4 * 64 + width * 16 : row % 4 * 64 + width * 16 + 16] for row in range(16)
        ]
        out_ref[width] = jnp.concatenate(rows, axis=0).T.astype(BF16)
    lane = lax.broadcasted_iota(jnp.int32, (GROUP, 128), 1)
    for member in range(4):
        for tile in range(2):
            packed = jnp.zeros((GROUP, 128), F32)
            for height in range(4):
                part = cells_ref[place_ref[3], tile * 4 + height].astype(F32)[SLOT:]
                shift = (32 * height - 32 * member) % 128
                part = pltpu.roll(part, shift, 1) if shift else part
                packed += jnp.where((lane >= 32 * height) & (lane < 32 * height + 32), part, 0.0)
            latent_ref[member * GROUP : member * GROUP + GROUP, tile * 128 : tile * 128 + 128] = packed


def hidden_body(part_ref, latent_ref, out_ref):
    summed = latent_ref[...]
    for source in range(4):
        summed += part_ref[source].astype(F32)
    hidden = summed.astype(BF16)
    for target in range(16):
        out_ref[target] = hidden


def column_scale(values, gain):
    mean_sq = jnp.mean(values * values, axis=0, keepdims=True)
    return values * lax.rsqrt(mean_sq + 1e-06) * gain


def fold_body(w_ref, w_out_ref, score_ref, update_ref):
    order = one_hot((384, 384), channel_of)
    turned = jnp.dot(order, w_ref[...], preferred_element_type=F32).astype(BF16)
    score = lax.dot_general(
        turned[:, :384], turned[:, 384:768], (((1,), (1,)), ((), ())), preferred_element_type=F32
    )
    score_ref[...] = (score * (1.0 / 384.0**0.5)).astype(BF16)
    update_ref[...] = jnp.dot(turned[:, 768:], w_out_ref[...], preferred_element_type=F32).astype(BF16)


def attend_body(place_ref, block_ref, gain_ref, score_ref, update_ref, keep_ref, send_ref, hidden_ref, cells_ref):
    for row in range(4):
        for width in range(4):
            hidden_ref[row * SLOT : row * SLOT + SLOT, width * 256 : width * 256 + 256] = block_ref[
                width * 4 + row
            ].astype(F32)
    cells = column_scale(hidden_ref[...], gain_ref[...]).astype(BF16)
    cells_ref[...] = cells
    own_cut = pl.ds(pl.multiple_of(place_ref[3] * 256 + place_ref[1] // 2 * 128, 128), 128)
    upper = place_ref[1] % 2 == 0
    own_normed = cells_ref[:, own_cut].astype(F32).T
    own_normed = jnp.where(upper, own_normed[:64], own_normed[64:]).astype(BF16)
    own = hidden_ref[:, own_cut].T
    own = jnp.where(upper, own[:64], own[64:]).astype(BF16)
    order = one_hot((384, 384), channel_of)
    own = jnp.dot(own, order, preferred_element_type=F32)
    query = jnp.dot(own_normed, score_ref[...], preferred_element_type=F32).astype(BF16)
    scores = jnp.dot(query, cells, preferred_element_type=F32)
    powers = jnp.exp(scores - jnp.max(scores, axis=-1, keepdims=True))
    total = jnp.sum(powers, axis=-1, keepdims=True)
    mixed = lax.dot_general(
        powers.astype(BF16), cells, (((1,), (1,)), ((), ())), preferred_element_type=F32
    )
    mixed = (mixed / total).astype(BF16)
    decoded = (own + jnp.dot(mixed, update_ref[...], preferred_element_type=F32)).astype(BF16)
    first = place_ref[2] == 0
    keep_ref[...] = jnp.where(first, decoded[:32], decoded[32:])
    send_ref[...] = jnp.where(first, decoded[32:], decoded[:32])


def rms_scale(values, gain):
    mean_sq = jnp.mean(values * values, axis=-1, keepdims=True)
    return values * lax.rsqrt(mean_sq + 1e-06) * gain


def local(latent, norm_gain, conv_weight, attn_gain, w_qkv, w_out):
    channels = 384
    core = lax.axis_index("core")
    place = [lax.axis_index("tm"), lax.axis_index("y"), core, lax.axis_index("width")]
    place = jnp.stack(place).astype(jnp.int32)
    swap = [(0, 1), (1, 0)]
    shape = jax.ShapeDtypeStruct
    with jax.named_scope("earlier_frames"):
        cells = latent.reshape(64, channels)
        before = lax.ppermute(cells, "tm", [(i, i + 1) for i in range(15)])
    with jax.named_scope("activated"):
        gain = norm_gain.reshape(1, channels)
        turned = jnp.transpose(conv_weight.reshape(TAPS, channels, GROUP), (0, 2, 1))
        piece, now, pack = call(
            first_body,
            [shape((16, 1024), BF16), shape((64, channels), F32), shape((4, 2, GROUP, 128), BF16)],
            [SMEM, HBM, HBM, VMEM],
            scratch=[
                pltpu.VMEM((TAPS, GROUP, channels), BF16),
                pltpu.VMEM((64, channels), BF16),
                pltpu.SemaphoreType.DMA((2,)),
            ],
            limit=FIRST_LIMIT,
        )(place, turned, cells, gain)
        blocks = call(block_body, shape((4, 4, 2, SLOT + GROUP, 128), BF16), [VMEM] * 4)(
            before, now, pack, gain
        )
        piece, blocks = lax.optimization_barrier((piece, blocks))
        weight = lax.all_gather(piece, "tm", axis=0, tiled=True)
        blocks = lax.all_to_all(blocks.reshape(32, SLOT + GROUP, 128), ("width", "y", "core"), 0, 0)
    with jax.named_scope("conv"):
        parts, own = call(
            conv_body,
            [shape((4, SLOT, 256), BF16), shape((SLOT, 256), F32)],
            [SMEM, VMEM, VMEM],
            700_000_000,
            scratch=[pltpu.VMEM((BAND, 1024), BF16)],
        )(place, blocks.reshape(4, 8, SLOT + GROUP, 128), weight)
        parts = lax.all_to_all(parts, "width", 0, 0)
    with jax.named_scope("hidden"):
        hidden = call(hidden_body, shape((16, SLOT, 256), BF16), [VMEM] * 2)(parts, own)
        hidden = lax.all_to_all(hidden, PLANE, 0, 0)
    with jax.named_scope("attention"):
        gain = attn_gain.reshape(16, 4, 6).transpose(1, 0, 2).reshape(channels, 1)
        square, half = shape((channels, channels), BF16), shape((32, channels), BF16)
        score, update = call(fold_body, [square, square], [VMEM] * 2, 600_000_000)(w_qkv, w_out)
        keep, send = call(
            attend_body,
            [half, half],
            [SMEM] + [VMEM] * 4,
            200_000_000,
            scratch=[pltpu.VMEM((channels, 1024), F32), pltpu.VMEM((channels, 1024), BF16)],
        )(place, hidden, gain, score, update)
        got = lax.ppermute(send, "core", swap)
        out = jnp.where(core == 0, jnp.concatenate([keep, got]), jnp.concatenate([got, keep]))
    return out.reshape(latent.shape)


def solution(mesh):
    devices = mesh.devices.reshape(16, 4, 2, 4)
    fine = Mesh(devices, ("tm", "y", "core", "width"))
    cells = P("tm", ("y", "core"), "width", None)
    in_specs = (cells, P(), P(None, None, None, None, "tm"), P(), P(), P())
    return jax.shard_map(local, mesh=fine, in_specs=in_specs, out_specs=cells, check_vma=False)
```

time: 95.3 us -> 91.9 us (0.964)
  waiting for transfers between devices: 11 us -> 8.95 us
  blocking collectives: 41.2 us -> 39.9 us
    all_to_all x1, waiting for transfers between devices: 10.1 us -> 8.12 us  [local(): hidden = lax.all_to_all(hidden, PLANE, 0, 0)]
    all_gather x1, blocking collectives: 32.8 us -> 31 us  [local(): weight = lax.all_gather(piece, 'tm', axis=0, tiled=True)]
    pallas_call x4, Pallas kernels: 6.13 us -> 7.15 us  [the longest x1 2.64 us: local(): call(conv_body, [shape((4, SLOT, 256), BF16), shape((SLOT, 256), F32)], [...]
  transfers between devices with their start and end apart: 4 -> 4, of which waited for: 2 -> 2; matrix products, arithmetic and copies ran while one was open for 1% -> 0% of each run, Pallas kernels for 1% -> 4%
where the time goes in v5:
time: 91.9 us; the launch traced here: 91.3 us
  blocking collectives  39.9 us (43%)
  starting transfers between devices  28.9 us (31%)
  Pallas kernels  10.5 us (11%)
  waiting for transfers between devices  8.95 us (10%)
  local copies, waits for them, and re-layouts  2.33 us (3%)
    all_gather x1, blocking collectives, local(): weight = lax.all_gather(piece, 'tm', axis=0, tiled=True)  31 us
    ppermute x1, starting transfers between devices, local(): got = lax.ppermute(send, 'core', swap)  11.6 us
    all_to_all x1, blocking collectives, local(): parts = lax.all_to_all(parts, 'width', 0, 0)  8.86 us
    all_to_all x1, waiting for transfers between devices, local(): hidden = lax.all_to_all(hidden, PLANE, 0, 0)  8.12 us
    all_to_all x1, starting transfers between devices, local(): lax.all_to_all(blocks.reshape(32, SLOT + GROUP, 128), ('width', 'y', 'cor...  8.04 us
    all_to_all x1, starting transfers between devices, local(): hidden = lax.all_to_all(hidden, PLANE, 0, 0)  4.85 us
    ppermute x1, starting transfers between devices, local(): before = lax.ppermute(cells, 'tm', [(i, i + 1) for i in range(15)])  4.36 us
    pallas_call x1, Pallas kernels, local(): call(conv_body, [shape((4, SLOT, 256), BF16), shape((SLOT, 256), F32)], [...  2.64 us
  transfers between devices with their start and end apart: 4, of which 2 were waited for; matrix products, arithmetic and copies ran while one was open for 0% of the time, Pallas kernels for 4%

profile of v5, /device:TPU:1, one launch (start us, length us, event | category | flops | bytes accessed | tf_op | source)
XLA Modules:
  0.0 91.3 jit_solution(1988455684795106297)
XLA Ops:
  0.0 4.4 %collective-permute-start = (bf16[64,384]{1,0:T(8,128)(2,1)}, bf16[64,384]{1,0:T(8,128)(2,1)S(1)}, u32[]{:S(2)}, u32[]{:S(2)}) collective-permute-start(bf16[64,384]{1,0:T(8,128)(2,1)} %bitcast.13), channel_id=1, source_target_pairs={{0,32},{32,64},{64,96},{96,128},{128,160},{160,192},{192,224},{224... | collective-permute-start | bytes 147464 | tf_op jit(solution)/shard_map/earlier_frames/ppermute | solution.py:258
  4.4 0.0 copy-start.4
  4.4 0.1 pad_add_fusion.place_ref
  4.5 0.6 copy-done.4
  5.1 0.0 copy-start
  5.1 0.8 copy-done
  5.9 2.0 %activated.2 = (bf16[16,1024]{1,0:T(8,128)(2,1)S(1)}, f32[64,384]{1,0:T(8,128)S(1)}, bf16[4,2,24,128]{3,2,1,0:T(8,128)(2,1)S(1)}) custom-call(s32[4]{0:T(128)S(1)} %pad_add_fusion.place_ref, bf16[27,24,384]{2,1,0:T(8,128)(2,1)} %bitcast.15, bf16[64,384]{1,0:T(8,128)(2,1)S(1)} %bitcast.14, f32[1,384]{1,0:T(1,128)S(1)} %reshape.28.gain_ref), custom_call_target="tpu_custom_call" | custom-call | flops 1000000 | bytes 1000000 | tf_op jit(solution)/shard_map/activated/pallas_call | solution.py:262
  7.9 0.0 collective-permute-done.before_ref
  7.9 1.2 %activated.3 = bf16[4,4,2,120,128]{4,3,2,1,0:T(8,128)(2,1)} custom-call(bf16[64,384]{1,0:T(8,128)(2,1)S(1)} %collective-permute-done.before_ref, f32[64,384]{1,0:T(8,128)S(1)} %get-tuple-element.17.own_ref, bf16[4,2,24,128]{3,2,1,0:T(8,128)(2,1)S(1)} %get-tuple-element.18.pack_ref, f32[1,384]{1,0:T(1,128)S(1)} %reshape.28.gain_ref), custom_call_target="tpu_custom_call" | custom-call | flops 1000000 | bytes 1000000 | tf_op jit(solution)/shard_map/activated/pallas_call | solution.py:273
  9.1 8.0 %all-to-all-start = ((bf16[32,120,128]{2,1,0:T(8,128)(2,1)}), bf16[32,120,128]{2,1,0:T(8,128)(2,1)S(1)}, u32[]{:S(2)}, u32[]{:S(2)}) async-start(bf16[32,120,128]{2,1,0:T(8,128)(2,1)} %bitcast.7), calls=%async_computation | async-start | bytes 1966080 | tf_op jit(solution)/shard_map/activated/all_to_all | solution.py:278
  17.2 31.0 %all_gather.3.weight_ref = bf16[256,1024]{1,0:T(8,128)(2,1)S(1)} all-gather(bf16[16,1024]{1,0:T(8,128)(2,1)S(1)} %get-tuple-element.20), channel_id=1, replica_groups=mesh['tm'=16,'y'=4,'core'=2,'width'=4] {'tm'}, dimensions={0}, use_global_device_ids=true | all-gather | bytes 557056 | tf_op jit(solution)/shard_map/activated/all_gather | solution.py:277
  48.2 0.0 all-to-all-done
  48.2 2.6 %conv.1 = (bf16[4,96,256]{2,1,0:T(8,128)(2,1)S(1)}, f32[96,256]{1,0:T(8,128)S(1)}) custom-call(s32[4]{0:T(128)S(1)} %pad_add_fusion.place_ref, bf16[4,8,120,128]{3,2,1,0:T(8,128)(2,1)S(1)} %bitcast.12, bf16[256,1024]{1,0:T(8,128)(2,1)S(1)} %all_gather.3.weight_ref), custom_call_target="tpu_custom_call" | custom-call | flops 700000000 | bytes 1000000 | tf_op jit(solution)/shard_map/conv/pallas_call | solution.py:280
  50.8 8.9 %all_to_all.15.part_ref = bf16[4,96,256]{2,1,0:T(8,128)(2,1)S(1)} all-to-all(bf16[4,96,256]{2,1,0:T(8,128)(2,1)S(1)} %get-tuple-element.21), channel_id=1, replica_groups=mesh['tm'=16,'y'=4,'core'=2,'width'=4] {'width'}, dimensions={0} | all-to-all | bytes 393216 | tf_op jit(solution)/shard_map/conv/all_to_all | solution.py:287
  59.7 1.0 %hidden.1 = bf16[16,96,256]{2,1,0:T(8,128)(2,1)} custom-call(bf16[4,96,256]{2,1,0:T(8,128)(2,1)S(1)} %all_to_all.15.part_ref, f32[96,256]{1,0:T(8,128)S(1)} %get-tuple-element.22.latent_ref), custom_call_target="tpu_custom_call" | custom-call | flops 1000000 | bytes 1000000 | tf_op jit(solution)/shard_map/hidden/pallas_call | solution.py:289
  60.7 0.0 copy-start.3
  60.7 0.0 copy-start.1
  60.7 4.8 %all-to-all-start.2 = ((bf16[16,96,256]{2,1,0:T(8,128)(2,1)}), bf16[16,96,256]{2,1,0:T(8,128)(2,1)S(1)}, u32[]{:S(2)}, u32[]{:S(2)}) async-start(bf16[16,96,256]{2,1,0:T(8,128)(2,1)} %hidden.1), calls=%async_computation.2 | async-start | bytes 1572864 | tf_op jit(solution)/shard_map/hidden/all_to_all | solution.py:290
  65.6 0.0 copy-done.3
  65.6 0.0 copy-start.2
  65.6 0.2 reshape.31
  65.8 0.1 reshape.33.gain_ref
  65.9 0.0 copy-done.1
  65.9 0.7 copy-done.2
  66.5 1.2 %attention.2 = (bf16[384,384]{1,0:T(8,128)(2,1)S(1)}, bf16[384,384]{1,0:T(8,128)(2,1)S(1)}) custom-call(bf16[384,1152]{1,0:T(8,128)(2,1)S(1)} %copy-done.1, bf16[384,384]{1,0:T(8,128)(2,1)S(1)} %copy-done.2), custom_call_target="tpu_custom_call" | custom-call | flops 600000000 | bytes 1000000 | tf_op jit(solution)/shard_map/attention/pallas_call | solution.py:294
  67.8 8.1 %all-to-all-done.2.block_ref = bf16[16,96,256]{2,1,0:T(8,128)(2,1)S(1)} async-done(((bf16[16,96,256]{2,1,0:T(8,128)(2,1)}), bf16[16,96,256]{2,1,0:T(8,128)(2,1)S(1)}, u32[]{:S(2)}, u32[]{:S(2)}) %all-to-all-start.2) | async-done | bytes 786464 | tf_op jit(solution)/shard_map/hidden/all_to_all | solution.py:290
  75.9 2.3 %attention.3 = (bf16[32,384]{1,0:T(8,128)(2,1)S(1)}, bf16[32,384]{1,0:T(8,128)(2,1)S(1)}) custom-call(s32[4]{0:T(128)S(1)} %pad_add_fusion.place_ref, bf16[16,96,256]{2,1,0:T(8,128)(2,1)S(1)} %all-to-all-done.2.block_ref, f32[384,1]{1,0:T(8,128)S(1)} %reshape.33.gain_ref, bf16[384,384]{1,0:T(8,128)(2,1)S(1)} %get-tuple-element.23.score_ref, ...), custom_call_target="tpu_custom_call" | custom-call | flops 200000000 | bytes 1000000 | tf_op jit(solution)/shard_map/attention/pallas_call | solution.py:295
  78.2 11.6 %collective-permute-start.1 = (bf16[32,384]{1,0:T(8,128)(2,1)S(1)}, bf16[32,384]{1,0:T(8,128)(2,1)S(1)}, u32[]{:S(2)}, u32[]{:S(2)}) collective-permute-start(bf16[32,384]{1,0:T(8,128)(2,1)S(1)} %get-tuple-element.26), channel_id=1, source_target_pairs={{0,4},{4,0},{1,5},{5,1},{2,6},{6,2},{3,7},{7,3},{8,12},{12,8},{9,1... | collective-permute-start | bytes 73736 | tf_op jit(solution)/shard_map/attention/ppermute | solution.py:302
  89.9 0.8 collective-permute-done.1
  90.7 0.6 maximum_select_fusion
  (2 shorter events, 0.0 us)
Async XLA Ops:
  0.0 7.9 %collective-permute-start = (bf16[64,384]{1,0:T(8,128)(2,1)}, bf16[64,384]{1,0:T(8,128)(2,1)S(1)}, u32[]{:S(2)}, u32[]{:S(2)}) collective-permute-start(bf16[64,384]{1,0:T(8,128)(2,1)} %bitcast.13), channel_id=1, source_target_pairs={{0,32},{32,64},{64,96},{96,128},{128,160},{160,192},{192,224},{224... | collective-permute-start | bytes 147464 | tf_op jit(solution)/shard_map/earlier_frames/ppermute | solution.py:258
  4.4 0.7 copy-start.4
  5.1 0.8 copy-start
  9.1 39.1 %all-to-all-start = ((bf16[32,120,128]{2,1,0:T(8,128)(2,1)}), bf16[32,120,128]{2,1,0:T(8,128)(2,1)S(1)}, u32[]{:S(2)}, u32[]{:S(2)}) async-start(bf16[32,120,128]{2,1,0:T(8,128)(2,1)} %bitcast.7), calls=%async_computation | async-start | bytes 1966080 | tf_op jit(solution)/shard_map/activated/all_to_all | solution.py:278
  60.7 4.9 %copy-start.3 = (f32[384]{0:T(512)S(1)}, f32[384]{0:T(512)}, u32[]{:S(2)}) copy-start(f32[384]{0:T(512)} %param.9) | copy-start | bytes 4612
  60.7 5.2 %copy-start.1 = (bf16[384,1152]{1,0:T(8,128)(2,1)S(1)}, bf16[384,1152]{1,0:T(8,128)(2,1)}, u32[]{:S(2)}) copy-start(bf16[384,1152]{1,0:T(8,128)(2,1)} %w_ref.1) | copy-start | bytes 2654212
  60.7 15.2 %all-to-all-start.2 = ((bf16[16,96,256]{2,1,0:T(8,128)(2,1)}), bf16[16,96,256]{2,1,0:T(8,128)(2,1)S(1)}, u32[]{:S(2)}, u32[]{:S(2)}) async-start(bf16[16,96,256]{2,1,0:T(8,128)(2,1)} %hidden.1), calls=%async_computation.2 | async-start | bytes 1572864 | tf_op jit(solution)/shard_map/hidden/all_to_all | solution.py:290
  65.6 1.0 %copy-start.2 = (bf16[384,384]{1,0:T(8,128)(2,1)S(1)}, bf16[384,384]{1,0:T(8,128)(2,1)}, u32[]{:S(2)}) copy-start(bf16[384,384]{1,0:T(8,128)(2,1)} %w_out_ref.1) | copy-start | bytes 884740
  78.2 12.5 %collective-permute-start.1 = (bf16[32,384]{1,0:T(8,128)(2,1)S(1)}, bf16[32,384]{1,0:T(8,128)(2,1)S(1)}, u32[]{:S(2)}, u32[]{:S(2)}) collective-permute-start(bf16[32,384]{1,0:T(8,128)(2,1)S(1)} %get-tuple-element.26), channel_id=1, source_target_pairs={{0,4},{4,0},{1,5},{5,1},{2,6},{6,2},{3,7},{7,3},{8,12},{12,8},{9,1... | collective-permute-start | bytes 73736 | tf_op jit(solution)/shard_map/attention/ppermute | solution.py:302

commit v6 on v5

--- a/solution.py
+++ b/solution.py
@@ -18,7 +18,7 @@
 SMEM = pl.BlockSpec(memory_space=pltpu.SMEM)
 HBM = pl.BlockSpec(memory_space=pltpu.HBM)
 LIMIT = 12 * 1024 * 1024
-FIRST_LIMIT = 54784 * 1024
+FIRST_LIMIT = 55072 * 1024
 
 
 def call(body, out, specs, flops=1_000_000, moved=1_000_000, scratch=(), limit=LIMIT):
@@ -49,17 +49,22 @@
     return scaled / (1.0 + jnp.exp(-scaled))
 
 
-def first_body(place_ref, weight_hbm, latent_hbm, gain_ref, piece_ref, own_ref, pack_ref, weight_ref, latent_ref, sems):
+def first_body(
+    place_ref, weight_hbm, latent_hbm, gain_hbm, piece_ref, own_ref, pack_ref, weight_ref, latent_ref, gain_ref, sems
+):
     weight_copy = pltpu.make_async_copy(weight_hbm, weight_ref, sems.at[0])
     latent_copy = pltpu.make_async_copy(latent_hbm, latent_ref, sems.at[1])
+    gain_copy = pltpu.make_async_copy(gain_hbm, gain_ref, sems.at[2])
+    latent_copy.start()
+    gain_copy.start()
     weight_copy.start()
-    latent_copy.start()
     start = place_ref[3] * SLOT
     pick = one_hot((384, 128), lambda row: jnp.where(row - start < SLOT, row - start, -1))
     order = one_hot((384, 384), channel_of)
     latent_copy.wait()
+    gain_copy.wait()
     now = latent_ref[...]
-    own_ref[...] = activated(now, gain_ref[...])
+    own_ref[...] = activated(now, gain_ref[...].reshape(1, 384)).astype(BF16)
     latent = lax.dot_general(
         order, jnp.concatenate([now, now], axis=0), (((1,), (1,)), ((), ())), preferred_element_type=F32
     )
@@ -104,8 +109,8 @@
 
 
 def block_body(before_ref, own_ref, pack_ref, gain_ref, out_ref):
-    early = activated(before_ref[...], gain_ref[...])
-    turned = jnp.concatenate([early, own_ref[...]], axis=0).T
+    early = activated(before_ref[...], gain_ref[...].reshape(1, 384))
+    turned = jnp.concatenate([early, own_ref[...].astype(F32)], axis=0).T
     later = pltpu.roll(turned, 96, 1).astype(BF16)
     turned = turned.astype(BF16)
     for row in range(4):
@@ -196,46 +201,48 @@
         out_ref[target] = hidden
 
 
-def column_scale(values, gain):
-    mean_sq = jnp.mean(values * values, axis=0, keepdims=True)
-    return values * lax.rsqrt(mean_sq + 1e-06) * gain
-
-
-def fold_body(w_ref, w_out_ref, score_ref, update_ref):
+def fold_body(w_ref, w_out_ref, row_ref, column_ref, score_ref, update_ref):
     order = one_hot((384, 384), channel_of)
-    turned = jnp.dot(order, w_ref[...], preferred_element_type=F32).astype(BF16)
+    gain = column_ref[...]
     score = lax.dot_general(
-        turned[:, :384], turned[:, 384:768], (((1,), (1,)), ((), ())), preferred_element_type=F32
+        w_ref[:, :384], w_ref[:, 384:768], (((1,), (1,)), ((), ())), preferred_element_type=F32
     )
-    score_ref[...] = (score * (1.0 / 384.0**0.5)).astype(BF16)
-    update_ref[...] = jnp.dot(turned[:, 768:], w_out_ref[...], preferred_element_type=F32).astype(BF16)
-
-
-def attend_body(place_ref, block_ref, gain_ref, score_ref, update_ref, keep_ref, send_ref, hidden_ref, cells_ref):
-    for row in range(4):
-        for width in range(4):
-            hidden_ref[row * SLOT : row * SLOT + SLOT, width * 256 : width * 256 + 256] = block_ref[
-                width * 4 + row
-            ].astype(F32)
-    cells = column_scale(hidden_ref[...], gain_ref[...]).astype(BF16)
-    cells_ref[...] = cells
-    own_cut = pl.ds(pl.multiple_of(place_ref[3] * 256 + place_ref[1] // 2 * 128, 128), 128)
-    upper = place_ref[1] % 2 == 0
-    own_normed = cells_ref[:, own_cut].astype(F32).T
-    own_normed = jnp.where(upper, own_normed[:64], own_normed[64:]).astype(BF16)
-    own = hidden_ref[:, own_cut].T
-    own = jnp.where(upper, own[:64], own[64:]).astype(BF16)
-    order = one_hot((384, 384), channel_of)
-    own = jnp.dot(own, order, preferred_element_type=F32)
-    query = jnp.dot(own_normed, score_ref[...], preferred_element_type=F32).astype(BF16)
-    scores = jnp.dot(query, cells, preferred_element_type=F32)
-    powers = jnp.exp(scores - jnp.max(scores, axis=-1, keepdims=True))
-    total = jnp.sum(powers, axis=-1, keepdims=True)
-    mixed = lax.dot_general(
-        powers.astype(BF16), cells, (((1,), (1,)), ((), ())), preferred_element_type=F32
-    )
+    score = (score * (gain * (1.0 / 384.0**0.5)) * row_ref[...]).astype(BF16)
+    score = jnp.dot(order, score, preferred_element_type=F32).astype(BF16)
+    score = lax.dot_general(score, order, (((1,), (1,)), ((), ())), preferred_element_type=F32)
+    score_ref[...] = score.astype(BF16)
+    update = jnp.dot(w_ref[:, 768:], w_out_ref[...], preferred_element_type=F32) * gain
+    update_ref[...] = jnp.dot(order, update.astype(BF16), preferred_element_type=F32).astype(BF16)
+
+
+def attend_body(place_ref, block_ref, score_ref, update_ref, keep_ref, send_ref):
+    own = block_ref[place_ref[3]]
+    own = jnp.where(place_ref[1] < 2, own[:, :128], own[:, 128:]).astype(F32).T
+    own = jnp.where(place_ref[1] % 2 == 0, own[:64], own[64:])
+    own_scale = lax.rsqrt(jnp.mean(own * own, axis=-1, keepdims=True) + 1e-06)
+    own = own.astype(BF16)
+    query = jnp.dot(own, score_ref[...], preferred_element_type=F32)
+    query = (query * own_scale).astype(BF16)
+    hidden = jnp.dot(own, one_hot((384, 384), channel_of), preferred_element_type=F32)
+    scales, scores = [], []
+    for width in range(4):
+        cells = block_ref[width]
+        values = cells.astype(F32)
+        scale = lax.rsqrt(jnp.mean(values * values, axis=0, keepdims=True) + 1e-06)
+        scales.append(scale)
+        scores.append(jnp.dot(query, cells, preferred_element_type=F32) * scale)
+    peak = functools.reduce(jnp.maximum, [jnp.max(part, axis=-1, keepdims=True) for part in scores])
+    total = jnp.zeros((64, 1), F32)
+    mixed = jnp.zeros((64, 384), F32)
+    for width in range(4):
+        powers = jnp.exp(scores[width] - peak)
+        total += jnp.sum(powers, axis=-1, keepdims=True)
+        powers = (powers * scales[width]).astype(BF16)
+        mixed += lax.dot_general(
+            powers, block_ref[width], (((1,), (1,)), ((), ())), preferred_element_type=F32
+        )
     mixed = (mixed / total).astype(BF16)
-    decoded = (own + jnp.dot(mixed, update_ref[...], preferred_element_type=F32)).astype(BF16)
+    decoded = (hidden + jnp.dot(mixed, update_ref[...], preferred_element_type=F32)).astype(BF16)
     first = place_ref[2] == 0
     keep_ref[...] = jnp.where(first, decoded[:32], decoded[32:])
     send_ref[...] = jnp.where(first, decoded[32:], decoded[:32])
@@ -257,21 +264,21 @@
         cells = latent.reshape(64, channels)
         before = lax.ppermute(cells, "tm", [(i, i + 1) for i in range(15)])
     with jax.named_scope("activated"):
-        gain = norm_gain.reshape(1, channels)
         turned = jnp.transpose(conv_weight.reshape(TAPS, channels, GROUP), (0, 2, 1))
         piece, now, pack = call(
             first_body,
-            [shape((16, 1024), BF16), shape((64, channels), F32), shape((4, 2, GROUP, 128), BF16)],
-            [SMEM, HBM, HBM, VMEM],
+            [shape((16, 1024), BF16), shape((64, channels), BF16), shape((4, 2, GROUP, 128), BF16)],
+            [SMEM, HBM, HBM, HBM],
             scratch=[
                 pltpu.VMEM((TAPS, GROUP, channels), BF16),
                 pltpu.VMEM((64, channels), BF16),
-                pltpu.SemaphoreType.DMA((2,)),
+                pltpu.VMEM((channels,), F32),
+                pltpu.SemaphoreType.DMA((3,)),
             ],
             limit=FIRST_LIMIT,
-        )(place, turned, cells, gain)
+        )(place, turned, cells, norm_gain)
         blocks = call(block_body, shape((4, 4, 2, SLOT + GROUP, 128), BF16), [VMEM] * 4)(
-            before, now, pack, gain
+            before, now, pack, norm_gain
         )
         piece, blocks = lax.optimization_barrier((piece, blocks))
         weight = lax.all_gather(piece, "tm", axis=0, tiled=True)
@@ -289,16 +296,13 @@
         hidden = call(hidden_body, shape((16, SLOT, 256), BF16), [VMEM] * 2)(parts, own)
         hidden = lax.all_to_all(hidden, PLANE, 0, 0)
     with jax.named_scope("attention"):
-        gain = attn_gain.reshape(16, 4, 6).transpose(1, 0, 2).reshape(channels, 1)
         square, half = shape((channels, channels), BF16), shape((32, channels), BF16)
-        score, update = call(fold_body, [square, square], [VMEM] * 2, 600_000_000)(w_qkv, w_out)
-        keep, send = call(
-            attend_body,
-            [half, half],
-            [SMEM] + [VMEM] * 4,
-            200_000_000,
-            scratch=[pltpu.VMEM((channels, 1024), F32), pltpu.VMEM((channels, 1024), BF16)],
-        )(place, hidden, gain, score, update)
+        score, update = call(fold_body, [square, square], [VMEM] * 4, 600_000_000)(
+            w_qkv, w_out, attn_gain.reshape(1, channels), attn_gain.reshape(channels, 1)
+        )
+        keep, send = call(attend_body, [half, half], [SMEM] + [VMEM] * 3, 200_000_000)(
+            place, hidden.reshape(4, channels, 256), score, update
+        )
         got = lax.ppermute(send, "core", swap)
         out = jnp.where(core == 0, jnp.concatenate([keep, got]), jnp.concatenate([got, keep]))
     return out.reshape(latent.shape)

time: 91.9 us -> 91.3 us (level)
  local copies, waits for them, and re-layouts: 2.33 us -> 0.72 us
    unnamed x10 -> x8, local copies, waits for them, and re-layouts: 2.06 us -> 0.61 us
where the time goes in v6:
time: 91.3 us; the launch traced here: 90.9 us
  blocking collectives  40.2 us (44%)
  starting transfers between devices  29.3 us (32%)
  Pallas kernels  10.3 us (11%)
  waiting for transfers between devices  9.49 us (10%)
    all_gather x1, blocking collectives, local(): weight = lax.all_gather(piece, 'tm', axis=0, tiled=True)  31.7 us
    ppermute x1, starting transfers between devices, local(): got = lax.ppermute(send, 'core', swap)  12.1 us
    all_to_all x1, waiting for transfers between devices, local(): hidden = lax.all_to_all(hidden, PLANE, 0, 0)  8.66 us
    all_to_all x1, blocking collectives, local(): parts = lax.all_to_all(parts, 'width', 0, 0)  8.5 us
    all_to_all x1, starting transfers between devices, local(): lax.all_to_all(blocks.reshape(32, SLOT + GROUP, 128), ('width', 'y', 'cor...  8.04 us
    all_to_all x1, starting transfers between devices, local(): hidden = lax.all_to_all(hidden, PLANE, 0, 0)  4.83 us
    ppermute x1, starting transfers between devices, local(): before = lax.ppermute(cells, 'tm', [(i, i + 1) for i in range(15)])  4.36 us
    pallas_call x1, Pallas kernels, local(): call(conv_body, [shape((4, SLOT, 256), BF16), shape((SLOT, 256), F32)], [...  2.64 us
  transfers between devices with their start and end apart: 4, of which 2 were waited for; matrix products, arithmetic and copies ran while one was open for 0% of the time, Pallas kernels for 4%

profile of v6, /device:TPU:1, one launch (start us, length us, event | category | flops | bytes accessed | tf_op | source)
XLA Modules:
  0.0 90.9 jit_solution(7065175375865323888)
XLA Ops:
  0.0 4.4 %collective-permute-start = (bf16[64,384]{1,0:T(8,128)(2,1)}, bf16[64,384]{1,0:T(8,128)(2,1)S(1)}, u32[]{:S(2)}, u32[]{:S(2)}) collective-permute-start(bf16[64,384]{1,0:T(8,128)(2,1)} %bitcast.15), channel_id=1, source_target_pairs={{0,32},{32,64},{64,96},{96,128},{128,160},{160,192},{192,224},{224... | collective-permute-start | bytes 147464 | tf_op jit(solution)/shard_map/earlier_frames/ppermute | solution.py:265
  4.4 0.0 copy-start
  4.4 0.1 pad_add_fusion.place_ref
  4.5 0.6 copy-done
  5.1 2.1 %activated.2 = (bf16[16,1024]{1,0:T(8,128)(2,1)S(1)}, bf16[64,384]{1,0:T(8,128)(2,1)S(1)}, bf16[4,2,24,128]{3,2,1,0:T(8,128)(2,1)S(1)}) custom-call(s32[4]{0:T(128)S(1)} %pad_add_fusion.place_ref, bf16[27,24,384]{2,1,0:T(8,128)(2,1)} %bitcast.14, bf16[64,384]{1,0:T(8,128)(2,1)} %bitcast.16, f32[384]{0:T(512)S(1)} %copy-done), custom_call_target="tpu_custom_call" | custom-call | flops 1000000 | bytes 1000000 | tf_op jit(solution)/shard_map/activated/pallas_call | solution.py:268
  7.2 0.0 collective-permute-done.before_ref
  7.2 1.2 %activated.3 = bf16[4,4,2,120,128]{4,3,2,1,0:T(8,128)(2,1)} custom-call(bf16[64,384]{1,0:T(8,128)(2,1)S(1)} %collective-permute-done.before_ref, bf16[64,384]{1,0:T(8,128)(2,1)S(1)} %get-tuple-element.17.own_ref, bf16[4,2,24,128]{3,2,1,0:T(8,128)(2,1)S(1)} %get-tuple-element.18.pack_ref, f32[384]{0:T(512)S(1)} %copy-done), custom_call_target="tpu_custom_call" | custom-call | flops 1000000 | bytes 1000000 | tf_op jit(solution)/shard_map/activated/pallas_call | solution.py:280
  8.4 8.0 %all-to-all-start = ((bf16[32,120,128]{2,1,0:T(8,128)(2,1)}), bf16[32,120,128]{2,1,0:T(8,128)(2,1)S(1)}, u32[]{:S(2)}, u32[]{:S(2)}) async-start(bf16[32,120,128]{2,1,0:T(8,128)(2,1)} %bitcast.7), calls=%async_computation | async-start | bytes 1966080 | tf_op jit(solution)/shard_map/activated/all_to_all | solution.py:285
  16.5 31.7 %all_gather.3.weight_ref = bf16[256,1024]{1,0:T(8,128)(2,1)S(1)} all-gather(bf16[16,1024]{1,0:T(8,128)(2,1)S(1)} %get-tuple-element.20), channel_id=1, replica_groups=mesh['tm'=16,'y'=4,'core'=2,'width'=4] {'tm'}, dimensions={0}, use_global_device_ids=true | all-gather | bytes 557056 | tf_op jit(solution)/shard_map/activated/all_gather | solution.py:284
  48.2 0.0 all-to-all-done
  48.2 2.6 %conv.1 = (bf16[4,96,256]{2,1,0:T(8,128)(2,1)S(1)}, f32[96,256]{1,0:T(8,128)S(1)}) custom-call(s32[4]{0:T(128)S(1)} %pad_add_fusion.place_ref, bf16[4,8,120,128]{3,2,1,0:T(8,128)(2,1)S(1)} %bitcast.13, bf16[256,1024]{1,0:T(8,128)(2,1)S(1)} %all_gather.3.weight_ref), custom_call_target="tpu_custom_call" | custom-call | flops 700000000 | bytes 1000000 | tf_op jit(solution)/shard_map/conv/pallas_call | solution.py:287
  50.8 8.5 %all_to_all.15.part_ref = bf16[4,96,256]{2,1,0:T(8,128)(2,1)S(1)} all-to-all(bf16[4,96,256]{2,1,0:T(8,128)(2,1)S(1)} %get-tuple-element.21), channel_id=1, replica_groups=mesh['tm'=16,'y'=4,'core'=2,'width'=4] {'width'}, dimensions={0} | all-to-all | bytes 393216 | tf_op jit(solution)/shard_map/conv/all_to_all | solution.py:294
  59.3 1.0 %hidden.1 = bf16[16,96,256]{2,1,0:T(8,128)(2,1)} custom-call(bf16[4,96,256]{2,1,0:T(8,128)(2,1)S(1)} %all_to_all.15.part_ref, f32[96,256]{1,0:T(8,128)S(1)} %get-tuple-element.22.latent_ref), custom_call_target="tpu_custom_call" | custom-call | flops 1000000 | bytes 1000000 | tf_op jit(solution)/shard_map/hidden/pallas_call | solution.py:296
  60.3 0.0 copy-start.3
  60.3 0.0 copy-start.1
  60.3 0.0 copy-start.2
  60.3 4.8 %all-to-all-start.2 = ((bf16[16,96,256]{2,1,0:T(8,128)(2,1)}), bf16[16,96,256]{2,1,0:T(8,128)(2,1)S(1)}, u32[]{:S(2)}, u32[]{:S(2)}) async-start(bf16[16,96,256]{2,1,0:T(8,128)(2,1)} %hidden.1), calls=%async_computation.2 | async-start | bytes 1572864 | tf_op jit(solution)/shard_map/hidden/all_to_all | solution.py:297
  65.2 0.0 copy-done.3
  65.2 0.1 reshape.33.column_ref
  65.3 0.0 copy-done.1
  65.3 0.0 copy-done.2
  65.3 1.5 %attention.2 = (bf16[384,384]{1,0:T(8,128)(2,1)S(1)}, bf16[384,384]{1,0:T(8,128)(2,1)S(1)}) custom-call(bf16[384,1152]{1,0:T(8,128)(2,1)S(1)} %copy-done.1, bf16[384,384]{1,0:T(8,128)(2,1)S(1)} %copy-done.2, f32[1,384]{1,0:T(1,128)S(1)} %reshape.31.row_ref, f32[384,1]{1,0:T(8,128)S(1)} %reshape.33.column_ref), custom_call_target="tpu_custom_call" | custom-call | flops 600000000 | bytes 1000000 | tf_op jit(solution)/shard_map/attention/pallas_call | solution.py:300
  66.9 8.7 %all-to-all-done.2 = bf16[16,96,256]{2,1,0:T(8,128)(2,1)S(1)} async-done(((bf16[16,96,256]{2,1,0:T(8,128)(2,1)}), bf16[16,96,256]{2,1,0:T(8,128)(2,1)S(1)}, u32[]{:S(2)}, u32[]{:S(2)}) %all-to-all-start.2) | async-done | bytes 786464 | tf_op jit(solution)/shard_map/hidden/all_to_all | solution.py:297
  75.5 1.8 %attention.3 = (bf16[32,384]{1,0:T(8,128)(2,1)S(1)}, bf16[32,384]{1,0:T(8,128)(2,1)S(1)}) custom-call(s32[4]{0:T(128)S(1)} %pad_add_fusion.place_ref, bf16[4,384,256]{2,1,0:T(8,128)(2,1)S(1)} %bitcast.12, bf16[384,384]{1,0:T(8,128)(2,1)S(1)} %get-tuple-element.23.score_ref, bf16[384,384]{1,0:T(8,128)(2,1)S(1)} %get-tuple-element.24.update_ref), custom_call_target="tpu_custom_call" | custom-call | flops 200000000 | bytes 1000000 | tf_op jit(solution)/shard_map/attention/pallas_call | solution.py:303
  77.3 12.1 %collective-permute-start.1 = (bf16[32,384]{1,0:T(8,128)(2,1)S(1)}, bf16[32,384]{1,0:T(8,128)(2,1)S(1)}, u32[]{:S(2)}, u32[]{:S(2)}) collective-permute-start(bf16[32,384]{1,0:T(8,128)(2,1)S(1)} %get-tuple-element.26), channel_id=1, source_target_pairs={{0,4},{4,0},{1,5},{5,1},{2,6},{6,2},{3,7},{7,3},{8,12},{12,8},{9,1... | collective-permute-start | bytes 73736 | tf_op jit(solution)/shard_map/attention/ppermute | solution.py:306
  89.4 0.8 collective-permute-done.1
  90.2 0.6 maximum_select_fusion
  (1 shorter events, 0.0 us)
Async XLA Ops:
  0.0 7.2 %collective-permute-start = (bf16[64,384]{1,0:T(8,128)(2,1)}, bf16[64,384]{1,0:T(8,128)(2,1)S(1)}, u32[]{:S(2)}, u32[]{:S(2)}) collective-permute-start(bf16[64,384]{1,0:T(8,128)(2,1)} %bitcast.15), channel_id=1, source_target_pairs={{0,32},{32,64},{64,96},{96,128},{128,160},{160,192},{192,224},{224... | collective-permute-start | bytes 147464 | tf_op jit(solution)/shard_map/earlier_frames/ppermute | solution.py:265
  4.4 0.7 copy-start
  8.4 39.8 %all-to-all-start = ((bf16[32,120,128]{2,1,0:T(8,128)(2,1)}), bf16[32,120,128]{2,1,0:T(8,128)(2,1)S(1)}, u32[]{:S(2)}, u32[]{:S(2)}) async-start(bf16[32,120,128]{2,1,0:T(8,128)(2,1)} %bitcast.7), calls=%async_computation | async-start | bytes 1966080 | tf_op jit(solution)/shard_map/activated/all_to_all | solution.py:285
  60.3 4.8 %copy-start.3 = (f32[384]{0:T(512)S(1)}, f32[384]{0:T(512)}, u32[]{:S(2)}) copy-start(f32[384]{0:T(512)} %param.9) | copy-start | bytes 4612
  60.3 5.0 %copy-start.1 = (bf16[384,1152]{1,0:T(8,128)(2,1)S(1)}, bf16[384,1152]{1,0:T(8,128)(2,1)}, u32[]{:S(2)}) copy-start(bf16[384,1152]{1,0:T(8,128)(2,1)} %w_ref.1) | copy-start | bytes 2654212
  60.3 5.0 %copy-start.2 = (bf16[384,384]{1,0:T(8,128)(2,1)S(1)}, bf16[384,384]{1,0:T(8,128)(2,1)}, u32[]{:S(2)}) copy-start(bf16[384,384]{1,0:T(8,128)(2,1)} %w_out_ref.1) | copy-start | bytes 884740
  60.3 15.2 %all-to-all-start.2 = ((bf16[16,96,256]{2,1,0:T(8,128)(2,1)}), bf16[16,96,256]{2,1,0:T(8,128)(2,1)S(1)}, u32[]{:S(2)}, u32[]{:S(2)}) async-start(bf16[16,96,256]{2,1,0:T(8,128)(2,1)} %hidden.1), calls=%async_computation.2 | async-start | bytes 1572864 | tf_op jit(solution)/shard_map/hidden/all_to_all | solution.py:297
  77.3 12.9 %collective-permute-start.1 = (bf16[32,384]{1,0:T(8,128)(2,1)S(1)}, bf16[32,384]{1,0:T(8,128)(2,1)S(1)}, u32[]{:S(2)}, u32[]{:S(2)}) collective-permute-start(bf16[32,384]{1,0:T(8,128)(2,1)S(1)} %get-tuple-element.26), channel_id=1, source_target_pairs={{0,4},{4,0},{1,5},{5,1},{2,6},{6,2},{3,7},{7,3},{8,12},{12,8},{9,1... | collective-permute-start | bytes 73736 | tf_op jit(solution)/shard_map/attention/ppermute | solution.py:306

commit v7 on v6

v7 whole, which is shorter than its diff:
```python
import functools

import jax
import jax.numpy as jnp
from jax import lax
from jax.experimental import pallas as pl
from jax.experimental.pallas import tpu as pltpu
from jax.sharding import Mesh, PartitionSpec as P

F32 = jnp.float32
BF16 = jnp.bfloat16
TAPS = 27
GROUP = 24
SLOT = 96
BAND = 896
PLANE = ("width", "y")
VMEM = pl.BlockSpec(memory_space=pltpu.VMEM)
SMEM = pl.BlockSpec(memory_space=pltpu.SMEM)
LIMIT = 12 * 1024 * 1024


def call(body, out, specs, flops=1_000_000, moved=1_000_000, scratch=()):
    many = isinstance(out, (tuple, list))
    return pl.pallas_call(
        body,
        out_shape=out,
        in_specs=specs,
        out_specs=[VMEM] * len(out) if many else VMEM,
        scratch_shapes=list(scratch),
        compiler_params=pltpu.CompilerParams(vmem_limit_bytes=LIMIT),
        cost_estimate=pl.CostEstimate(flops=flops, bytes_accessed=moved, transcendentals=0),
    )


def one_hot(shape, column_of):
    row = lax.broadcasted_iota(jnp.int32, (shape[0], 1), 0)
    col = lax.broadcasted_iota(jnp.int32, shape, 1)
    return (col == column_of(row)).astype(F32).astype(BF16)


def channel_of(place):
    return place % SLOT // 6 * GROUP + place // SLOT * 6 + place % 6


def activated(values, gain):
    scaled = rms_scale(values.astype(F32), gain)
    return scaled / (1.0 + jnp.exp(-scaled))


def weight_body(place_ref, weight_ref, piece_ref):
    start = place_ref[3] * SLOT
    pick = one_hot((384, 128), lambda row: jnp.where(row - start < SLOT, row - start, -1))
    rows = jnp.concatenate([weight_ref[tap] for tap in range(TAPS)], axis=0)
    picked = jnp.dot(rows, pick, preferred_element_type=F32)
    upper = place_ref[1] // 2
    picked = jnp.where(upper == 0, picked, pltpu.roll(picked, TAPS * GROUP - 12, 0))
    picked = jnp.where(place_ref[1] % 2 == 0, picked, pltpu.roll(picked, TAPS * GROUP - 6, 0))
    lane = lax.broadcasted_iota(jnp.int32, (8, 128), 1)
    kept = lax.broadcasted_iota(jnp.int32, (8, 128), 0) < 6
    tiles = [jnp.zeros((8, 128), F32) for _ in range(3 * BAND // 128)]
    for row_tap in range(3):
        for slot in range(9):
            tap = slot // 3 * 9 + row_tap * 3 + slot % 3
            value = jnp.where(kept, picked[tap * GROUP : tap * GROUP + 8], 0.0)
            tile, offset = divmod(row_tap * BAND + slot * SLOT, 128)
            value = pltpu.roll(value, offset, 1) if offset else value
            if offset + SLOT > 128:
                tiles[tile] += jnp.where(lane >= offset, value, 0.0)
                tiles[tile + 1] += jnp.where(lane < offset, value, 0.0)
            else:
                tiles[tile] += value
    main, spare = [], [[], []]
    for tile in range(BAND // 128):
        stack = jnp.concatenate([tiles[band * 7 + tile][:6] for band in range(3)], axis=0)
        main.append(stack[:16])
        spare[0].append(stack[16:17])
        spare[1].append(stack[17:])
    spare = jnp.concatenate(spare[0] + spare[1] + [jnp.zeros((2, 128), F32)], axis=0)
    piece_ref[...] = jnp.concatenate(main + [spare], axis=1).astype(BF16)


def activated(values, gain):
    scaled = rms_scale(values.astype(F32), gain)
    return scaled / (1.0 + jnp.exp(-scaled))


def by_frame(ref):
    return jnp.concatenate([ref[0:32], ref[64:96], ref[32:64], ref[96:128]], axis=0)


def block_body(before_ref, now_ref, gain_ref, out_ref):
    now = by_frame(now_ref)
    both = activated(jnp.concatenate([by_frame(before_ref), now], axis=0), gain_ref[...]).T.astype(BF16)
    latent = lax.dot_general(
        one_hot((384, 384), channel_of), now, (((1,), (1,)), ((), ())), preferred_element_type=F32
    )
    blank = jnp.zeros((GROUP, 128), BF16)
    for width in range(4):
        for row in range(4):
            start = row * SLOT + width * GROUP
            out_ref[width, row, :SLOT, :] = both[width * SLOT : width * SLOT + SLOT]
            out_ref[width, row, SLOT:, :128] = latent[start : start + GROUP].astype(BF16)
            out_ref[width, row, SLOT:, 128:] = blank


def grid_place(odd, row):
    target = row // 16 % 4 * 64 + row // 128 * 16 + row % 16
    return jnp.where(row // 64 % 2 == odd, target, -1)


def patch_body(place_ref, mine_ref, handed_ref, flat_ref, latent_ref):
    core = place_ref[2]
    lane = lax.broadcasted_iota(jnp.int32, (4 * SLOT, 256), 1) % 64
    blocks = [[None] * 4 for _ in range(4)]
    for width in range(4):
        for row in range(4):
            blocks[row][width] = jnp.where(core == 0, mine_ref[width, row], handed_ref[width, row])
    places = [one_hot((512, 256), functools.partial(grid_place, odd)) for odd in range(2)]
    frames = []
    for pair in range(2):
        cut = slice(pair * 128, pair * 128 + 128)
        rows = [
            jnp.concatenate([blocks[row][width][:SLOT, cut] for width in range(4)], axis=1) for row in range(4)
        ]
        rows = jnp.concatenate(rows, axis=0)
        frames += [jnp.dot(rows, place, preferred_element_type=F32) for place in places]
    for time_tap in range(3):
        still = jnp.where(core == 0, frames[time_tap], frames[time_tap + 1])
        left = jnp.where(lane == 0, 0.0, pltpu.roll(still, 1, 1))
        right = jnp.where(lane == 63, 0.0, pltpu.roll(still, 255, 1))
        for col_tap, base in enumerate((left, still, right)):
            slot = (time_tap * 3 + col_tap) * SLOT
            base = base.astype(BF16)
            for row in range(4):
                flat_ref[slot : slot + SLOT, row * 256 : row * 256 + 256] = base[row * SLOT : row * SLOT + SLOT]
    flat_ref[9 * SLOT :, :] = jnp.zeros((BAND - 9 * SLOT, 1024), BF16)
    place = jnp.where(core == 0, places[0], places[1])
    for row in range(4):
        part = jnp.concatenate([blocks[row][width][SLOT:, :128] for width in range(4)], axis=1)
        latent_ref[:, row * 256 : row * 256 + 256] = jnp.dot(part, place, preferred_element_type=F32)


def main_place(row):
    part = row // SLOT * 6 + row % 6
    return jnp.where(part < 16, row % SLOT // 6 * 16 + part, -1)


def spare_place(tile, row):
    part = row % 6 - 4
    return jnp.where(part >= 0, row // 6 * 16 + part * 7 + tile, -1)


def conv_body(place_ref, flat_ref, latent_ref, mine_ref, handed_ref, out_ref):
    gathered = jnp.where(place_ref[2] == 1, mine_ref[...], handed_ref[...])
    main = jnp.dot(one_hot((3 * SLOT, 256), main_place), gathered[:, :BAND], preferred_element_type=F32)
    spare = [
        jnp.dot(
            one_hot((SLOT, 256), functools.partial(spare_place, tile)),
            gathered[:, BAND:],
            preferred_element_type=F32,
        )
        for tile in range(BAND // 128)
    ]
    last = main[2 * SLOT :] + jnp.concatenate(spare, axis=1)
    weight = jnp.concatenate([main[: 2 * SLOT], last], axis=0).astype(BF16)
    whole = jnp.dot(weight, flat_ref[...], preferred_element_type=F32)
    lane = lax.broadcasted_iota(jnp.int32, (SLOT, 1024), 1)
    total = whole[SLOT : 2 * SLOT]
    total += jnp.where(lane < 64, 0.0, pltpu.roll(whole[:SLOT], 64, 1))
    total += jnp.where(lane < 960, pltpu.roll(whole[2 * SLOT :], 960, 1), 0.0)
    owner = lax.broadcasted_iota(jnp.int32, (SLOT, 1024), 0) // GROUP
    total += jnp.where(owner == place_ref[3], jnp.concatenate([latent_ref[...]] * 4, axis=0), 0.0)
    pieces = [total[:, part * 256 : part * 256 + 256].T for part in range(4)]
    for width in range(4):
        rows = [
            pieces[row // 4][row % 4 * 64 + width * 16 : row % 4 * 64 + width * 16 + 16] for row in range(16)
        ]
        out_ref[width] = jnp.concatenate(rows, axis=0).T.astype(BF16)


def hidden_body(part_ref, out_ref):
    summed = part_ref[0].astype(F32)
    for source in range(1, 4):
        summed += part_ref[source].astype(F32)
    hidden = summed.astype(BF16)
    for target in range(16):
        out_ref[target] = hidden


def fold_body(w_ref, w_out_ref, row_ref, column_ref, score_ref, update_ref):
    order = one_hot((384, 384), channel_of)
    gain = column_ref[...]
    score = lax.dot_general(
        w_ref[:, :384], w_ref[:, 384:768], (((1,), (1,)), ((), ())), preferred_element_type=F32
    )
    score = (score * (gain * (1.0 / 384.0**0.5)) * row_ref[...]).astype(BF16)
    score = jnp.dot(order, score, preferred_element_type=F32).astype(BF16)
    score = lax.dot_general(score, order, (((1,), (1,)), ((), ())), preferred_element_type=F32)
    score_ref[...] = score.astype(BF16)
    update = jnp.dot(w_ref[:, 768:], w_out_ref[...], preferred_element_type=F32) * gain
    update_ref[...] = jnp.dot(order, update.astype(BF16), preferred_element_type=F32).astype(BF16)


def attend_body(place_ref, block_ref, score_ref, update_ref, keep_ref, send_ref):
    own = block_ref[place_ref[3]]
    own = jnp.where(place_ref[1] < 2, own[:, :128], own[:, 128:]).astype(F32).T
    own = jnp.where(place_ref[1] % 2 == 0, own[:64], own[64:])
    own_scale = lax.rsqrt(jnp.mean(own * own, axis=-1, keepdims=True) + 1e-06)
    own = own.astype(BF16)
    query = jnp.dot(own, score_ref[...], preferred_element_type=F32)
    query = (query * own_scale).astype(BF16)
    hidden = jnp.dot(own, one_hot((384, 384), channel_of), preferred_element_type=F32)
    scales, scores = [], []
    for width in range(4):
        cells = block_ref[width]
        values = cells.astype(F32)
        scale = lax.rsqrt(jnp.mean(values * values, axis=0, keepdims=True) + 1e-06)
        scales.append(scale)
        scores.append(jnp.dot(query, cells, preferred_element_type=F32) * scale)
    peak = functools.reduce(jnp.maximum, [jnp.max(part, axis=-1, keepdims=True) for part in scores])
    total = jnp.zeros((64, 1), F32)
    mixed = jnp.zeros((64, 384), F32)
    for width in range(4):
        powers = jnp.exp(scores[width] - peak)
        total += jnp.sum(powers, axis=-1, keepdims=True)
        powers = (powers * scales[width]).astype(BF16)
        mixed += lax.dot_general(
            powers, block_ref[width], (((1,), (1,)), ((), ())), preferred_element_type=F32
        )
    mixed = (mixed / total).astype(BF16)
    decoded = (hidden + jnp.dot(mixed, update_ref[...], preferred_element_type=F32)).astype(BF16)
    first = place_ref[2] == 0
    keep_ref[...] = jnp.where(first, decoded[:32], decoded[32:])
    send_ref[...] = jnp.where(first, decoded[32:], decoded[:32])


def rms_scale(values, gain):
    mean_sq = jnp.mean(values * values, axis=-1, keepdims=True)
    return values * lax.rsqrt(mean_sq + 1e-06) * gain


def local(latent, norm_gain, conv_weight, attn_gain, w_qkv, w_out):
    channels = 384
    core = lax.axis_index("core")
    place = [lax.axis_index("tm"), lax.axis_index("y"), core, lax.axis_index("width")]
    place = jnp.stack(place).astype(jnp.int32)
    swap = [(0, 1), (1, 0)]
    shape = jax.ShapeDtypeStruct
    cells = latent.reshape(64, channels)
    weight_shape, block_shape = (256, 1024), (16, SLOT + GROUP, 256)

    def gather_weights(cells, lower, gain, turned):
        piece = call(weight_body, shape((16, 1024), BF16), [SMEM, VMEM])(place, turned)
        weight = lax.all_gather(piece, "tm", axis=0, tiled=True)
        return weight, jnp.zeros(block_shape, BF16)

    def exchange_cells(cells, lower, gain, turned):
        now = jnp.concatenate([cells, lower], axis=0)
        before = lax.ppermute(now, ("tm", "core"), [(2 * i, 2 * i + 2) for i in range(15)])
        blocks = call(block_body, shape((4, 4, SLOT + GROUP, 256), BF16), [VMEM] * 3)(before, now, gain)
        return jnp.zeros(weight_shape, BF16), lax.all_to_all(blocks.reshape(block_shape), PLANE, 0, 0)

    with jax.named_scope("weights_and_cells"):
        lower = lax.ppermute(cells, "core", [(1, 0)])
        turned = jnp.transpose(conv_weight.reshape(TAPS, channels, GROUP), (0, 2, 1))
        weight, blocks = lax.cond(
            core == 1, gather_weights, exchange_cells, cells, lower, norm_gain.reshape(1, channels), turned
        )
    with jax.named_scope("patches"):
        handed_blocks = lax.ppermute(blocks, "core", [(0, 1)])
        handed_weight = lax.ppermute(weight, "core", [(1, 0)])
        grouped = (4, 4, SLOT + GROUP, 256)
        flat, own = call(
            patch_body, [shape((BAND, 1024), BF16), shape((GROUP, 1024), F32)], [SMEM] + [VMEM] * 2
        )(place, blocks.reshape(grouped), handed_blocks.reshape(grouped))
    with jax.named_scope("conv"):
        parts = call(conv_body, shape((4, SLOT, 256), BF16), [SMEM] + [VMEM] * 4, 700_000_000)(
            place, flat, own, weight, handed_weight
        )
        parts = lax.all_to_all(parts, "width", 0, 0)
    with jax.named_scope("hidden"):
        hidden = call(hidden_body, shape((16, SLOT, 256), BF16), [VMEM])(parts)
        hidden = lax.all_to_all(hidden, PLANE, 0, 0)
    with jax.named_scope("attention"):
        square, half = shape((channels, channels), BF16), shape((32, channels), BF16)
        score, update = call(fold_body, [square, square], [VMEM] * 4, 600_000_000)(
            w_qkv, w_out, attn_gain.reshape(1, channels), attn_gain.reshape(channels, 1)
        )
        keep, send = call(attend_body, [half, half], [SMEM] + [VMEM] * 3, 200_000_000)(
            place, hidden.reshape(4, channels, 256), score, update
        )
        got = lax.ppermute(send, "core", swap)
        out = jnp.where(core == 0, jnp.concatenate([keep, got]), jnp.concatenate([got, keep]))
    return out.reshape(latent.shape)


def solution(mesh):
    devices = mesh.devices.reshape(16, 4, 2, 4)
    fine = Mesh(devices, ("tm", "y", "core", "width"))
    cells = P("tm", ("y", "core"), "width", None)
    in_specs = (cells, P(), P(None, None, None, None, "tm"), P(), P(), P())
    return jax.shard_map(local, mesh=fine, in_specs=in_specs, out_specs=cells, check_vma=False)
```

time: 91.3 us -> 82.1 us (0.90)
  starting transfers between devices: 29.3 us -> 23.4 us
  blocking collectives: 40.2 us -> 35.6 us
  waiting for transfers between devices: 9.49 us -> 12.4 us
  Pallas kernels: 10.3 us -> 9.18 us
    ppermute x1 -> x3, starting transfers between devices: 4.36 us -> 13.2 us  [the longest x1 8.77 us: local(): lower = lax.ppermute(cells, 'core', [(1, 0)])]
    all_to_all x1 -> x0, starting transfers between devices: 8.04 us -> none  [local(): lax.all_to_all(blocks.reshape(32, SLOT + GROUP, 128), ('width', 'y', 'cor...]
    ppermute x1, starting transfers between devices: 12.1 us -> 5.03 us  [local(): got = lax.ppermute(send, 'core', swap)]
    all_gather x1, blocking collectives: 31.7 us -> 26.2 us  [gather_weights(): weight = lax.all_gather(piece, 'tm', axis=0, tiled=True)]
    all_to_all x1, waiting for transfers between devices: 8.66 us -> 10.4 us  [local(): hidden = lax.all_to_all(hidden, PLANE, 0, 0)]
    pallas_call x4, Pallas kernels: 6.99 us -> 5.84 us  [the longest x1 2.04 us: local(): call(conv_body, shape((4, SLOT, 256), BF16), [SMEM] + [VMEM] * 4, 700000000)]
    ppermute x1 -> x3, waiting for transfers between devices: 0.01 us -> 1.11 us  [the longest x1 0.99 us: local(): lower = lax.ppermute(cells, 'core', [(1, 0)])]
  transfers between devices with their start and end apart: 4 -> 5, of which waited for: 2 -> 4; matrix products, arithmetic and copies ran while one was open for 0% -> 0% of each run, Pallas kernels for 4% -> 4%
where the time goes in v7:
time: 82.1 us; the launch traced here: 81.6 us
  blocking collectives  35.6 us (43%)
  starting transfers between devices  23.4 us (29%)
  waiting for transfers between devices  12.4 us (15%)
  Pallas kernels  9.18 us (11%)
    all_gather x1, blocking collectives, gather_weights(): weight = lax.all_gather(piece, 'tm', axis=0, tiled=True)  26.2 us
    all_to_all x1, waiting for transfers between devices, local(): hidden = lax.all_to_all(hidden, PLANE, 0, 0)  10.4 us
    all_to_all x1, blocking collectives, local(): parts = lax.all_to_all(parts, 'width', 0, 0)  9.38 us
    ppermute x1, starting transfers between devices, local(): lower = lax.ppermute(cells, 'core', [(1, 0)])  8.77 us
    all_to_all x1, starting transfers between devices, local(): hidden = lax.all_to_all(hidden, PLANE, 0, 0)  5.18 us
    ppermute x1, starting transfers between devices, local(): got = lax.ppermute(send, 'core', swap)  5.03 us
    ppermute x1, starting transfers between devices, local(): handed_weight = lax.ppermute(weight, 'core', [(1, 0)])  3.12 us
    pallas_call x1, Pallas kernels, local(): call(conv_body, shape((4, SLOT, 256), BF16), [SMEM] + [VMEM] * 4, 700000000)  2.04 us
  transfers between devices with their start and end apart: 5, of which 4 were waited for; matrix products, arithmetic and copies ran while one was open for 0% of the time, Pallas kernels for 4%

profile of v7, /device:TPU:1, one launch (start us, length us, event | category | flops | bytes accessed | tf_op | source)
XLA Modules:
  0.0 81.6 jit_solution(10702465070398650424)
XLA Ops:
  0.0 8.8 %collective-permute-start.1 = (bf16[64,384]{1,0:T(8,128)(2,1)}, bf16[64,384]{1,0:T(8,128)(2,1)S(1)}, u32[]{:S(2)}, u32[]{:S(2)}) collective-permute-start(bf16[64,384]{1,0:T(8,128)(2,1)} %bitcast.18), channel_id=1, source_target_pairs={{4,0},{5,1},{6,2},{7,3},{12,8},{13,9},{14,10},{15,11},{20,16},{21,... | collective-permute-start | bytes 147464 | tf_op jit(solution)/shard_map/weights_and_cells/ppermute | solution.py:264
  8.8 0.1 pad_add_fusion.place_ref
  8.9 1.0 %collective-permute-done.1 = bf16[64,384]{1,0:T(8,128)(2,1)S(1)} collective-permute-done((bf16[64,384]{1,0:T(8,128)(2,1)}, bf16[64,384]{1,0:T(8,128)(2,1)S(1)}, u32[]{:S(2)}, u32[]{:S(2)}) %collective-permute-start.1) | collective-permute-done | bytes 49184 | tf_op jit(solution)/shard_map/weights_and_cells/ppermute | solution.py:264
  9.9 27.8 %conditional.1 = (bf16[256,1024]{1,0:T(8,128)(2,1)S(1)}, bf16[16,120,256]{2,1,0:T(8,128)(2,1)S(1)}, bf16[4,4,120,256]{3,2,1,0:T(8,128)(2,1)S(1)}) conditional(s32[]{:T(128)} %convert_element_type.3, (bf16[64,384]{1,0:T(8,128)(2,1)}, bf16[64,384]{1,0:T(8,128)(2,1)S(1)}, f32[384]{0:T(512)}) %tuple.20, (s32[4]{0:T(128)S(1)}, ...), branch_computations={%region_0.0_spmd, %region_1.0_spmd} | conditional | flops 1000000 | bytes 6049410 | solution.py:266
  9.9 1.5 %branch_1_fun.1 = bf16[16,1024]{1,0:T(8,128)(2,1)S(1)} custom-call(s32[4]{0:T(128)S(1)} %get-tuple-element.20.place_ref, bf16[27,24,384]{2,1,0:T(8,128)(2,1)} %get-tuple-element.21.weight_ref), custom_call_target="tpu_custom_call" | custom-call | flops 1000000 | bytes 1000000 | tf_op jit(solution)/shard_map/weights_and_cells/cond/branch_1_fun/pallas_call | solution.py:253
  11.3 26.2 %all_gather.2 = bf16[256,1024]{1,0:T(8,128)(2,1)S(1)} all-gather(bf16[16,1024]{1,0:T(8,128)(2,1)S(1)} %branch_1_fun.1), channel_id=1, replica_groups=mesh['tm'=16,'y'=4,'core'=2,'width'=4] {'tm'}, dimensions={0}, use_global_device_ids=true | all-gather | bytes 557056 | tf_op jit(solution)/shard_map/weights_and_cells/cond/branch_1_fun/all_gather | solution.py:254
  37.5 0.1 broadcast.10
  37.6 0.1 reshape.28
  37.6 1.3 %collective-permute-start.2 = (bf16[16,120,256]{2,1,0:T(8,128)(2,1)S(1)}, bf16[16,120,256]{2,1,0:T(8,128)(2,1)S(1)}, u32[]{:S(2)}, u32[]{:S(2)}) collective-permute-start(bf16[16,120,256]{2,1,0:T(8,128)(2,1)S(1)} %get-tuple-element.32), channel_id=1, source_target_pairs={{0,4},{1,5},{2,6},{3,7},{8,12},{9,13},{10,14},{11,15},{16,20},{17,... | collective-permute-start | bytes 2949128 | tf_op jit(solution)/shard_map/patches/ppermute | solution.py:270
  38.9 3.1 %collective-permute-start.3 = (bf16[256,1024]{1,0:T(8,128)(2,1)S(1)}, bf16[256,1024]{1,0:T(8,128)(2,1)S(1)}, u32[]{:S(2)}, u32[]{:S(2)}) collective-permute-start(bf16[256,1024]{1,0:T(8,128)(2,1)S(1)} %get-tuple-element.35.mine_ref), channel_id=1, source_target_pairs={{4,0},{5,1},{6,2},{7,3},{12,8},{13,9},{14,10},{15,11},{20,16},{21,... | collective-permute-start | bytes 1572872 | tf_op jit(solution)/shard_map/patches/ppermute | solution.py:271
  42.1 0.0 collective-permute-done.2
  42.1 1.4 %patches.1 = (bf16[896,1024]{1,0:T(8,128)(2,1)S(1)}, f32[24,1024]{1,0:T(8,128)S(1)}) custom-call(s32[4]{0:T(128)S(1)} %pad_add_fusion.place_ref, bf16[4,4,120,256]{3,2,1,0:T(8,128)(2,1)S(1)} %get-tuple-element.31.mine_ref, bf16[4,4,120,256]{3,2,1,0:T(8,128)(2,1)S(1)} %bitcast.15), custom_call_target="tpu_custom_call" | custom-call | flops 1000000 | bytes 1000000 | tf_op jit(solution)/shard_map/patches/pallas_call | solution.py:273
  43.5 0.1 collective-permute-done.3.handed_ref
  43.6 2.0 %conv.1 = bf16[4,96,256]{2,1,0:T(8,128)(2,1)S(1)} custom-call(s32[4]{0:T(128)S(1)} %pad_add_fusion.place_ref, bf16[896,1024]{1,0:T(8,128)(2,1)S(1)} %get-tuple-element.33.flat_ref, f32[24,1024]{1,0:T(8,128)S(1)} %get-tuple-element.34.latent_ref, bf16[256,1024]{1,0:T(8,128)(2,1)S(1)} %get-tuple-element.35.mine_ref, ...), custom_call_target="tpu_custom_call" | custom-call | flops 700000000 | bytes 1000000 | tf_op jit(solution)/shard_map/conv/pallas_call | solution.py:277
  45.6 0.0 copy-start.2
  45.6 0.0 copy-start
  45.6 0.0 copy-start.1
  45.6 9.4 %all_to_all.15.part_ref = bf16[4,96,256]{2,1,0:T(8,128)(2,1)S(1)} all-to-all(bf16[4,96,256]{2,1,0:T(8,128)(2,1)S(1)} %conv.1), channel_id=1, replica_groups=mesh['tm'=16,'y'=4,'core'=2,'width'=4] {'width'}, dimensions={0} | all-to-all | bytes 393216 | tf_op jit(solution)/shard_map/conv/all_to_all | solution.py:280
  55.0 1.0 %hidden.1 = bf16[16,96,256]{2,1,0:T(8,128)(2,1)} custom-call(bf16[4,96,256]{2,1,0:T(8,128)(2,1)S(1)} %all_to_all.15.part_ref), custom_call_target="tpu_custom_call" | custom-call | flops 1000000 | bytes 1000000 | tf_op jit(solution)/shard_map/hidden/pallas_call | solution.py:282
  56.0 5.2 %all-to-all-start.2 = ((bf16[16,96,256]{2,1,0:T(8,128)(2,1)}), bf16[16,96,256]{2,1,0:T(8,128)(2,1)S(1)}, u32[]{:S(2)}, u32[]{:S(2)}) async-start(bf16[16,96,256]{2,1,0:T(8,128)(2,1)} %hidden.1), calls=%async_computation.2 | async-start | bytes 1572864 | tf_op jit(solution)/shard_map/hidden/all_to_all | solution.py:283
  61.2 0.0 copy-done.2
  61.2 0.1 reshape.41.column_ref
  61.3 0.0 copy-done
  61.3 0.0 copy-done.1
  61.4 1.5 %attention.2 = (bf16[384,384]{1,0:T(8,128)(2,1)S(1)}, bf16[384,384]{1,0:T(8,128)(2,1)S(1)}) custom-call(bf16[384,1152]{1,0:T(8,128)(2,1)S(1)} %copy-done, bf16[384,384]{1,0:T(8,128)(2,1)S(1)} %copy-done.1, f32[1,384]{1,0:T(1,128)S(1)} %reshape.39.row_ref, f32[384,1]{1,0:T(8,128)S(1)} %reshape.41.column_ref), custom_call_target="tpu_custom_call" | custom-call | flops 600000000 | bytes 1000000 | tf_op jit(solution)/shard_map/attention/pallas_call | solution.py:286
  62.9 10.4 %all-to-all-done.2 = bf16[16,96,256]{2,1,0:T(8,128)(2,1)S(1)} async-done(((bf16[16,96,256]{2,1,0:T(8,128)(2,1)}), bf16[16,96,256]{2,1,0:T(8,128)(2,1)S(1)}, u32[]{:S(2)}, u32[]{:S(2)}) %all-to-all-start.2) | async-done | bytes 786464 | tf_op jit(solution)/shard_map/hidden/all_to_all | solution.py:283
  73.3 1.8 %attention.3 = (bf16[32,384]{1,0:T(8,128)(2,1)S(1)}, bf16[32,384]{1,0:T(8,128)(2,1)S(1)}) custom-call(s32[4]{0:T(128)S(1)} %pad_add_fusion.place_ref, bf16[4,384,256]{2,1,0:T(8,128)(2,1)S(1)} %bitcast.14, bf16[384,384]{1,0:T(8,128)(2,1)S(1)} %get-tuple-element.36.score_ref, bf16[384,384]{1,0:T(8,128)(2,1)S(1)} %get-tuple-element.37.update_ref), custom_call_target="tpu_custom_call" | custom-call | flops 200000000 | bytes 1000000 | tf_op jit(solution)/shard_map/attention/pallas_call | solution.py:289
  75.1 5.0 %collective-permute-start.4 = (bf16[32,384]{1,0:T(8,128)(2,1)S(1)}, bf16[32,384]{1,0:T(8,128)(2,1)S(1)}, u32[]{:S(2)}, u32[]{:S(2)}) collective-permute-start(bf16[32,384]{1,0:T(8,128)(2,1)S(1)} %get-tuple-element.39), channel_id=1, source_target_pairs={{0,4},{4,0},{1,5},{5,1},{2,6},{6,2},{3,7},{7,3},{8,12},{12,8},{9,1... | collective-permute-start | bytes 73736 | tf_op jit(solution)/shard_map/attention/ppermute | solution.py:292
  80.2 0.8 %collective-permute-done.4 = bf16[32,384]{1,0:T(8,128)(2,1)S(1)} collective-permute-done((bf16[32,384]{1,0:T(8,128)(2,1)S(1)}, bf16[32,384]{1,0:T(8,128)(2,1)S(1)}, u32[]{:S(2)}, u32[]{:S(2)}) %collective-permute-start.4) | collective-permute-done | bytes 24608 | tf_op jit(solution)/shard_map/attention/ppermute | solution.py:292
  81.0 0.6 maximum_select_fusion
  (1 shorter events, 0.0 us)
Async XLA Ops:
  0.0 9.9 %collective-permute-start.1 = (bf16[64,384]{1,0:T(8,128)(2,1)}, bf16[64,384]{1,0:T(8,128)(2,1)S(1)}, u32[]{:S(2)}, u32[]{:S(2)}) collective-permute-start(bf16[64,384]{1,0:T(8,128)(2,1)} %bitcast.18), channel_id=1, source_target_pairs={{4,0},{5,1},{6,2},{7,3},{12,8},{13,9},{14,10},{15,11},{20,16},{21,... | collective-permute-start | bytes 147464 | tf_op jit(solution)/shard_map/weights_and_cells/ppermute | solution.py:264
  37.6 4.5 %collective-permute-start.2 = (bf16[16,120,256]{2,1,0:T(8,128)(2,1)S(1)}, bf16[16,120,256]{2,1,0:T(8,128)(2,1)S(1)}, u32[]{:S(2)}, u32[]{:S(2)}) collective-permute-start(bf16[16,120,256]{2,1,0:T(8,128)(2,1)S(1)} %get-tuple-element.32), channel_id=1, source_target_pairs={{0,4},{1,5},{2,6},{3,7},{8,12},{9,13},{10,14},{11,15},{16,20},{17,... | collective-permute-start | bytes 2949128 | tf_op jit(solution)/shard_map/patches/ppermute | solution.py:270
  38.9 4.6 %collective-permute-start.3 = (bf16[256,1024]{1,0:T(8,128)(2,1)S(1)}, bf16[256,1024]{1,0:T(8,128)(2,1)S(1)}, u32[]{:S(2)}, u32[]{:S(2)}) collective-permute-start(bf16[256,1024]{1,0:T(8,128)(2,1)S(1)} %get-tuple-element.35.mine_ref), channel_id=1, source_target_pairs={{4,0},{5,1},{6,2},{7,3},{12,8},{13,9},{14,10},{15,11},{20,16},{21,... | collective-permute-start | bytes 1572872 | tf_op jit(solution)/shard_map/patches/ppermute | solution.py:271
  45.6 15.6 %copy-start.2 = (f32[384]{0:T(512)S(1)}, f32[384]{0:T(512)}, u32[]{:S(2)}) copy-start(f32[384]{0:T(512)} %param.11) | copy-start | bytes 4612
  45.6 15.7 %copy-start = (bf16[384,1152]{1,0:T(8,128)(2,1)S(1)}, bf16[384,1152]{1,0:T(8,128)(2,1)}, u32[]{:S(2)}) copy-start(bf16[384,1152]{1,0:T(8,128)(2,1)} %w_ref.1) | copy-start | bytes 2654212
  45.6 15.7 %copy-start.1 = (bf16[384,384]{1,0:T(8,128)(2,1)S(1)}, bf16[384,384]{1,0:T(8,128)(2,1)}, u32[]{:S(2)}) copy-start(bf16[384,384]{1,0:T(8,128)(2,1)} %w_out_ref.1) | copy-start | bytes 884740
  56.0 17.3 %all-to-all-start.2 = ((bf16[16,96,256]{2,1,0:T(8,128)(2,1)}), bf16[16,96,256]{2,1,0:T(8,128)(2,1)S(1)}, u32[]{:S(2)}, u32[]{:S(2)}) async-start(bf16[16,96,256]{2,1,0:T(8,128)(2,1)} %hidden.1), calls=%async_computation.2 | async-start | bytes 1572864 | tf_op jit(solution)/shard_map/hidden/all_to_all | solution.py:283
  75.1 5.9 %collective-permute-start.4 = (bf16[32,384]{1,0:T(8,128)(2,1)S(1)}, bf16[32,384]{1,0:T(8,128)(2,1)S(1)}, u32[]{:S(2)}, u32[]{:S(2)}) collective-permute-start(bf16[32,384]{1,0:T(8,128)(2,1)S(1)} %get-tuple-element.39), channel_id=1, source_target_pairs={{0,4},{4,0},{1,5},{5,1},{2,6},{6,2},{3,7},{7,3},{8,12},{12,8},{9,1... | collective-permute-start | bytes 73736 | tf_op jit(solution)/shard_map/attention/ppermute | solution.py:292

commit v8 on v7

--- a/solution.py
+++ b/solution.py
@@ -187,8 +187,9 @@
         out_ref[target] = hidden
 
 
-def fold_body(w_ref, w_out_ref, row_ref, column_ref, score_ref, update_ref):
+def fold_body(w_ref, w_out_ref, row_ref, column_ref, score_ref, update_ref, order_ref):
     order = one_hot((384, 384), channel_of)
+    order_ref[...] = order
     gain = column_ref[...]
     score = lax.dot_general(
         w_ref[:, :384], w_ref[:, 384:768], (((1,), (1,)), ((), ())), preferred_element_type=F32
@@ -201,7 +202,7 @@
     update_ref[...] = jnp.dot(order, update.astype(BF16), preferred_element_type=F32).astype(BF16)
 
 
-def attend_body(place_ref, block_ref, score_ref, update_ref, keep_ref, send_ref):
+def attend_body(place_ref, block_ref, score_ref, update_ref, order_ref, keep_ref, send_ref):
     own = block_ref[place_ref[3]]
     own = jnp.where(place_ref[1] < 2, own[:, :128], own[:, 128:]).astype(F32).T
     own = jnp.where(place_ref[1] % 2 == 0, own[:64], own[64:])
@@ -209,7 +210,7 @@
     own = own.astype(BF16)
     query = jnp.dot(own, score_ref[...], preferred_element_type=F32)
     query = (query * own_scale).astype(BF16)
-    hidden = jnp.dot(own, one_hot((384, 384), channel_of), preferred_element_type=F32)
+    hidden = jnp.dot(own, order_ref[...], preferred_element_type=F32)
     scales, scores = [], []
     for width in range(4):
         cells = block_ref[width]
@@ -249,12 +250,11 @@
     cells = latent.reshape(64, channels)
     weight_shape, block_shape = (256, 1024), (16, SLOT + GROUP, 256)
 
-    def gather_weights(cells, lower, gain, turned):
-        piece = call(weight_body, shape((16, 1024), BF16), [SMEM, VMEM])(place, turned)
+    def gather_weights(cells, lower, gain, piece):
         weight = lax.all_gather(piece, "tm", axis=0, tiled=True)
         return weight, jnp.zeros(block_shape, BF16)
 
-    def exchange_cells(cells, lower, gain, turned):
+    def exchange_cells(cells, lower, gain, piece):
         now = jnp.concatenate([cells, lower], axis=0)
         before = lax.ppermute(now, ("tm", "core"), [(2 * i, 2 * i + 2) for i in range(15)])
         blocks = call(block_body, shape((4, 4, SLOT + GROUP, 256), BF16), [VMEM] * 3)(before, now, gain)
@@ -263,8 +263,9 @@
     with jax.named_scope("weights_and_cells"):
         lower = lax.ppermute(cells, "core", [(1, 0)])
         turned = jnp.transpose(conv_weight.reshape(TAPS, channels, GROUP), (0, 2, 1))
+        piece = call(weight_body, shape((16, 1024), BF16), [SMEM, VMEM])(place, turned)
         weight, blocks = lax.cond(
-            core == 1, gather_weights, exchange_cells, cells, lower, norm_gain.reshape(1, channels), turned
+            core == 1, gather_weights, exchange_cells, cells, lower, norm_gain.reshape(1, channels), piece
         )
     with jax.named_scope("patches"):
         handed_blocks = lax.ppermute(blocks, "core", [(0, 1)])
@@ -283,11 +284,11 @@
         hidden = lax.all_to_all(hidden, PLANE, 0, 0)
     with jax.named_scope("attention"):
         square, half = shape((channels, channels), BF16), shape((32, channels), BF16)
-        score, update = call(fold_body, [square, square], [VMEM] * 4, 600_000_000)(
+        score, update, order = call(fold_body, [square] * 3, [VMEM] * 4, 600_000_000)(
             w_qkv, w_out, attn_gain.reshape(1, channels), attn_gain.reshape(channels, 1)
         )
-        keep, send = call(attend_body, [half, half], [SMEM] + [VMEM] * 3, 200_000_000)(
-            place, hidden.reshape(4, channels, 256), score, update
+        keep, send = call(attend_body, [half, half], [SMEM] + [VMEM] * 4, 200_000_000)(
+            place, hidden.reshape(4, channels, 256), score, update, order
         )
         got = lax.ppermute(send, "core", swap)
         out = jnp.where(core == 0, jnp.concatenate([keep, got]), jnp.concatenate([got, keep]))

time: 82.1 us -> 81.5 us (level)
  waiting for transfers between devices: 12.4 us -> 11.3 us
  local copies, waits for them, and re-layouts: 0.26 us -> 1.29 us
    unnamed x6 -> x8, local copies, waits for them, and re-layouts: 0.02 us -> 1.05 us
    ppermute x1, waiting for transfers between devices: 0.99 us -> 0.01 us  [local(): lower = lax.ppermute(cells, 'core', [(1, 0)])]
  transfers between devices with their start and end apart: 5 -> 5, of which waited for: 4 -> 3; matrix products, arithmetic and copies ran while one was open for 0% -> 0% of each run, Pallas kernels for 4% -> 5%
where the time goes in v8:
time: 81.5 us; the launch traced here: 81 us
  blocking collectives  35.4 us (43%)
  starting transfers between devices  23.4 us (29%)
  waiting for transfers between devices  11.3 us (14%)
  Pallas kernels  8.62 us (11%)
  local copies, waits for them, and re-layouts  1.29 us (2%)
    all_gather x1, blocking collectives, gather_weights(): weight = lax.all_gather(piece, 'tm', axis=0, tiled=True)  26.2 us
    all_to_all x1, waiting for transfers between devices, local(): hidden = lax.all_to_all(hidden, PLANE, 0, 0)  10.4 us
    all_to_all x1, blocking collectives, local(): parts = lax.all_to_all(parts, 'width', 0, 0)  9.26 us
    ppermute x1, starting transfers between devices, local(): lower = lax.ppermute(cells, 'core', [(1, 0)])  8.77 us
    all_to_all x1, starting transfers between devices, local(): hidden = lax.all_to_all(hidden, PLANE, 0, 0)  5.21 us
    ppermute x1, starting transfers between devices, local(): got = lax.ppermute(send, 'core', swap)  5.02 us
    ppermute x1, starting transfers between devices, local(): handed_weight = lax.ppermute(weight, 'core', [(1, 0)])  3.12 us
    pallas_call x1, Pallas kernels, local(): call(conv_body, shape((4, SLOT, 256), BF16), [SMEM] + [VMEM] * 4, 700000000)  2.05 us
  transfers between devices with their start and end apart: 5, of which 3 were waited for; matrix products, arithmetic and copies ran while one was open for 0% of the time, Pallas kernels for 5%

profile of v8, /device:TPU:1, one launch (start us, length us, event | category | flops | bytes accessed | tf_op | source)
XLA Modules:
  0.0 81.0 jit_solution(18254984221250608292)
XLA Ops:
  0.0 8.8 %collective-permute-start.1 = (bf16[64,384]{1,0:T(8,128)(2,1)}, bf16[64,384]{1,0:T(8,128)(2,1)S(1)}, u32[]{:S(2)}, u32[]{:S(2)}) collective-permute-start(bf16[64,384]{1,0:T(8,128)(2,1)} %bitcast.18), channel_id=1, source_target_pairs={{4,0},{5,1},{6,2},{7,3},{12,8},{13,9},{14,10},{15,11},{20,16},{21,... | collective-permute-start | bytes 147464 | tf_op jit(solution)/shard_map/weights_and_cells/ppermute | solution.py:264
  8.8 0.1 pad_add_fusion.place_ref
  8.9 0.0 copy-start
  8.9 1.0 %copy-done = bf16[3,3,3,384,24]{3,4,2,1,0:T(8,128)(2,1)S(1)} copy-done((bf16[3,3,3,384,24]{3,4,2,1,0:T(8,128)(2,1)S(1)}, bf16[3,3,3,384,24]{3,4,2,1,0:T(8,128)(2,1)}, u32[]{:S(2)}) %copy-start) | copy-done | bytes 497688
  9.9 1.0 %weights_and_cells.1 = bf16[16,1024]{1,0:T(8,128)(2,1)S(1)} custom-call(s32[4]{0:T(128)S(1)} %pad_add_fusion.place_ref, bf16[27,24,384]{2,1,0:T(8,128)(2,1)S(1)} %bitcast.16), custom_call_target="tpu_custom_call" | custom-call | flops 1000000 | bytes 1000000 | tf_op jit(solution)/shard_map/weights_and_cells/pallas_call | solution.py:266
  10.9 0.0 collective-permute-done.1
  10.9 26.3 %conditional.1 = (bf16[256,1024]{1,0:T(8,128)(2,1)S(1)}, bf16[16,120,256]{2,1,0:T(8,128)(2,1)S(1)}, bf16[4,4,120,256]{3,2,1,0:T(8,128)(2,1)S(1)}) conditional(s32[]{:T(128)} %convert_element_type.3, (bf16[64,384]{1,0:T(8,128)(2,1)}, bf16[64,384]{1,0:T(8,128)(2,1)S(1)}, f32[384]{0:T(512)}) %tuple.18, bf16[16,1024]{1,0:T(8,128)(2,1)S(1)} %weights_and_cells.1), branch_computations={%region_0.0_spmd, %region_1.0_spmd} | conditional | flops 1000000 | bytes 6049410 | solution.py:267
  10.9 26.2 %all_gather.2 = bf16[256,1024]{1,0:T(8,128)(2,1)S(1)} all-gather(bf16[16,1024]{1,0:T(8,128)(2,1)S(1)} %param.1), channel_id=1, replica_groups=mesh['tm'=16,'y'=4,'core'=2,'width'=4] {'tm'}, dimensions={0}, use_global_device_ids=true | all-gather | bytes 557056 | tf_op jit(solution)/shard_map/weights_and_cells/cond/branch_1_fun/all_gather | solution.py:254
  37.1 0.1 broadcast.10
  37.1 0.1 reshape.28
  37.2 1.3 %collective-permute-start.2 = (bf16[16,120,256]{2,1,0:T(8,128)(2,1)S(1)}, bf16[16,120,256]{2,1,0:T(8,128)(2,1)S(1)}, u32[]{:S(2)}, u32[]{:S(2)}) collective-permute-start(bf16[16,120,256]{2,1,0:T(8,128)(2,1)S(1)} %get-tuple-element.28), channel_id=1, source_target_pairs={{0,4},{1,5},{2,6},{3,7},{8,12},{9,13},{10,14},{11,15},{16,20},{17,... | collective-permute-start | bytes 2949128 | tf_op jit(solution)/shard_map/patches/ppermute | solution.py:271
  38.5 3.1 %collective-permute-start.3 = (bf16[256,1024]{1,0:T(8,128)(2,1)S(1)}, bf16[256,1024]{1,0:T(8,128)(2,1)S(1)}, u32[]{:S(2)}, u32[]{:S(2)}) collective-permute-start(bf16[256,1024]{1,0:T(8,128)(2,1)S(1)} %get-tuple-element.31.mine_ref), channel_id=1, source_target_pairs={{4,0},{5,1},{6,2},{7,3},{12,8},{13,9},{14,10},{15,11},{20,16},{21,... | collective-permute-start | bytes 1572872 | tf_op jit(solution)/shard_map/patches/ppermute | solution.py:272
  41.6 0.0 collective-permute-done.2
  41.7 1.4 %patches.1 = (bf16[896,1024]{1,0:T(8,128)(2,1)S(1)}, f32[24,1024]{1,0:T(8,128)S(1)}) custom-call(s32[4]{0:T(128)S(1)} %pad_add_fusion.place_ref, bf16[4,4,120,256]{3,2,1,0:T(8,128)(2,1)S(1)} %get-tuple-element.27.mine_ref, bf16[4,4,120,256]{3,2,1,0:T(8,128)(2,1)S(1)} %bitcast.15), custom_call_target="tpu_custom_call" | custom-call | flops 1000000 | bytes 1000000 | tf_op jit(solution)/shard_map/patches/pallas_call | solution.py:274
  43.0 0.1 collective-permute-done.3.handed_ref
  43.1 2.1 %conv.1 = bf16[4,96,256]{2,1,0:T(8,128)(2,1)S(1)} custom-call(s32[4]{0:T(128)S(1)} %pad_add_fusion.place_ref, bf16[896,1024]{1,0:T(8,128)(2,1)S(1)} %get-tuple-element.29.flat_ref, f32[24,1024]{1,0:T(8,128)S(1)} %get-tuple-element.30.latent_ref, bf16[256,1024]{1,0:T(8,128)(2,1)S(1)} %get-tuple-element.31.mine_ref, ...), custom_call_target="tpu_custom_call" | custom-call | flops 700000000 | bytes 1000000 | tf_op jit(solution)/shard_map/conv/pallas_call | solution.py:278
  45.2 0.0 copy-start.3
  45.2 0.0 copy-start.1
  45.2 0.0 copy-start.2
  45.2 9.3 %all_to_all.15.part_ref = bf16[4,96,256]{2,1,0:T(8,128)(2,1)S(1)} all-to-all(bf16[4,96,256]{2,1,0:T(8,128)(2,1)S(1)} %conv.1), channel_id=1, replica_groups=mesh['tm'=16,'y'=4,'core'=2,'width'=4] {'width'}, dimensions={0} | all-to-all | bytes 393216 | tf_op jit(solution)/shard_map/conv/all_to_all | solution.py:281
  54.5 1.0 %hidden.1 = bf16[16,96,256]{2,1,0:T(8,128)(2,1)} custom-call(bf16[4,96,256]{2,1,0:T(8,128)(2,1)S(1)} %all_to_all.15.part_ref), custom_call_target="tpu_custom_call" | custom-call | flops 1000000 | bytes 1000000 | tf_op jit(solution)/shard_map/hidden/pallas_call | solution.py:283
  55.5 5.2 %all-to-all-start.2 = ((bf16[16,96,256]{2,1,0:T(8,128)(2,1)}), bf16[16,96,256]{2,1,0:T(8,128)(2,1)S(1)}, u32[]{:S(2)}, u32[]{:S(2)}) async-start(bf16[16,96,256]{2,1,0:T(8,128)(2,1)} %hidden.1), calls=%async_computation.2 | async-start | bytes 1572864 | tf_op jit(solution)/shard_map/hidden/all_to_all | solution.py:284
  60.7 0.0 copy-done.3
  60.7 0.1 reshape.41.column_ref
  60.8 0.0 copy-done.1
  60.8 0.0 copy-done.2
  60.9 1.6 %attention.2 = (bf16[384,384]{1,0:T(8,128)(2,1)S(1)}, bf16[384,384]{1,0:T(8,128)(2,1)S(1)}, bf16[384,384]{1,0:T(8,128)(2,1)S(1)}) custom-call(bf16[384,1152]{1,0:T(8,128)(2,1)S(1)} %copy-done.1, bf16[384,384]{1,0:T(8,128)(2,1)S(1)} %copy-done.2, f32[1,384]{1,0:T(1,128)S(1)} %reshape.39.row_ref, f32[384,1]{1,0:T(8,128)S(1)} %reshape.41.column_ref), custom_call_target="tpu_custom_call" | custom-call | flops 600000000 | bytes 1000000 | tf_op jit(solution)/shard_map/attention/pallas_call | solution.py:287
  62.4 10.4 %all-to-all-done.2 = bf16[16,96,256]{2,1,0:T(8,128)(2,1)S(1)} async-done(((bf16[16,96,256]{2,1,0:T(8,128)(2,1)}), bf16[16,96,256]{2,1,0:T(8,128)(2,1)S(1)}, u32[]{:S(2)}, u32[]{:S(2)}) %all-to-all-start.2) | async-done | bytes 786464 | tf_op jit(solution)/shard_map/hidden/all_to_all | solution.py:284
  72.8 1.7 %attention.3 = (bf16[32,384]{1,0:T(8,128)(2,1)S(1)}, bf16[32,384]{1,0:T(8,128)(2,1)S(1)}) custom-call(s32[4]{0:T(128)S(1)} %pad_add_fusion.place_ref, bf16[4,384,256]{2,1,0:T(8,128)(2,1)S(1)} %bitcast.14, bf16[384,384]{1,0:T(8,128)(2,1)S(1)} %get-tuple-element.32.score_ref, bf16[384,384]{1,0:T(8,128)(2,1)S(1)} %get-tuple-element.33.update_ref, ...), custom_call_target="tpu_custom_call" | custom-call | flops 200000000 | bytes 1000000 | tf_op jit(solution)/shard_map/attention/pallas_call | solution.py:290
  74.5 5.0 %collective-permute-start.4 = (bf16[32,384]{1,0:T(8,128)(2,1)S(1)}, bf16[32,384]{1,0:T(8,128)(2,1)S(1)}, u32[]{:S(2)}, u32[]{:S(2)}) collective-permute-start(bf16[32,384]{1,0:T(8,128)(2,1)S(1)} %get-tuple-element.36), channel_id=1, source_target_pairs={{0,4},{4,0},{1,5},{5,1},{2,6},{6,2},{3,7},{7,3},{8,12},{12,8},{9,1... | collective-permute-start | bytes 73736 | tf_op jit(solution)/shard_map/attention/ppermute | solution.py:293
  79.6 0.8 %collective-permute-done.4 = bf16[32,384]{1,0:T(8,128)(2,1)S(1)} collective-permute-done((bf16[32,384]{1,0:T(8,128)(2,1)S(1)}, bf16[32,384]{1,0:T(8,128)(2,1)S(1)}, u32[]{:S(2)}, u32[]{:S(2)}) %collective-permute-start.4) | collective-permute-done | bytes 24608 | tf_op jit(solution)/shard_map/attention/ppermute | solution.py:293
  80.4 0.6 maximum_select_fusion
  (1 shorter events, 0.0 us)
Async XLA Ops:
  0.0 10.9 %collective-permute-start.1 = (bf16[64,384]{1,0:T(8,128)(2,1)}, bf16[64,384]{1,0:T(8,128)(2,1)S(1)}, u32[]{:S(2)}, u32[]{:S(2)}) collective-permute-start(bf16[64,384]{1,0:T(8,128)(2,1)} %bitcast.18), channel_id=1, source_target_pairs={{4,0},{5,1},{6,2},{7,3},{12,8},{13,9},{14,10},{15,11},{20,16},{21,... | collective-permute-start | bytes 147464 | tf_op jit(solution)/shard_map/weights_and_cells/ppermute | solution.py:264
  8.9 1.0 %copy-start = (bf16[3,3,3,384,24]{3,4,2,1,0:T(8,128)(2,1)S(1)}, bf16[3,3,3,384,24]{3,4,2,1,0:T(8,128)(2,1)}, u32[]{:S(2)}) copy-start(bf16[3,3,3,384,24]{3,4,2,1,0:T(8,128)(2,1)} %param.10) | copy-start | bytes 1492996
  37.2 4.5 %collective-permute-start.2 = (bf16[16,120,256]{2,1,0:T(8,128)(2,1)S(1)}, bf16[16,120,256]{2,1,0:T(8,128)(2,1)S(1)}, u32[]{:S(2)}, u32[]{:S(2)}) collective-permute-start(bf16[16,120,256]{2,1,0:T(8,128)(2,1)S(1)} %get-tuple-element.28), channel_id=1, source_target_pairs={{0,4},{1,5},{2,6},{3,7},{8,12},{9,13},{10,14},{11,15},{16,20},{17,... | collective-permute-start | bytes 2949128 | tf_op jit(solution)/shard_map/patches/ppermute | solution.py:271
  38.5 4.6 %collective-permute-start.3 = (bf16[256,1024]{1,0:T(8,128)(2,1)S(1)}, bf16[256,1024]{1,0:T(8,128)(2,1)S(1)}, u32[]{:S(2)}, u32[]{:S(2)}) collective-permute-start(bf16[256,1024]{1,0:T(8,128)(2,1)S(1)} %get-tuple-element.31.mine_ref), channel_id=1, source_target_pairs={{4,0},{5,1},{6,2},{7,3},{12,8},{13,9},{14,10},{15,11},{20,16},{21,... | collective-permute-start | bytes 1572872 | tf_op jit(solution)/shard_map/patches/ppermute | solution.py:272
  45.2 15.5 %copy-start.3 = (f32[384]{0:T(512)S(1)}, f32[384]{0:T(512)}, u32[]{:S(2)}) copy-start(f32[384]{0:T(512)} %param.11) | copy-start | bytes 4612
  45.2 15.6 %copy-start.1 = (bf16[384,1152]{1,0:T(8,128)(2,1)S(1)}, bf16[384,1152]{1,0:T(8,128)(2,1)}, u32[]{:S(2)}) copy-start(bf16[384,1152]{1,0:T(8,128)(2,1)} %w_ref.1) | copy-start | bytes 2654212
  45.2 15.6 %copy-start.2 = (bf16[384,384]{1,0:T(8,128)(2,1)S(1)}, bf16[384,384]{1,0:T(8,128)(2,1)}, u32[]{:S(2)}) copy-start(bf16[384,384]{1,0:T(8,128)(2,1)} %w_out_ref.1) | copy-start | bytes 884740
  55.5 17.4 %all-to-all-start.2 = ((bf16[16,96,256]{2,1,0:T(8,128)(2,1)}), bf16[16,96,256]{2,1,0:T(8,128)(2,1)S(1)}, u32[]{:S(2)}, u32[]{:S(2)}) async-start(bf16[16,96,256]{2,1,0:T(8,128)(2,1)} %hidden.1), calls=%async_computation.2 | async-start | bytes 1572864 | tf_op jit(solution)/shard_map/hidden/all_to_all | solution.py:284
  74.5 5.9 %collective-permute-start.4 = (bf16[32,384]{1,0:T(8,128)(2,1)S(1)}, bf16[32,384]{1,0:T(8,128)(2,1)S(1)}, u32[]{:S(2)}, u32[]{:S(2)}) collective-permute-start(bf16[32,384]{1,0:T(8,128)(2,1)S(1)} %get-tuple-element.36), channel_id=1, source_target_pairs={{0,4},{4,0},{1,5},{5,1},{2,6},{6,2},{3,7},{7,3},{8,12},{12,8},{9,1... | collective-permute-start | bytes 73736 | tf_op jit(solution)/shard_map/attention/ppermute | solution.py:293

commit v9 on v8

--- a/solution.py
+++ b/solution.py
@@ -12,14 +12,16 @@
 TAPS = 27
 GROUP = 24
 SLOT = 96
+ROWS = SLOT + 16
 BAND = 896
 PLANE = ("width", "y")
 VMEM = pl.BlockSpec(memory_space=pltpu.VMEM)
 SMEM = pl.BlockSpec(memory_space=pltpu.SMEM)
 LIMIT = 12 * 1024 * 1024
-
-
-def call(body, out, specs, flops=1_000_000, moved=1_000_000, scratch=()):
+FIRST_LIMIT = 55040 * 1024
+
+
+def call(body, out, specs, flops=1_000_000, moved=1_000_000, scratch=(), limit=LIMIT):
     many = isinstance(out, (tuple, list))
     return pl.pallas_call(
         body,
@@ -27,7 +29,7 @@
         in_specs=specs,
         out_specs=[VMEM] * len(out) if many else VMEM,
         scratch_shapes=list(scratch),
-        compiler_params=pltpu.CompilerParams(vmem_limit_bytes=LIMIT),
+        compiler_params=pltpu.CompilerParams(vmem_limit_bytes=limit),
         cost_estimate=pl.CostEstimate(flops=flops, bytes_accessed=moved, transcendentals=0),
     )
 
@@ -94,13 +96,14 @@
     latent = lax.dot_general(
         one_hot((384, 384), channel_of), now, (((1,), (1,)), ((), ())), preferred_element_type=F32
     )
-    blank = jnp.zeros((GROUP, 128), BF16)
+    blank = jnp.zeros((8, 128), F32)
     for width in range(4):
         for row in range(4):
             start = row * SLOT + width * GROUP
             out_ref[width, row, :SLOT, :] = both[width * SLOT : width * SLOT + SLOT]
-            out_ref[width, row, SLOT:, :128] = latent[start : start + GROUP].astype(BF16)
-            out_ref[width, row, SLOT:, 128:] = blank
+            out_ref[width, row, SLOT:, :128] = latent[start : start + 16].astype(BF16)
+            rest = jnp.concatenate([latent[start + 16 : start + GROUP], blank], axis=0)
+            out_ref[width, row, SLOT:, 128:] = rest.astype(BF16)
 
 
 def grid_place(odd, row):
@@ -136,8 +139,11 @@
     flat_ref[9 * SLOT :, :] = jnp.zeros((BAND - 9 * SLOT, 1024), BF16)
     place = jnp.where(core == 0, places[0], places[1])
     for row in range(4):
-        part = jnp.concatenate([blocks[row][width][SLOT:, :128] for width in range(4)], axis=1)
-        latent_ref[:, row * 256 : row * 256 + 256] = jnp.dot(part, place, preferred_element_type=F32)
+        for half, count in ((0, 16), (1, 8)):
+            cut = slice(half * 128, half * 128 + 128)
+            part = jnp.concatenate([blocks[row][width][SLOT:, cut] for width in range(4)], axis=1)
+            part = jnp.dot(part, place, preferred_element_type=F32)[:count]
+            latent_ref[half * 16 : half * 16 + count, row * 256 : row * 256 + 256] = part
 
 
 def main_place(row):
@@ -248,7 +254,7 @@
     swap = [(0, 1), (1, 0)]
     shape = jax.ShapeDtypeStruct
     cells = latent.reshape(64, channels)
-    weight_shape, block_shape = (256, 1024), (16, SLOT + GROUP, 256)
+    weight_shape, block_shape = (256, 1024), (16, ROWS, 256)
 
     def gather_weights(cells, lower, gain, piece):
         weight = lax.all_gather(piece, "tm", axis=0, tiled=True)
@@ -257,20 +263,20 @@
     def exchange_cells(cells, lower, gain, piece):
         now = jnp.concatenate([cells, lower], axis=0)
         before = lax.ppermute(now, ("tm", "core"), [(2 * i, 2 * i + 2) for i in range(15)])
-        blocks = call(block_body, shape((4, 4, SLOT + GROUP, 256), BF16), [VMEM] * 3)(before, now, gain)
+        blocks = call(block_body, shape((4, 4, ROWS, 256), BF16), [VMEM] * 3)(before, now, gain)
         return jnp.zeros(weight_shape, BF16), lax.all_to_all(blocks.reshape(block_shape), PLANE, 0, 0)
 
     with jax.named_scope("weights_and_cells"):
         lower = lax.ppermute(cells, "core", [(1, 0)])
         turned = jnp.transpose(conv_weight.reshape(TAPS, channels, GROUP), (0, 2, 1))
-        piece = call(weight_body, shape((16, 1024), BF16), [SMEM, VMEM])(place, turned)
+        piece = call(weight_body, shape((16, 1024), BF16), [SMEM, VMEM], limit=FIRST_LIMIT)(place, turned)
         weight, blocks = lax.cond(
             core == 1, gather_weights, exchange_cells, cells, lower, norm_gain.reshape(1, channels), piece
         )
     with jax.named_scope("patches"):
         handed_blocks = lax.ppermute(blocks, "core", [(0, 1)])
         handed_weight = lax.ppermute(weight, "core", [(1, 0)])
-        grouped = (4, 4, SLOT + GROUP, 256)
+        grouped = (4, 4, ROWS, 256)
         flat, own = call(
             patch_body, [shape((BAND, 1024), BF16), shape((GROUP, 1024), F32)], [SMEM] + [VMEM] * 2
         )(place, blocks.reshape(grouped), handed_blocks.reshape(grouped))

time: 81.5 us -> 81 us (level)
  local copies, waits for them, and re-layouts: 1.29 us -> 0.25 us
    unnamed x8 -> x6, local copies, waits for them, and re-layouts: 1.05 us -> 0.02 us
  transfers between devices with their start and end apart: 5 -> 5, of which waited for: 3 -> 2; matrix products, arithmetic and copies ran while one was open for 0% -> 0% of each run, Pallas kernels for 5% -> 6%
where the time goes in v9:
time: 81 us; the launch traced here: 80.5 us
  blocking collectives  35.4 us (44%)
  starting transfers between devices  23.4 us (29%)
  waiting for transfers between devices  11.2 us (14%)
  Pallas kernels  9.24 us (11%)
    all_gather x1, blocking collectives, gather_weights(): weight = lax.all_gather(piece, 'tm', axis=0, tiled=True)  26.2 us
    all_to_all x1, waiting for transfers between devices, local(): hidden = lax.all_to_all(hidden, PLANE, 0, 0)  10.4 us
    all_to_all x1, blocking collectives, local(): parts = lax.all_to_all(parts, 'width', 0, 0)  9.23 us
    ppermute x1, starting transfers between devices, local(): lower = lax.ppermute(cells, 'core', [(1, 0)])  8.77 us
    all_to_all x1, starting transfers between devices, local(): hidden = lax.all_to_all(hidden, PLANE, 0, 0)  5.24 us
    ppermute x1, starting transfers between devices, local(): got = lax.ppermute(send, 'core', swap)  5.03 us
    ppermute x1, starting transfers between devices, local(): handed_weight = lax.ppermute(weight, 'core', [(1, 0)])  3.12 us
    pallas_call x1, Pallas kernels, local(): call(conv_body, shape((4, SLOT, 256), BF16), [SMEM] + [VMEM] * 4, 700000000)  2.05 us
  transfers between devices with their start and end apart: 5, of which 2 were waited for; matrix products, arithmetic and copies ran while one was open for 0% of the time, Pallas kernels for 6%

profile of v9, /device:TPU:1, one launch (start us, length us, event | category | flops | bytes accessed | tf_op | source)
XLA Modules:
  0.0 80.5 jit_solution(9074633079410468489)
XLA Ops:
  0.0 8.8 %collective-permute-start.1 = (bf16[64,384]{1,0:T(8,128)(2,1)}, bf16[64,384]{1,0:T(8,128)(2,1)S(1)}, u32[]{:S(2)}, u32[]{:S(2)}) collective-permute-start(bf16[64,384]{1,0:T(8,128)(2,1)} %bitcast.18), channel_id=1, source_target_pairs={{4,0},{5,1},{6,2},{7,3},{12,8},{13,9},{14,10},{15,11},{20,16},{21,... | collective-permute-start | bytes 147464 | tf_op jit(solution)/shard_map/weights_and_cells/ppermute | solution.py:270
  8.8 0.1 pad_add_fusion.place_ref
  8.9 1.5 %weights_and_cells.1 = bf16[16,1024]{1,0:T(8,128)(2,1)S(1)} custom-call(s32[4]{0:T(128)S(1)} %pad_add_fusion.place_ref, bf16[27,24,384]{2,1,0:T(8,128)(2,1)} %bitcast.17), custom_call_target="tpu_custom_call" | custom-call | flops 1000000 | bytes 1000000 | tf_op jit(solution)/shard_map/weights_and_cells/pallas_call | solution.py:272
  10.3 0.0 collective-permute-done.1
  10.3 26.3 %conditional.1 = (bf16[256,1024]{1,0:T(8,128)(2,1)S(1)}, bf16[16,112,256]{2,1,0:T(8,128)(2,1)S(1)}, bf16[4,4,112,256]{3,2,1,0:T(8,128)(2,1)S(1)}) conditional(s32[]{:T(128)} %convert_element_type.3, (bf16[64,384]{1,0:T(8,128)(2,1)}, bf16[64,384]{1,0:T(8,128)(2,1)S(1)}, f32[384]{0:T(512)}) %tuple.18, bf16[16,1024]{1,0:T(8,128)(2,1)S(1)} %weights_and_cells.1), branch_computations={%region_0.0_spmd, %region_1.0_spmd} | conditional | flops 1000000 | bytes 5787266 | solution.py:273
  10.4 26.2 %all_gather.2 = bf16[256,1024]{1,0:T(8,128)(2,1)S(1)} all-gather(bf16[16,1024]{1,0:T(8,128)(2,1)S(1)} %param.1), channel_id=1, replica_groups=mesh['tm'=16,'y'=4,'core'=2,'width'=4] {'tm'}, dimensions={0}, use_global_device_ids=true | all-gather | bytes 557056 | tf_op jit(solution)/shard_map/weights_and_cells/cond/branch_1_fun/all_gather | solution.py:260
  36.5 0.1 broadcast.10
  36.6 0.1 reshape.28
  36.7 1.3 %collective-permute-start.2 = (bf16[16,112,256]{2,1,0:T(8,128)(2,1)S(1)}, bf16[16,112,256]{2,1,0:T(8,128)(2,1)S(1)}, u32[]{:S(2)}, u32[]{:S(2)}) collective-permute-start(bf16[16,112,256]{2,1,0:T(8,128)(2,1)S(1)} %get-tuple-element.28), channel_id=1, source_target_pairs={{0,4},{1,5},{2,6},{3,7},{8,12},{9,13},{10,14},{11,15},{16,20},{17,... | collective-permute-start | bytes 2752520 | tf_op jit(solution)/shard_map/patches/ppermute | solution.py:277
  38.0 3.1 %collective-permute-start.3 = (bf16[256,1024]{1,0:T(8,128)(2,1)S(1)}, bf16[256,1024]{1,0:T(8,128)(2,1)S(1)}, u32[]{:S(2)}, u32[]{:S(2)}) collective-permute-start(bf16[256,1024]{1,0:T(8,128)(2,1)S(1)} %get-tuple-element.31.mine_ref), channel_id=1, source_target_pairs={{4,0},{5,1},{6,2},{7,3},{12,8},{13,9},{14,10},{15,11},{20,16},{21,... | collective-permute-start | bytes 1572872 | tf_op jit(solution)/shard_map/patches/ppermute | solution.py:278
  41.1 0.0 collective-permute-done.2
  41.1 1.5 %patches.1 = (bf16[896,1024]{1,0:T(8,128)(2,1)S(1)}, f32[24,1024]{1,0:T(8,128)S(1)}) custom-call(s32[4]{0:T(128)S(1)} %pad_add_fusion.place_ref, bf16[4,4,112,256]{3,2,1,0:T(8,128)(2,1)S(1)} %get-tuple-element.27.mine_ref, bf16[4,4,112,256]{3,2,1,0:T(8,128)(2,1)S(1)} %bitcast.15), custom_call_target="tpu_custom_call" | custom-call | flops 1000000 | bytes 1000000 | tf_op jit(solution)/shard_map/patches/pallas_call | solution.py:280
  42.6 0.0 collective-permute-done.3.handed_ref
  42.6 2.1 %conv.1 = bf16[4,96,256]{2,1,0:T(8,128)(2,1)S(1)} custom-call(s32[4]{0:T(128)S(1)} %pad_add_fusion.place_ref, bf16[896,1024]{1,0:T(8,128)(2,1)S(1)} %get-tuple-element.29.flat_ref, f32[24,1024]{1,0:T(8,128)S(1)} %get-tuple-element.30.latent_ref, bf16[256,1024]{1,0:T(8,128)(2,1)S(1)} %get-tuple-element.31.mine_ref, ...), custom_call_target="tpu_custom_call" | custom-call | flops 700000000 | bytes 1000000 | tf_op jit(solution)/shard_map/conv/pallas_call | solution.py:284
  44.6 0.0 copy-start.2
  44.7 0.0 copy-start
  44.7 0.0 copy-start.1
  44.7 9.2 %all_to_all.15.part_ref = bf16[4,96,256]{2,1,0:T(8,128)(2,1)S(1)} all-to-all(bf16[4,96,256]{2,1,0:T(8,128)(2,1)S(1)} %conv.1), channel_id=1, replica_groups=mesh['tm'=16,'y'=4,'core'=2,'width'=4] {'width'}, dimensions={0} | all-to-all | bytes 393216 | tf_op jit(solution)/shard_map/conv/all_to_all | solution.py:287
  53.9 1.0 %hidden.1 = bf16[16,96,256]{2,1,0:T(8,128)(2,1)} custom-call(bf16[4,96,256]{2,1,0:T(8,128)(2,1)S(1)} %all_to_all.15.part_ref), custom_call_target="tpu_custom_call" | custom-call | flops 1000000 | bytes 1000000 | tf_op jit(solution)/shard_map/hidden/pallas_call | solution.py:289
  54.9 5.2 %all-to-all-start.2 = ((bf16[16,96,256]{2,1,0:T(8,128)(2,1)}), bf16[16,96,256]{2,1,0:T(8,128)(2,1)S(1)}, u32[]{:S(2)}, u32[]{:S(2)}) async-start(bf16[16,96,256]{2,1,0:T(8,128)(2,1)} %hidden.1), calls=%async_computation.2 | async-start | bytes 1572864 | tf_op jit(solution)/shard_map/hidden/all_to_all | solution.py:290
  60.2 0.0 copy-done.2
  60.2 0.1 reshape.41.column_ref
  60.3 0.0 copy-done
  60.3 0.0 copy-done.1
  60.3 1.6 %attention.2 = (bf16[384,384]{1,0:T(8,128)(2,1)S(1)}, bf16[384,384]{1,0:T(8,128)(2,1)S(1)}, bf16[384,384]{1,0:T(8,128)(2,1)S(1)}) custom-call(bf16[384,1152]{1,0:T(8,128)(2,1)S(1)} %copy-done, bf16[384,384]{1,0:T(8,128)(2,1)S(1)} %copy-done.1, f32[1,384]{1,0:T(1,128)S(1)} %reshape.39.row_ref, f32[384,1]{1,0:T(8,128)S(1)} %reshape.41.column_ref), custom_call_target="tpu_custom_call" | custom-call | flops 600000000 | bytes 1000000 | tf_op jit(solution)/shard_map/attention/pallas_call | solution.py:293
  61.9 10.4 %all-to-all-done.2 = bf16[16,96,256]{2,1,0:T(8,128)(2,1)S(1)} async-done(((bf16[16,96,256]{2,1,0:T(8,128)(2,1)}), bf16[16,96,256]{2,1,0:T(8,128)(2,1)S(1)}, u32[]{:S(2)}, u32[]{:S(2)}) %all-to-all-start.2) | async-done | bytes 786464 | tf_op jit(solution)/shard_map/hidden/all_to_all | solution.py:290
  72.3 1.7 %attention.3 = (bf16[32,384]{1,0:T(8,128)(2,1)S(1)}, bf16[32,384]{1,0:T(8,128)(2,1)S(1)}) custom-call(s32[4]{0:T(128)S(1)} %pad_add_fusion.place_ref, bf16[4,384,256]{2,1,0:T(8,128)(2,1)S(1)} %bitcast.14, bf16[384,384]{1,0:T(8,128)(2,1)S(1)} %get-tuple-element.32.score_ref, bf16[384,384]{1,0:T(8,128)(2,1)S(1)} %get-tuple-element.33.update_ref, ...), custom_call_target="tpu_custom_call" | custom-call | flops 200000000 | bytes 1000000 | tf_op jit(solution)/shard_map/attention/pallas_call | solution.py:296
  74.0 5.0 %collective-permute-start.4 = (bf16[32,384]{1,0:T(8,128)(2,1)S(1)}, bf16[32,384]{1,0:T(8,128)(2,1)S(1)}, u32[]{:S(2)}, u32[]{:S(2)}) collective-permute-start(bf16[32,384]{1,0:T(8,128)(2,1)S(1)} %get-tuple-element.36), channel_id=1, source_target_pairs={{0,4},{4,0},{1,5},{5,1},{2,6},{6,2},{3,7},{7,3},{8,12},{12,8},{9,1... | collective-permute-start | bytes 73736 | tf_op jit(solution)/shard_map/attention/ppermute | solution.py:299
  79.0 0.8 %collective-permute-done.4 = bf16[32,384]{1,0:T(8,128)(2,1)S(1)} collective-permute-done((bf16[32,384]{1,0:T(8,128)(2,1)S(1)}, bf16[32,384]{1,0:T(8,128)(2,1)S(1)}, u32[]{:S(2)}, u32[]{:S(2)}) %collective-permute-start.4) | collective-permute-done | bytes 24608 | tf_op jit(solution)/shard_map/attention/ppermute | solution.py:299
  79.9 0.6 maximum_select_fusion
  (1 shorter events, 0.0 us)
Async XLA Ops:
  0.0 10.3 %collective-permute-start.1 = (bf16[64,384]{1,0:T(8,128)(2,1)}, bf16[64,384]{1,0:T(8,128)(2,1)S(1)}, u32[]{:S(2)}, u32[]{:S(2)}) collective-permute-start(bf16[64,384]{1,0:T(8,128)(2,1)} %bitcast.18), channel_id=1, source_target_pairs={{4,0},{5,1},{6,2},{7,3},{12,8},{13,9},{14,10},{15,11},{20,16},{21,... | collective-permute-start | bytes 147464 | tf_op jit(solution)/shard_map/weights_and_cells/ppermute | solution.py:270
  36.7 4.4 %collective-permute-start.2 = (bf16[16,112,256]{2,1,0:T(8,128)(2,1)S(1)}, bf16[16,112,256]{2,1,0:T(8,128)(2,1)S(1)}, u32[]{:S(2)}, u32[]{:S(2)}) collective-permute-start(bf16[16,112,256]{2,1,0:T(8,128)(2,1)S(1)} %get-tuple-element.28), channel_id=1, source_target_pairs={{0,4},{1,5},{2,6},{3,7},{8,12},{9,13},{10,14},{11,15},{16,20},{17,... | collective-permute-start | bytes 2752520 | tf_op jit(solution)/shard_map/patches/ppermute | solution.py:277
  38.0 4.6 %collective-permute-start.3 = (bf16[256,1024]{1,0:T(8,128)(2,1)S(1)}, bf16[256,1024]{1,0:T(8,128)(2,1)S(1)}, u32[]{:S(2)}, u32[]{:S(2)}) collective-permute-start(bf16[256,1024]{1,0:T(8,128)(2,1)S(1)} %get-tuple-element.31.mine_ref), channel_id=1, source_target_pairs={{4,0},{5,1},{6,2},{7,3},{12,8},{13,9},{14,10},{15,11},{20,16},{21,... | collective-permute-start | bytes 1572872 | tf_op jit(solution)/shard_map/patches/ppermute | solution.py:278
  44.6 15.5 %copy-start.2 = (f32[384]{0:T(512)S(1)}, f32[384]{0:T(512)}, u32[]{:S(2)}) copy-start(f32[384]{0:T(512)} %param.11) | copy-start | bytes 4612
  44.7 15.6 %copy-start = (bf16[384,1152]{1,0:T(8,128)(2,1)S(1)}, bf16[384,1152]{1,0:T(8,128)(2,1)}, u32[]{:S(2)}) copy-start(bf16[384,1152]{1,0:T(8,128)(2,1)} %w_ref.1) | copy-start | bytes 2654212
  44.7 15.6 %copy-start.1 = (bf16[384,384]{1,0:T(8,128)(2,1)S(1)}, bf16[384,384]{1,0:T(8,128)(2,1)}, u32[]{:S(2)}) copy-start(bf16[384,384]{1,0:T(8,128)(2,1)} %w_out_ref.1) | copy-start | bytes 884740
  54.9 17.4 %all-to-all-start.2 = ((bf16[16,96,256]{2,1,0:T(8,128)(2,1)}), bf16[16,96,256]{2,1,0:T(8,128)(2,1)S(1)}, u32[]{:S(2)}, u32[]{:S(2)}) async-start(bf16[16,96,256]{2,1,0:T(8,128)(2,1)} %hidden.1), calls=%async_computation.2 | async-start | bytes 1572864 | tf_op jit(solution)/shard_map/hidden/all_to_all | solution.py:290
  74.0 5.9 %collective-permute-start.4 = (bf16[32,384]{1,0:T(8,128)(2,1)S(1)}, bf16[32,384]{1,0:T(8,128)(2,1)S(1)}, u32[]{:S(2)}, u32[]{:S(2)}) collective-permute-start(bf16[32,384]{1,0:T(8,128)(2,1)S(1)} %get-tuple-element.36), channel_id=1, source_target_pairs={{0,4},{4,0},{1,5},{5,1},{2,6},{6,2},{3,7},{7,3},{8,12},{12,8},{9,1... | collective-permute-start | bytes 73736 | tf_op jit(solution)/shard_map/attention/ppermute | solution.py:299

commit v10 on v9

--- a/solution.py
+++ b/solution.py
@@ -285,14 +285,16 @@
             place, flat, own, weight, handed_weight
         )
         parts = lax.all_to_all(parts, "width", 0, 0)
+    with jax.named_scope("folded_weights"):
+        square, half = shape((channels, channels), BF16), shape((32, channels), BF16)
+        score, update, order = call(fold_body, [square] * 3, [VMEM] * 4, 600_000_000)(
+            w_qkv, w_out, attn_gain.reshape(1, channels), attn_gain.reshape(channels, 1)
+        )
+        parts, score, update, order = lax.optimization_barrier((parts, score, update, order))
     with jax.named_scope("hidden"):
         hidden = call(hidden_body, shape((16, SLOT, 256), BF16), [VMEM])(parts)
         hidden = lax.all_to_all(hidden, PLANE, 0, 0)
     with jax.named_scope("attention"):
-        square, half = shape((channels, channels), BF16), shape((32, channels), BF16)
-        score, update, order = call(fold_body, [square] * 3, [VMEM] * 4, 600_000_000)(
-            w_qkv, w_out, attn_gain.reshape(1, channels), attn_gain.reshape(channels, 1)
-        )
         keep, send = call(attend_body, [half, half], [SMEM] + [VMEM] * 4, 200_000_000)(
             place, hidden.reshape(4, channels, 256), score, update, order
         )

time: 81 us -> 80.3 us (level)
  blocking collectives: 35.4 us -> 42.9 us
  waiting for transfers between devices: 11.2 us -> 4.31 us
  starting transfers between devices: 23.4 us -> 22.5 us
    all_to_all x1, blocking collectives: 9.23 us -> 16.7 us  [local(): hidden = lax.all_to_all(hidden, PLANE, 0, 0)]
    all_to_all x1, waiting for transfers between devices: 10.4 us -> 3.46 us  [local(): parts = lax.all_to_all(parts, 'width', 0, 0)]
    all_to_all x1, starting transfers between devices: 5.24 us -> 4.01 us  [local(): parts = lax.all_to_all(parts, 'width', 0, 0)]
    pallas_call x1, Pallas kernels: 1 us -> 0.07 us  [local(): hidden = call(hidden_body, shape((16, SLOT, 256), BF16), [VMEM])(parts)]
where the time goes in v10:
time: 80.3 us; the launch traced here: 79.8 us
  blocking collectives  42.9 us (53%)
  starting transfers between devices  22.5 us (28%)
  Pallas kernels  9 us (11%)
  waiting for transfers between devices  4.31 us (5%)
    all_gather x1, blocking collectives, gather_weights(): weight = lax.all_gather(piece, 'tm', axis=0, tiled=True)  26.2 us
    all_to_all x1, blocking collectives, local(): hidden = lax.all_to_all(hidden, PLANE, 0, 0)  16.7 us
    ppermute x1, starting transfers between devices, local(): lower = lax.ppermute(cells, 'core', [(1, 0)])  8.77 us
    ppermute x1, starting transfers between devices, local(): got = lax.ppermute(send, 'core', swap)  5.26 us
    all_to_all x1, starting transfers between devices, local(): parts = lax.all_to_all(parts, 'width', 0, 0)  4.01 us
    all_to_all x1, waiting for transfers between devices, local(): parts = lax.all_to_all(parts, 'width', 0, 0)  3.46 us
    ppermute x1, starting transfers between devices, local(): handed_weight = lax.ppermute(weight, 'core', [(1, 0)])  3.12 us
    pallas_call x1, Pallas kernels, local(): call(conv_body, shape((4, SLOT, 256), BF16), [SMEM] + [VMEM] * 4, 700000000)  2.75 us
  transfers between devices with their start and end apart: 5, of which 2 were waited for; matrix products, arithmetic and copies ran while one was open for 0% of the time, Pallas kernels for 6%

profile of v10, /device:TPU:1, one launch (start us, length us, event | category | flops | bytes accessed | tf_op | source)
XLA Modules:
  0.0 79.8 jit_solution(6011329203134663831)
XLA Ops:
  0.0 8.8 %collective-permute-start.1 = (bf16[64,384]{1,0:T(8,128)(2,1)}, bf16[64,384]{1,0:T(8,128)(2,1)S(1)}, u32[]{:S(2)}, u32[]{:S(2)}) collective-permute-start(bf16[64,384]{1,0:T(8,128)(2,1)} %bitcast.18), channel_id=1, source_target_pairs={{4,0},{5,1},{6,2},{7,3},{12,8},{13,9},{14,10},{15,11},{20,16},{21,... | collective-permute-start | bytes 147464 | tf_op jit(solution)/shard_map/weights_and_cells/ppermute | solution.py:270
  8.8 0.1 pad_add_fusion.place_ref
  8.9 1.5 %weights_and_cells.1 = bf16[16,1024]{1,0:T(8,128)(2,1)S(1)} custom-call(s32[4]{0:T(128)S(1)} %pad_add_fusion.place_ref, bf16[27,24,384]{2,1,0:T(8,128)(2,1)} %bitcast.17), custom_call_target="tpu_custom_call" | custom-call | flops 1000000 | bytes 1000000 | tf_op jit(solution)/shard_map/weights_and_cells/pallas_call | solution.py:272
  10.3 0.0 collective-permute-done.1
  10.3 26.3 %conditional.1 = (bf16[256,1024]{1,0:T(8,128)(2,1)S(1)}, bf16[16,112,256]{2,1,0:T(8,128)(2,1)S(1)}, bf16[4,4,112,256]{3,2,1,0:T(8,128)(2,1)S(1)}) conditional(s32[]{:T(128)} %convert_element_type.3, (bf16[64,384]{1,0:T(8,128)(2,1)}, bf16[64,384]{1,0:T(8,128)(2,1)S(1)}, f32[384]{0:T(512)}) %tuple.20, bf16[16,1024]{1,0:T(8,128)(2,1)S(1)} %weights_and_cells.1), branch_computations={%region_0.0_spmd, %region_1.0_spmd} | conditional | flops 1000000 | bytes 5787266 | solution.py:273
  10.4 26.2 %all_gather.2 = bf16[256,1024]{1,0:T(8,128)(2,1)S(1)} all-gather(bf16[16,1024]{1,0:T(8,128)(2,1)S(1)} %param.1), channel_id=1, replica_groups=mesh['tm'=16,'y'=4,'core'=2,'width'=4] {'tm'}, dimensions={0}, use_global_device_ids=true | all-gather | bytes 557056 | tf_op jit(solution)/shard_map/weights_and_cells/cond/branch_1_fun/all_gather | solution.py:260
  36.5 0.1 broadcast.10
  36.6 0.1 reshape.28
  36.7 1.3 %collective-permute-start.2 = (bf16[16,112,256]{2,1,0:T(8,128)(2,1)S(1)}, bf16[16,112,256]{2,1,0:T(8,128)(2,1)S(1)}, u32[]{:S(2)}, u32[]{:S(2)}) collective-permute-start(bf16[16,112,256]{2,1,0:T(8,128)(2,1)S(1)} %get-tuple-element.32), channel_id=1, source_target_pairs={{0,4},{1,5},{2,6},{3,7},{8,12},{9,13},{10,14},{11,15},{16,20},{17,... | collective-permute-start | bytes 2752520 | tf_op jit(solution)/shard_map/patches/ppermute | solution.py:277
  38.0 3.1 %collective-permute-start.3 = (bf16[256,1024]{1,0:T(8,128)(2,1)S(1)}, bf16[256,1024]{1,0:T(8,128)(2,1)S(1)}, u32[]{:S(2)}, u32[]{:S(2)}) collective-permute-start(bf16[256,1024]{1,0:T(8,128)(2,1)S(1)} %get-tuple-element.35.mine_ref), channel_id=1, source_target_pairs={{4,0},{5,1},{6,2},{7,3},{12,8},{13,9},{14,10},{15,11},{20,16},{21,... | collective-permute-start | bytes 1572872 | tf_op jit(solution)/shard_map/patches/ppermute | solution.py:278
  41.1 0.0 collective-permute-done.2
  41.1 1.5 %patches.1 = (bf16[896,1024]{1,0:T(8,128)(2,1)S(1)}, f32[24,1024]{1,0:T(8,128)S(1)}) custom-call(s32[4]{0:T(128)S(1)} %pad_add_fusion.place_ref, bf16[4,4,112,256]{3,2,1,0:T(8,128)(2,1)S(1)} %get-tuple-element.31.mine_ref, bf16[4,4,112,256]{3,2,1,0:T(8,128)(2,1)S(1)} %bitcast.15), custom_call_target="tpu_custom_call" | custom-call | flops 1000000 | bytes 1000000 | tf_op jit(solution)/shard_map/patches/pallas_call | solution.py:280
  42.6 0.0 copy-start.2
  42.6 0.0 collective-permute-done.3.handed_ref
  42.6 0.0 copy-start
  42.6 0.0 copy-start.1
  42.6 2.7 %conv.1 = bf16[4,96,256]{2,1,0:T(8,128)(2,1)} custom-call(s32[4]{0:T(128)S(1)} %pad_add_fusion.place_ref, bf16[896,1024]{1,0:T(8,128)(2,1)S(1)} %get-tuple-element.33.flat_ref, f32[24,1024]{1,0:T(8,128)S(1)} %get-tuple-element.34.latent_ref, bf16[256,1024]{1,0:T(8,128)(2,1)S(1)} %get-tuple-element.35.mine_ref, ...), custom_call_target="tpu_custom_call" | custom-call | flops 700000000 | bytes 1000000 | tf_op jit(solution)/shard_map/conv/pallas_call | solution.py:284
  45.3 4.0 %all-to-all-start.1 = ((bf16[4,96,256]{2,1,0:T(8,128)(2,1)}), bf16[4,96,256]{2,1,0:T(8,128)(2,1)S(1)}, u32[]{:S(2)}, u32[]{:S(2)}) async-start(bf16[4,96,256]{2,1,0:T(8,128)(2,1)} %conv.1), calls=%async_computation.1 | async-start | bytes 393216 | tf_op jit(solution)/shard_map/conv/all_to_all | solution.py:287
  49.4 0.0 copy-done.2
  49.4 0.1 reshape.41.column_ref
  49.5 0.0 copy-done
  49.5 0.0 copy-done.1
  49.5 1.6 %folded_weights.1 = (bf16[384,384]{1,0:T(8,128)(2,1)S(1)}, bf16[384,384]{1,0:T(8,128)(2,1)S(1)}, bf16[384,384]{1,0:T(8,128)(2,1)S(1)}) custom-call(bf16[384,1152]{1,0:T(8,128)(2,1)S(1)} %copy-done, bf16[384,384]{1,0:T(8,128)(2,1)S(1)} %copy-done.1, f32[1,384]{1,0:T(1,128)S(1)} %reshape.38.row_ref, f32[384,1]{1,0:T(8,128)S(1)} %reshape.41.column_ref), custom_call_target="tpu_custom_call" | custom-call | flops 600000000 | bytes 1000000 | tf_op jit(solution)/shard_map/folded_weights/pallas_call | solution.py:290
  51.1 3.5 %all-to-all-done.1.part_ref = bf16[4,96,256]{2,1,0:T(8,128)(2,1)S(1)} async-done(((bf16[4,96,256]{2,1,0:T(8,128)(2,1)}), bf16[4,96,256]{2,1,0:T(8,128)(2,1)S(1)}, u32[]{:S(2)}, u32[]{:S(2)}) %all-to-all-start.1) | async-done | bytes 196640 | tf_op jit(solution)/shard_map/conv/all_to_all | solution.py:287
  54.6 0.1 hidden.1
  54.6 16.7 %all_to_all.15 = bf16[16,96,256]{2,1,0:T(8,128)(2,1)S(1)} all-to-all(bf16[16,96,256]{2,1,0:T(8,128)(2,1)S(1)} %hidden.1), channel_id=1, replica_groups=mesh['tm'=16,'y'=4,'core'=2,'width'=4] {'width','y'}, dimensions={0} | all-to-all | bytes 1572864 | tf_op jit(solution)/shard_map/hidden/all_to_all | solution.py:296
  71.4 1.7 %attention.1 = (bf16[32,384]{1,0:T(8,128)(2,1)S(1)}, bf16[32,384]{1,0:T(8,128)(2,1)S(1)}) custom-call(s32[4]{0:T(128)S(1)} %pad_add_fusion.place_ref, bf16[4,384,256]{2,1,0:T(8,128)(2,1)S(1)} %bitcast.14, bf16[384,384]{1,0:T(8,128)(2,1)S(1)} %get-tuple-element.40.score_ref, bf16[384,384]{1,0:T(8,128)(2,1)S(1)} %get-tuple-element.41.update_ref, ...), custom_call_target="tpu_custom_call" | custom-call | flops 200000000 | bytes 1000000 | tf_op jit(solution)/shard_map/attention/pallas_call | solution.py:298
  73.1 5.3 %collective-permute-start.4 = (bf16[32,384]{1,0:T(8,128)(2,1)S(1)}, bf16[32,384]{1,0:T(8,128)(2,1)S(1)}, u32[]{:S(2)}, u32[]{:S(2)}) collective-permute-start(bf16[32,384]{1,0:T(8,128)(2,1)S(1)} %get-tuple-element.44), channel_id=1, source_target_pairs={{0,4},{4,0},{1,5},{5,1},{2,6},{6,2},{3,7},{7,3},{8,12},{12,8},{9,1... | collective-permute-start | bytes 73736 | tf_op jit(solution)/shard_map/attention/ppermute | solution.py:301
  78.3 0.8 %collective-permute-done.4 = bf16[32,384]{1,0:T(8,128)(2,1)S(1)} collective-permute-done((bf16[32,384]{1,0:T(8,128)(2,1)S(1)}, bf16[32,384]{1,0:T(8,128)(2,1)S(1)}, u32[]{:S(2)}, u32[]{:S(2)}) %collective-permute-start.4) | collective-permute-done | bytes 24608 | tf_op jit(solution)/shard_map/attention/ppermute | solution.py:301
  79.2 0.6 maximum_select_fusion
  (1 shorter events, 0.0 us)
Async XLA Ops:
  0.0 10.3 %collective-permute-start.1 = (bf16[64,384]{1,0:T(8,128)(2,1)}, bf16[64,384]{1,0:T(8,128)(2,1)S(1)}, u32[]{:S(2)}, u32[]{:S(2)}) collective-permute-start(bf16[64,384]{1,0:T(8,128)(2,1)} %bitcast.18), channel_id=1, source_target_pairs={{4,0},{5,1},{6,2},{7,3},{12,8},{13,9},{14,10},{15,11},{20,16},{21,... | collective-permute-start | bytes 147464 | tf_op jit(solution)/shard_map/weights_and_cells/ppermute | solution.py:270
  36.7 4.4 %collective-permute-start.2 = (bf16[16,112,256]{2,1,0:T(8,128)(2,1)S(1)}, bf16[16,112,256]{2,1,0:T(8,128)(2,1)S(1)}, u32[]{:S(2)}, u32[]{:S(2)}) collective-permute-start(bf16[16,112,256]{2,1,0:T(8,128)(2,1)S(1)} %get-tuple-element.32), channel_id=1, source_target_pairs={{0,4},{1,5},{2,6},{3,7},{8,12},{9,13},{10,14},{11,15},{16,20},{17,... | collective-permute-start | bytes 2752520 | tf_op jit(solution)/shard_map/patches/ppermute | solution.py:277
  38.0 4.6 %collective-permute-start.3 = (bf16[256,1024]{1,0:T(8,128)(2,1)S(1)}, bf16[256,1024]{1,0:T(8,128)(2,1)S(1)}, u32[]{:S(2)}, u32[]{:S(2)}) collective-permute-start(bf16[256,1024]{1,0:T(8,128)(2,1)S(1)} %get-tuple-element.35.mine_ref), channel_id=1, source_target_pairs={{4,0},{5,1},{6,2},{7,3},{12,8},{13,9},{14,10},{15,11},{20,16},{21,... | collective-permute-start | bytes 1572872 | tf_op jit(solution)/shard_map/patches/ppermute | solution.py:278
  42.6 6.8 %copy-start.2 = (f32[384]{0:T(512)S(1)}, f32[384]{0:T(512)}, u32[]{:S(2)}) copy-start(f32[384]{0:T(512)} %param.11) | copy-start | bytes 4612
  42.6 6.9 %copy-start = (bf16[384,1152]{1,0:T(8,128)(2,1)S(1)}, bf16[384,1152]{1,0:T(8,128)(2,1)}, u32[]{:S(2)}) copy-start(bf16[384,1152]{1,0:T(8,128)(2,1)} %w_ref.1) | copy-start | bytes 2654212
  42.6 6.9 %copy-start.1 = (bf16[384,384]{1,0:T(8,128)(2,1)S(1)}, bf16[384,384]{1,0:T(8,128)(2,1)}, u32[]{:S(2)}) copy-start(bf16[384,384]{1,0:T(8,128)(2,1)} %w_out_ref.1) | copy-start | bytes 884740
  45.3 9.2 %all-to-all-start.1 = ((bf16[4,96,256]{2,1,0:T(8,128)(2,1)}), bf16[4,96,256]{2,1,0:T(8,128)(2,1)S(1)}, u32[]{:S(2)}, u32[]{:S(2)}) async-start(bf16[4,96,256]{2,1,0:T(8,128)(2,1)} %conv.1), calls=%async_computation.1 | async-start | bytes 393216 | tf_op jit(solution)/shard_map/conv/all_to_all | solution.py:287
  73.1 6.1 %collective-permute-start.4 = (bf16[32,384]{1,0:T(8,128)(2,1)S(1)}, bf16[32,384]{1,0:T(8,128)(2,1)S(1)}, u32[]{:S(2)}, u32[]{:S(2)}) collective-permute-start(bf16[32,384]{1,0:T(8,128)(2,1)S(1)} %get-tuple-element.44), channel_id=1, source_target_pairs={{0,4},{4,0},{1,5},{5,1},{2,6},{6,2},{3,7},{7,3},{8,12},{12,8},{9,1... | collective-permute-start | bytes 73736 | tf_op jit(solution)/shard_map/attention/ppermute | solution.py:301

commit v11 on v10

--- a/solution.py
+++ b/solution.py
@@ -111,7 +111,11 @@
     return jnp.where(row // 64 % 2 == odd, target, -1)
 
 
-def patch_body(place_ref, mine_ref, handed_ref, flat_ref, latent_ref):
+def patch_body(place_ref, mine_ref, handed_ref, flat_ref, latent_ref, dense_ref):
+    dense_ref[: 3 * SLOT, :] = one_hot((3 * SLOT, 256), main_place)
+    for tile in range(BAND // 128):
+        start = (3 + tile) * SLOT
+        dense_ref[start : start + SLOT, :] = one_hot((SLOT, 256), functools.partial(spare_place, tile))
     core = place_ref[2]
     lane = lax.broadcasted_iota(jnp.int32, (4 * SLOT, 256), 1) % 64
     blocks = [[None] * 4 for _ in range(4)]
@@ -156,12 +160,12 @@
     return jnp.where(part >= 0, row // 6 * 16 + part * 7 + tile, -1)
 
 
-def conv_body(place_ref, flat_ref, latent_ref, mine_ref, handed_ref, out_ref):
+def conv_body(place_ref, flat_ref, latent_ref, dense_ref, mine_ref, handed_ref, out_ref):
     gathered = jnp.where(place_ref[2] == 1, mine_ref[...], handed_ref[...])
-    main = jnp.dot(one_hot((3 * SLOT, 256), main_place), gathered[:, :BAND], preferred_element_type=F32)
+    main = jnp.dot(dense_ref[: 3 * SLOT, :], gathered[:, :BAND], preferred_element_type=F32)
     spare = [
         jnp.dot(
-            one_hot((SLOT, 256), functools.partial(spare_place, tile)),
+            dense_ref[(3 + tile) * SLOT : (4 + tile) * SLOT, :],
             gathered[:, BAND:],
             preferred_element_type=F32,
         )
@@ -277,12 +281,13 @@
         handed_blocks = lax.ppermute(blocks, "core", [(0, 1)])
         handed_weight = lax.ppermute(weight, "core", [(1, 0)])
         grouped = (4, 4, ROWS, 256)
-        flat, own = call(
-            patch_body, [shape((BAND, 1024), BF16), shape((GROUP, 1024), F32)], [SMEM] + [VMEM] * 2
+        flat, own, dense = call(
+            patch_body, [shape((BAND, 1024), BF16), shape((GROUP, 1024), F32), shape((10 * SLOT, 256), BF16)],
+            [SMEM] + [VMEM] * 2,
         )(place, blocks.reshape(grouped), handed_blocks.reshape(grouped))
     with jax.named_scope("conv"):
-        parts = call(conv_body, shape((4, SLOT, 256), BF16), [SMEM] + [VMEM] * 4, 700_000_000)(
-            place, flat, own, weight, handed_weight
+        parts = call(conv_body, shape((4, SLOT, 256), BF16), [SMEM] + [VMEM] * 5, 700_000_000)(
+            place, flat, own, dense, weight, handed_weight
         )
         parts = lax.all_to_all(parts, "width", 0, 0)
     with jax.named_scope("folded_weights"):

time: 80.3 us -> 80.7 us (level)
  no operation moved by 1% of the time
where the time goes in v11:
time: 80.7 us; the launch traced here: 80.2 us
  blocking collectives  42.9 us (53%)
  starting transfers between devices  22.5 us (28%)
  Pallas kernels  9.14 us (11%)
  waiting for transfers between devices  4.55 us (6%)
    all_gather x1, blocking collectives, gather_weights(): weight = lax.all_gather(piece, 'tm', axis=0, tiled=True)  26.2 us
    all_to_all x1, blocking collectives, local(): hidden = lax.all_to_all(hidden, PLANE, 0, 0)  16.8 us
    ppermute x1, starting transfers between devices, local(): lower = lax.ppermute(cells, 'core', [(1, 0)])  8.77 us
    ppermute x1, starting transfers between devices, local(): got = lax.ppermute(send, 'core', swap)  5.26 us
    all_to_all x1, starting transfers between devices, local(): parts = lax.all_to_all(parts, 'width', 0, 0)  4.02 us
    all_to_all x1, waiting for transfers between devices, local(): parts = lax.all_to_all(parts, 'width', 0, 0)  3.72 us
    ppermute x1, starting transfers between devices, local(): handed_weight = lax.ppermute(weight, 'core', [(1, 0)])  3.12 us
    pallas_call x1, Pallas kernels, local(): call(conv_body, shape((4, SLOT, 256), BF16), [SMEM] + [VMEM] * 5, 700000000)  2.55 us
  transfers between devices with their start and end apart: 5, of which 2 were waited for; matrix products, arithmetic and copies ran while one was open for 0% of the time, Pallas kernels for 6%

profile of v11, /device:TPU:1, one launch (start us, length us, event | category | flops | bytes accessed | tf_op | source)
XLA Modules:
  0.0 80.2 jit_solution(2923099543718028512)
XLA Ops:
  0.0 8.8 %collective-permute-start.1 = (bf16[64,384]{1,0:T(8,128)(2,1)}, bf16[64,384]{1,0:T(8,128)(2,1)S(1)}, u32[]{:S(2)}, u32[]{:S(2)}) collective-permute-start(bf16[64,384]{1,0:T(8,128)(2,1)} %bitcast.18), channel_id=1, source_target_pairs={{4,0},{5,1},{6,2},{7,3},{12,8},{13,9},{14,10},{15,11},{20,16},{21,... | collective-permute-start | bytes 147464 | tf_op jit(solution)/shard_map/weights_and_cells/ppermute | solution.py:274
  8.8 0.1 pad_add_fusion.place_ref
  8.9 1.5 %weights_and_cells.1 = bf16[16,1024]{1,0:T(8,128)(2,1)S(1)} custom-call(s32[4]{0:T(128)S(1)} %pad_add_fusion.place_ref, bf16[27,24,384]{2,1,0:T(8,128)(2,1)} %bitcast.17), custom_call_target="tpu_custom_call" | custom-call | flops 1000000 | bytes 1000000 | tf_op jit(solution)/shard_map/weights_and_cells/pallas_call | solution.py:276
  10.3 0.0 collective-permute-done.1
  10.3 26.3 %conditional.1 = (bf16[256,1024]{1,0:T(8,128)(2,1)S(1)}, bf16[16,112,256]{2,1,0:T(8,128)(2,1)S(1)}, bf16[4,4,112,256]{3,2,1,0:T(8,128)(2,1)S(1)}) conditional(s32[]{:T(128)} %convert_element_type.3, (bf16[64,384]{1,0:T(8,128)(2,1)}, bf16[64,384]{1,0:T(8,128)(2,1)S(1)}, f32[384]{0:T(512)}) %tuple.20, bf16[16,1024]{1,0:T(8,128)(2,1)S(1)} %weights_and_cells.1), branch_computations={%region_0.0_spmd, %region_1.0_spmd} | conditional | flops 1000000 | bytes 5787266 | solution.py:277
  10.4 26.2 %all_gather.2 = bf16[256,1024]{1,0:T(8,128)(2,1)S(1)} all-gather(bf16[16,1024]{1,0:T(8,128)(2,1)S(1)} %param.1), channel_id=1, replica_groups=mesh['tm'=16,'y'=4,'core'=2,'width'=4] {'tm'}, dimensions={0}, use_global_device_ids=true | all-gather | bytes 557056 | tf_op jit(solution)/shard_map/weights_and_cells/cond/branch_1_fun/all_gather | solution.py:264
  36.5 0.1 broadcast.10
  36.6 0.1 reshape.28
  36.7 1.3 %collective-permute-start.2 = (bf16[16,112,256]{2,1,0:T(8,128)(2,1)S(1)}, bf16[16,112,256]{2,1,0:T(8,128)(2,1)S(1)}, u32[]{:S(2)}, u32[]{:S(2)}) collective-permute-start(bf16[16,112,256]{2,1,0:T(8,128)(2,1)S(1)} %get-tuple-element.33), channel_id=1, source_target_pairs={{0,4},{1,5},{2,6},{3,7},{8,12},{9,13},{10,14},{11,15},{16,20},{17,... | collective-permute-start | bytes 2752520 | tf_op jit(solution)/shard_map/patches/ppermute | solution.py:281
  38.0 3.1 %collective-permute-start.3 = (bf16[256,1024]{1,0:T(8,128)(2,1)S(1)}, bf16[256,1024]{1,0:T(8,128)(2,1)S(1)}, u32[]{:S(2)}, u32[]{:S(2)}) collective-permute-start(bf16[256,1024]{1,0:T(8,128)(2,1)S(1)} %get-tuple-element.37.mine_ref), channel_id=1, source_target_pairs={{4,0},{5,1},{6,2},{7,3},{12,8},{13,9},{14,10},{15,11},{20,16},{21,... | collective-permute-start | bytes 1572872 | tf_op jit(solution)/shard_map/patches/ppermute | solution.py:282
  41.1 0.0 collective-permute-done.2
  41.1 1.8 %patches.1 = (bf16[896,1024]{1,0:T(8,128)(2,1)S(1)}, f32[24,1024]{1,0:T(8,128)S(1)}, bf16[960,256]{1,0:T(8,128)(2,1)S(1)}) custom-call(s32[4]{0:T(128)S(1)} %pad_add_fusion.place_ref, bf16[4,4,112,256]{3,2,1,0:T(8,128)(2,1)S(1)} %get-tuple-element.32.mine_ref, bf16[4,4,112,256]{3,2,1,0:T(8,128)(2,1)S(1)} %bitcast.15), custom_call_target="tpu_custom_call" | custom-call | flops 1000000 | bytes 1000000 | tf_op jit(solution)/shard_map/patches/pallas_call | solution.py:284
  42.9 0.0 collective-permute-done.3.handed_ref
  42.9 0.0 copy-start.2
  42.9 0.0 copy-start
  42.9 0.0 copy-start.1
  42.9 2.6 %conv.1 = bf16[4,96,256]{2,1,0:T(8,128)(2,1)} custom-call(s32[4]{0:T(128)S(1)} %pad_add_fusion.place_ref, bf16[896,1024]{1,0:T(8,128)(2,1)S(1)} %get-tuple-element.34.flat_ref, f32[24,1024]{1,0:T(8,128)S(1)} %get-tuple-element.35.latent_ref, bf16[960,256]{1,0:T(8,128)(2,1)S(1)} %get-tuple-element.36.dense_ref, ...), custom_call_target="tpu_custom_call" | custom-call | flops 700000000 | bytes 1000000 | tf_op jit(solution)/shard_map/conv/pallas_call | solution.py:289
  45.5 4.0 %all-to-all-start.1 = ((bf16[4,96,256]{2,1,0:T(8,128)(2,1)}), bf16[4,96,256]{2,1,0:T(8,128)(2,1)S(1)}, u32[]{:S(2)}, u32[]{:S(2)}) async-start(bf16[4,96,256]{2,1,0:T(8,128)(2,1)} %conv.1), calls=%async_computation.1 | async-start | bytes 393216 | tf_op jit(solution)/shard_map/conv/all_to_all | solution.py:292
  49.5 0.0 copy-done.2
  49.5 0.1 reshape.41.column_ref
  49.6 0.0 copy-done
  49.6 0.0 copy-done.1
  49.6 1.6 %folded_weights.1 = (bf16[384,384]{1,0:T(8,128)(2,1)S(1)}, bf16[384,384]{1,0:T(8,128)(2,1)S(1)}, bf16[384,384]{1,0:T(8,128)(2,1)S(1)}) custom-call(bf16[384,1152]{1,0:T(8,128)(2,1)S(1)} %copy-done, bf16[384,384]{1,0:T(8,128)(2,1)S(1)} %copy-done.1, f32[1,384]{1,0:T(1,128)S(1)} %reshape.38.row_ref, f32[384,1]{1,0:T(8,128)S(1)} %reshape.41.column_ref), custom_call_target="tpu_custom_call" | custom-call | flops 600000000 | bytes 1000000 | tf_op jit(solution)/shard_map/folded_weights/pallas_call | solution.py:295
  51.2 3.7 %all-to-all-done.1.part_ref = bf16[4,96,256]{2,1,0:T(8,128)(2,1)S(1)} async-done(((bf16[4,96,256]{2,1,0:T(8,128)(2,1)}), bf16[4,96,256]{2,1,0:T(8,128)(2,1)S(1)}, u32[]{:S(2)}, u32[]{:S(2)}) %all-to-all-start.1) | async-done | bytes 196640 | tf_op jit(solution)/shard_map/conv/all_to_all | solution.py:292
  55.0 0.1 hidden.1
  55.0 16.8 %all_to_all.15 = bf16[16,96,256]{2,1,0:T(8,128)(2,1)S(1)} all-to-all(bf16[16,96,256]{2,1,0:T(8,128)(2,1)S(1)} %hidden.1), channel_id=1, replica_groups=mesh['tm'=16,'y'=4,'core'=2,'width'=4] {'width','y'}, dimensions={0} | all-to-all | bytes 1572864 | tf_op jit(solution)/shard_map/hidden/all_to_all | solution.py:301
  71.8 1.7 %attention.1 = (bf16[32,384]{1,0:T(8,128)(2,1)S(1)}, bf16[32,384]{1,0:T(8,128)(2,1)S(1)}) custom-call(s32[4]{0:T(128)S(1)} %pad_add_fusion.place_ref, bf16[4,384,256]{2,1,0:T(8,128)(2,1)S(1)} %bitcast.14, bf16[384,384]{1,0:T(8,128)(2,1)S(1)} %get-tuple-element.42.score_ref, bf16[384,384]{1,0:T(8,128)(2,1)S(1)} %get-tuple-element.43.update_ref, ...), custom_call_target="tpu_custom_call" | custom-call | flops 200000000 | bytes 1000000 | tf_op jit(solution)/shard_map/attention/pallas_call | solution.py:303
  73.5 5.3 %collective-permute-start.4 = (bf16[32,384]{1,0:T(8,128)(2,1)S(1)}, bf16[32,384]{1,0:T(8,128)(2,1)S(1)}, u32[]{:S(2)}, u32[]{:S(2)}) collective-permute-start(bf16[32,384]{1,0:T(8,128)(2,1)S(1)} %get-tuple-element.46), channel_id=1, source_target_pairs={{0,4},{4,0},{1,5},{5,1},{2,6},{6,2},{3,7},{7,3},{8,12},{12,8},{9,1... | collective-permute-start | bytes 73736 | tf_op jit(solution)/shard_map/attention/ppermute | solution.py:306
  78.8 0.8 %collective-permute-done.4 = bf16[32,384]{1,0:T(8,128)(2,1)S(1)} collective-permute-done((bf16[32,384]{1,0:T(8,128)(2,1)S(1)}, bf16[32,384]{1,0:T(8,128)(2,1)S(1)}, u32[]{:S(2)}, u32[]{:S(2)}) %collective-permute-start.4) | collective-permute-done | bytes 24608 | tf_op jit(solution)/shard_map/attention/ppermute | solution.py:306
  79.6 0.6 maximum_select_fusion
  (1 shorter events, 0.0 us)
Async XLA Ops:
  0.0 10.3 %collective-permute-start.1 = (bf16[64,384]{1,0:T(8,128)(2,1)}, bf16[64,384]{1,0:T(8,128)(2,1)S(1)}, u32[]{:S(2)}, u32[]{:S(2)}) collective-permute-start(bf16[64,384]{1,0:T(8,128)(2,1)} %bitcast.18), channel_id=1, source_target_pairs={{4,0},{5,1},{6,2},{7,3},{12,8},{13,9},{14,10},{15,11},{20,16},{21,... | collective-permute-start | bytes 147464 | tf_op jit(solution)/shard_map/weights_and_cells/ppermute | solution.py:274
  36.7 4.4 %collective-permute-start.2 = (bf16[16,112,256]{2,1,0:T(8,128)(2,1)S(1)}, bf16[16,112,256]{2,1,0:T(8,128)(2,1)S(1)}, u32[]{:S(2)}, u32[]{:S(2)}) collective-permute-start(bf16[16,112,256]{2,1,0:T(8,128)(2,1)S(1)} %get-tuple-element.33), channel_id=1, source_target_pairs={{0,4},{1,5},{2,6},{3,7},{8,12},{9,13},{10,14},{11,15},{16,20},{17,... | collective-permute-start | bytes 2752520 | tf_op jit(solution)/shard_map/patches/ppermute | solution.py:281
  38.0 4.9 %collective-permute-start.3 = (bf16[256,1024]{1,0:T(8,128)(2,1)S(1)}, bf16[256,1024]{1,0:T(8,128)(2,1)S(1)}, u32[]{:S(2)}, u32[]{:S(2)}) collective-permute-start(bf16[256,1024]{1,0:T(8,128)(2,1)S(1)} %get-tuple-element.37.mine_ref), channel_id=1, source_target_pairs={{4,0},{5,1},{6,2},{7,3},{12,8},{13,9},{14,10},{15,11},{20,16},{21,... | collective-permute-start | bytes 1572872 | tf_op jit(solution)/shard_map/patches/ppermute | solution.py:282
  42.9 6.6 %copy-start.2 = (f32[384]{0:T(512)S(1)}, f32[384]{0:T(512)}, u32[]{:S(2)}) copy-start(f32[384]{0:T(512)} %param.11) | copy-start | bytes 4612
  42.9 6.7 %copy-start = (bf16[384,1152]{1,0:T(8,128)(2,1)S(1)}, bf16[384,1152]{1,0:T(8,128)(2,1)}, u32[]{:S(2)}) copy-start(bf16[384,1152]{1,0:T(8,128)(2,1)} %w_ref.1) | copy-start | bytes 2654212
  42.9 6.7 %copy-start.1 = (bf16[384,384]{1,0:T(8,128)(2,1)S(1)}, bf16[384,384]{1,0:T(8,128)(2,1)}, u32[]{:S(2)}) copy-start(bf16[384,384]{1,0:T(8,128)(2,1)} %w_out_ref.1) | copy-start | bytes 884740
  45.5 9.5 %all-to-all-start.1 = ((bf16[4,96,256]{2,1,0:T(8,128)(2,1)}), bf16[4,96,256]{2,1,0:T(8,128)(2,1)S(1)}, u32[]{:S(2)}, u32[]{:S(2)}) async-start(bf16[4,96,256]{2,1,0:T(8,128)(2,1)} %conv.1), calls=%async_computation.1 | async-start | bytes 393216 | tf_op jit(solution)/shard_map/conv/all_to_all | solution.py:292
  73.5 6.1 %collective-permute-start.4 = (bf16[32,384]{1,0:T(8,128)(2,1)S(1)}, bf16[32,384]{1,0:T(8,128)(2,1)S(1)}, u32[]{:S(2)}, u32[]{:S(2)}) collective-permute-start(bf16[32,384]{1,0:T(8,128)(2,1)S(1)} %get-tuple-element.46), channel_id=1, source_target_pairs={{0,4},{4,0},{1,5},{5,1},{2,6},{6,2},{3,7},{7,3},{8,12},{12,8},{9,1... | collective-permute-start | bytes 73736 | tf_op jit(solution)/shard_map/attention/ppermute | solution.py:306
